TPU v7x, 512 devices: a whole 4x8x8 slice. The times are simulated.
512 devices in a mesh: layer: 8 (over y), row: 8 (over x, core), col: 8 (over z).
Axes of the slice: x: 4, y: 8, z: 8, core: 2. Of those that a mesh axis runs over, the one named last changes fastest.
Arguments:
- density: bfloat16 [8192, 8192], P('row', ('col', 'layer')), may hold values from -0.125 to 0.125
- contributions: bfloat16 [32768, 128, 128], P(('layer', 'row', 'col')), may hold values from -5 to 5
- owners: int32 [32768, 1], P(('layer', 'row', 'col')), may hold values from 0 to 63; in each aligned block of 64 rows (0 to 63, 64 to 127, ...) at most 2 rows name the same one
- slots: int32 [32768], P(('layer', 'row', 'col')), may hold values from 0 to 7
- pattern: int32 [64, 64], replicated, may hold values 0 or 1
Outputs:
- product: bfloat16 [8192, 8192], P(('row', 'layer'), 'col')
Inputs may be any that keep to these rules, and one draw needn't show every extreme that they name: `owners`: within the rows of one device no owner is named by more than 2 rows; some owner is named by exactly 2.
All inputs are finite; a program needn't handle non-finite values.
Results may differ from a plain program's by a relative error of at most 0.017.
Values may be sent and summed in bfloat16 or wider, within the bound.
No kernel may reach another device: no remote copies, remote signals or barrier semaphores. Data moves between devices by JAX's collectives and lax.ppermute only.
A program may use at most 64 MiB of HBM per device.

v0:
```python
import jax
import jax.numpy as jnp
from jax import lax
from jax.sharding import PartitionSpec as P


def body(density, contributions, owners, slots, pattern):
    row_count = lax.axis_size("row")
    col_count = lax.axis_size("col")
    layer_count = lax.axis_size("layer")
    row_index = lax.axis_index("row")
    col_index = lax.axis_index("col")
    layer_index = lax.axis_index("layer")
    count = contributions.shape[0]
    strip = contributions.shape[1]
    tile = contributions.shape[2]
    width = strip * tile
    owner_count = row_count * col_count
    capacity = 2 * ((count + owner_count - 1) // owner_count)
    rows = density.shape[0]
    inner = density.shape[1]
    tile_rows = rows // tile
    inner_tiles = inner // tile
    place_count = inner // strip * tile_rows
    target = owners[:, 0]
    by_owner = (target[:, None] == jnp.arange(owner_count, dtype=jnp.int32)[None, :]).astype(
        jnp.int32
    )
    earlier = jnp.cumsum(by_owner, axis=0) - by_owner
    rank = jnp.sum(earlier * by_owner, axis=1)
    position = target * capacity + rank
    dispatch = position[:, None] == jnp.arange(owner_count * capacity, dtype=jnp.int32)[None, :]
    flat = contributions.reshape(count, width)
    packed = jnp.einsum(
        "np,nf->pf", dispatch.astype(jnp.bfloat16), flat, preferred_element_type=jnp.float32
    ).astype(jnp.bfloat16)
    packed_slots = jnp.sum(jnp.where(dispatch, slots[:, None] + 1, 0), axis=0) - 1
    received, received_slots = (
        lax.all_to_all(
            packed.reshape(owner_count, capacity, width),
            ("row", "col"),
            split_axis=0,
            concat_axis=0,
            tiled=True,
        ),
        lax.all_to_all(
            packed_slots.reshape(owner_count, capacity),
            ("row", "col"),
            split_axis=0,
            concat_axis=0,
            tiled=True,
        ),
    )
    received = received.reshape(owner_count * capacity, width)
    received_slots = received_slots.reshape(owner_count * capacity)
    collect = (received_slots[:, None] == jnp.arange(place_count, dtype=jnp.int32)[None, :]).astype(
        jnp.bfloat16
    )
    ham_flat = jnp.einsum(
        "ps,pf->sf", collect, received, preferred_element_type=jnp.float32
    ).astype(jnp.bfloat16)
    hamilton = (
        ham_flat.reshape(inner // strip, tile_rows, strip, tile)
        .transpose(0, 2, 1, 3)
        .reshape(inner, rows)
    )
    density_tiles = lax.dynamic_slice(
        pattern,
        (row_index * tile_rows, (col_index * layer_count + layer_index) * inner_tiles),
        (tile_rows, inner_tiles),
    )
    sparse = (
        density.reshape(tile_rows, tile, inner_tiles, tile)
        * density_tiles[:, None, :, None].astype(jnp.bfloat16)
    ).reshape(rows, inner)
    ham_whole = lax.all_gather(hamilton, "row", axis=0, tiled=True)
    partial_sum = jnp.dot(
        lax.all_gather(sparse, "col", axis=1, tiled=True),
        ham_whole,
        preferred_element_type=jnp.float32,
    )
    summed = lax.psum_scatter(
        partial_sum.astype(jnp.bfloat16), "layer", scatter_dimension=0, tiled=True
    ).astype(jnp.float32)
    kept_tiles = lax.dynamic_slice(
        pattern,
        (row_index * tile_rows + layer_index * inner_tiles, col_index * tile_rows),
        (inner_tiles, tile_rows),
    )
    kept = summed.reshape(inner_tiles, tile, tile_rows, tile) * kept_tiles[:, None, :, None].astype(
        jnp.float32
    )
    return kept.reshape(inner, rows).astype(jnp.bfloat16)


def solution(mesh):
    return jax.shard_map(
        body,
        mesh=mesh,
        in_specs=(
            P("row", ("col", "layer")),
            P(("layer", "row", "col"), None, None),
            P(("layer", "row", "col"), None),
            P(("layer", "row", "col")),
            P(),
        ),
        out_specs=P(("row", "layer"), "col"),
        check_vma=False,
    )
```

profile of v0, /device:TPU:1, one launch (start us, length us, event | category | flops | bytes accessed | tf_op | source)
XLA Modules:
  0.0 257.7 jit_solution(4141073834961469446)
XLA Ops:
  6.5 0.7 fusion.3
  7.3 0.1 reduce_window_sum.11
  7.4 0.8 select_reduce_fusion.1
  8.2 0.7 fusion.6
  8.9 0.7 broadcast_add_fusion.1
  9.5 0.1 select_reduce_fusion
  9.6 0.8 sub.11
  10.4 14.8 %all-to-all-start = ((s32[64,1,2]{2,1,0:T(1,128)}), s32[64,1,2]{2,1,0:T(1,128)S(1)}, u32[]{:S(2)}, u32[]{:S(2)}) async-start(s32[64,1,2]{2,1,0:T(1,128)} %bitcast.4), calls=%async_computation | async-start | bytes 65536 | tf_op jit(solution)/shard_map/all_to_all | solution.py:46
  25.2 5.1 %convolution_convert_fusion = bf16[128,16384]{1,0:T(8,128)(2,1)} fusion(bf16[8,8,128,128]{3,2,1,0:T(8,128)(2,1)} %bitcast.29, s32[64]{0:T(128)S(1)} %fusion.6), kind=kOutput, calls=%fused_computation | convolution fusion | flops 270540800 | bytes 6291712 | tf_op jit(solution)/shard_map/np,nf->pf/dot_general | solution.py:34
  30.4 7.6 %reshape.69 = bf16[64,2,16384]{2,1,0:T(2,128)(2,1)} reshape(bf16[128,16384]{1,0:T(8,128)(2,1)} %convolution_convert_fusion) | data formatting | bytes 8388608 | tf_op jit(solution)/shard_map/reshape | solution.py:40
  38.0 10.6 %all-to-all-start.1 = ((bf16[64,2,16384]{2,1,0:T(2,128)(2,1)}), bf16[64,2,16384]{2,1,0:T(2,128)(2,1)}, u32[]{:S(2)}, u32[]{:S(2)}) async-start(bf16[64,2,16384]{2,1,0:T(2,128)(2,1)} %reshape.69), calls=%async_computation.1 | async-start | bytes 8388608 | tf_op jit(solution)/shard_map/all_to_all | solution.py:39
  48.6 0.0 all-gather.3.cloned.1.call-start
  48.7 0.9 fusion.5
  49.6 0.1 broadcast_bitcast_fusion.1
  49.6 0.9 broadcast_multiply_fusion
  50.5 0.0 all-gather.3.cloned.1.call-update
  50.6 0.0 all-gather.5.cloned.1.call-start
  50.6 0.6 broadcast.37
  51.2 0.7 reduce.5
  52.0 0.1 eq.53
  52.1 111.2 %all-to-all-done.1 = bf16[64,2,16384]{2,1,0:T(2,128)(2,1)} async-done(((bf16[64,2,16384]{2,1,0:T(2,128)(2,1)}), bf16[64,2,16384]{2,1,0:T(2,128)(2,1)}, u32[]{:S(2)}, u32[]{:S(2)}) %all-to-all-start.1) | async-done | bytes 4194336 | tf_op jit(solution)/shard_map/all_to_all | solution.py:39
  163.3 7.2 %reshape.70 = bf16[128,16384]{1,0:T(8,128)(2,1)} reshape(bf16[64,2,16384]{2,1,0:T(2,128)(2,1)} %all-to-all-done.1) | data formatting | bytes 8388608 | tf_op jit(solution)/shard_map/reshape | solution.py:54
  170.5 2.9 %convolution_convert_fusion.1 = bf16[8,16384]{1,0:T(8,128)(2,1)S(1)} fusion(bf16[128,16384]{1,0:T(8,128)(2,1)} %reshape.70, s32[128]{0:T(128)S(1)} %eq.53), kind=kOutput, calls=%fused_computation.1 | convolution fusion | flops 33686528 | bytes 4456960 | tf_op jit(solution)/shard_map/ps,pf->sf/dot_general | solution.py:59
  173.4 0.8 copy.15
  174.2 0.0 reduce-scatter.2.cloned.1.call-start
  174.3 0.0 all-gather.3.cloned.1.call-done
  174.3 28.9 %all-gather.5.cloned.1.call-done = bf16[1024,1024]{1,0:T(8,128)(2,1)} async-done(((bf16[128,1024]{1,0:T(8,128)(2,1)}), bf16[1024,1024]{1,0:T(8,128)(2,1)}) %all-gather.5.cloned.1.call-update) | async-done | bytes 2097168 | tf_op jit(solution)/shard_map/all_gather | solution.py:76
  203.2 5.8 %convolution_convert_fusion.2 = bf16[1024,1024]{1,0:T(8,128)(2,1)} fusion(bf16[1024,1024]{1,0:T(8,128)(2,1)} %all-gather.3.cloned.1.call-done, bf16[1024,1024]{1,0:T(8,128)(2,1)} %all-gather.5.cloned.1.call-done), kind=kOutput, calls=%fused_computation.4 | convolution fusion | flops 2148532224 | bytes 6291456 | tf_op jit(solution)/shard_map/dot_general | solution.py:77
  209.1 0.8 convert_bitcast_fusion
  209.8 0.1 broadcast_bitcast_fusion
  209.9 39.5 %reduce-scatter.2.cloned.1.call-done = bf16[128,1024]{1,0:T(8,128)(2,1)} async-done(((bf16[1024,1024]{1,0:T(8,128)(2,1)}), bf16[128,1024]{1,0:T(8,128)(2,1)}) %reduce-scatter.2.cloned.1.call-update) | async-done | bytes 262160 | tf_op jit(solution)/shard_map/reduce_scatter | solution.py:82
  249.4 1.7 multiply_convert_fusion
  (6 shorter events, 0.0 us)
Async XLA Ops:
  10.4 27.6 %all-to-all-start = ((s32[64,1,2]{2,1,0:T(1,128)}), s32[64,1,2]{2,1,0:T(1,128)S(1)}, u32[]{:S(2)}, u32[]{:S(2)}) async-start(s32[64,1,2]{2,1,0:T(1,128)} %bitcast.4), calls=%async_computation | async-start | bytes 65536 | tf_op jit(solution)/shard_map/all_to_all | solution.py:46
  38.0 11.6 %copy-start = (bf16[1024,128]{1,0:T(8,128)(2,1)S(1)}, bf16[1024,128]{1,0:T(8,128)(2,1)}, u32[]{:S(2)}) copy-start(bf16[1024,128]{1,0:T(8,128)(2,1)} %param.5) | copy-start | bytes 786436
  38.0 125.3 %all-to-all-start.1 = ((bf16[64,2,16384]{2,1,0:T(2,128)(2,1)}), bf16[64,2,16384]{2,1,0:T(2,128)(2,1)}, u32[]{:S(2)}, u32[]{:S(2)}) async-start(bf16[64,2,16384]{2,1,0:T(2,128)(2,1)} %reshape.69), calls=%async_computation.1 | async-start | bytes 8388608 | tf_op jit(solution)/shard_map/all_to_all | solution.py:39
  48.6 125.7 %all-gather.3.cloned.1.call-start = ((), (), s32[]{:S(2)}) async-start(), calls=%async_computation.3 | async-start | bytes 2359296 | tf_op jit(solution)/shard_map/all_gather | solution.py:78
  50.6 152.6 %all-gather.5.cloned.1.call-start = ((), (), s32[]{:S(2)}) async-start(), calls=%async_computation.4 | async-start | bytes 2359296 | tf_op jit(solution)/shard_map/all_gather | solution.py:76
  174.2 75.2 %reduce-scatter.2.cloned.1.call-start = ((), (), s32[]{:S(2)}) async-start(), calls=%async_computation.5 | async-start | bytes 2359296 | tf_op jit(solution)/shard_map/reduce_scatter | solution.py:82
Sparse Core Ops, SparseCore 0:
  51.5 110.4 all-gather.2
  174.4 28.7 all-gather.4
  209.2 40.2 reduce-scatter.1
where the time goes:
time: 262 us; the launch traced here: 258 us
  waiting for transfers between devices  180 us (69%)
  starting transfers between devices  25.6 us (10%)
  local copies, waits for them, and re-layouts  17.2 us (7%)
  matrix products  13.9 us (5%)
  between operations  13.2 us (5%)
  other arithmetic  8.09 us (3%)
    all_to_all x1, waiting for transfers between devices, body(): lax.all_to_all(packed.reshape(owner_count, capacity, width), ('row', 'col...  111 us
    reduce_scatter x1, waiting for transfers between devices, body(): lax.psum_scatter(partial_sum.astype(jnp.bfloat16), 'layer', scatter_dimen...  39.5 us
    all_gather x1, waiting for transfers between devices, body(): ham_whole = lax.all_gather(hamilton, 'row', axis=0, tiled=True)  28.9 us
    all_to_all x1, starting transfers between devices, body(): lax.all_to_all(packed_slots.reshape(owner_count, capacity), ('row', 'col'...  14.8 us
    all_to_all x1, starting transfers between devices, body(): lax.all_to_all(packed.reshape(owner_count, capacity, width), ('row', 'col...  10.6 us
    reshape x1, local copies, waits for them, and re-layouts, body(): packed.reshape(owner_count, capacity, width)  7.62 us
    reshape x1, local copies, waits for them, and re-layouts, body(): received = received.reshape(owner_count * capacity, width)  7.2 us
    dot_general x1, matrix products, body(): jnp.dot(lax.all_gather(sparse, 'col', axis=1, tiled=True), ham_whole, pre...  5.85 us
  transfers between devices with their start and end apart: 5, of which 3 were waited for; matrix products, arithmetic and copies ran while one was open for 11% of the time, Pallas kernels for 0%

commit v1 on v0

v1 whole, which is shorter than its diff:
```python
import jax
import jax.numpy as jnp
from jax import lax
from jax.experimental import pallas as pl
from jax.experimental.pallas import tpu as pltpu
from jax.sharding import Mesh, PartitionSpec as P

TILE = 128
SIDE = 8
CAP = 16
BODY = CAP * TILE
META = 16
LAST = TILE - 1
MIB = 1 << 20


def pack_kernel(owners, slots, contributions, out, count, meta, sem, meta_sem):
    for r in range(SIDE):
        count[r] = 0
    row = lax.broadcasted_iota(jnp.int32, (SIDE, TILE), 0)
    lane = lax.broadcasted_iota(jnp.int32, (SIDE, TILE), 1)

    def one(i, places):
        owner = owners[i]
        r = owner // SIDE
        c = owner - r * SIDE
        pos = count[r]
        count[r] = pos + 1
        pltpu.make_async_copy(
            contributions.at[i], out.at[r, pl.ds(pl.multiple_of(pos * TILE, TILE), TILE)], sem
        ).start()
        here = (row == r) & (lane == pos)
        return jnp.where(here, c * SIDE + slots[i], places)

    places = lax.fori_loop(
        0, contributions.shape[0], one, jnp.zeros((SIDE, TILE), jnp.int32), unroll=8
    )
    for r in range(SIDE):
        places = jnp.where((row == r) & (lane == LAST), count[r], places)
    values = places.astype(jnp.float32)
    for r in range(SIDE):
        meta[r] = jnp.broadcast_to(values[r : r + 1], (META, TILE)).astype(jnp.bfloat16)
    tail = pltpu.make_async_copy(meta, out.at[:, pl.ds(BODY, META)], meta_sem)
    tail.start()
    pltpu.make_async_copy(contributions, contributions, sem).wait()
    tail.wait()


def pack(owners, slots, contributions):
    return pl.pallas_call(
        pack_kernel,
        out_shape=jax.ShapeDtypeStruct((SIDE, BODY + META, TILE), jnp.bfloat16),
        in_specs=[
            pl.BlockSpec(memory_space=pltpu.SMEM),
            pl.BlockSpec(memory_space=pltpu.SMEM),
            pl.BlockSpec(memory_space=pl.ANY),
        ],
        out_specs=pl.BlockSpec(memory_space=pl.ANY),
        scratch_shapes=[
            pltpu.SMEM((SIDE,), jnp.int32),
            pltpu.VMEM((SIDE, META, TILE), jnp.bfloat16),
            pltpu.SemaphoreType.DMA,
            pltpu.SemaphoreType.DMA,
        ],
        cost_estimate=pl.CostEstimate(flops=0, bytes_accessed=4 * MIB, transcendentals=0),
        name="pack",
    )(owners, slots, contributions)


def combine_kernel(got, out, data, meta, places, table, total, sems, meta_sem, table_sem):
    head = pltpu.make_async_copy(got.at[:, pl.ds(BODY, META)], meta, meta_sem)
    head.start()
    loads = [
        pltpu.make_async_copy(got.at[r, pl.ds(0, BODY)], data.at[r], sems.at[r])
        for r in range(SIDE)
    ]
    for load in loads:
        load.start()
    total[...] = jnp.zeros_like(total)
    head.wait()
    for r in range(SIDE):
        places[r : r + 1] = meta[r].astype(jnp.float32)[:1].astype(jnp.int32)
    listing = pltpu.make_async_copy(places, table, table_sem)
    listing.start()
    listing.wait()
    for r in range(SIDE):
        loads[r].wait()

        def one(pos, carry, r=r):
            place = table[r, pos]
            rows = pl.ds(pl.multiple_of(pos * TILE, TILE), TILE)
            total[place] += data[r, rows].astype(jnp.float32)
            return carry

        lax.fori_loop(0, table[r, LAST], one, 0)

    def write(c, carry):
        for s in range(SIDE):
            out[c, :, s * TILE : (s + 1) * TILE] = total[c * SIDE + s].astype(jnp.bfloat16)
        return carry

    lax.fori_loop(0, SIDE, write, 0)


def combine(got):
    return pl.pallas_call(
        combine_kernel,
        out_shape=jax.ShapeDtypeStruct((SIDE, TILE, SIDE * TILE), jnp.bfloat16),
        in_specs=[pl.BlockSpec(memory_space=pl.ANY)],
        out_specs=pl.BlockSpec(memory_space=pltpu.VMEM),
        scratch_shapes=[
            pltpu.VMEM((SIDE, BODY, TILE), jnp.bfloat16),
            pltpu.VMEM((SIDE, META, TILE), jnp.bfloat16),
            pltpu.VMEM((SIDE, TILE), jnp.int32),
            pltpu.SMEM((SIDE, TILE), jnp.int32),
            pltpu.VMEM((SIDE * SIDE, TILE, TILE), jnp.float32),
            pltpu.SemaphoreType.DMA((SIDE,)),
            pltpu.SemaphoreType.DMA,
            pltpu.SemaphoreType.DMA,
        ],
        compiler_params=pltpu.CompilerParams(vmem_limit_bytes=24 * MIB),
        cost_estimate=pl.CostEstimate(
            flops=4 * MIB, bytes_accessed=6 * MIB, transcendentals=0
        ),
        name="combine",
    )(got)


def product_kernel(at, near, far, own, other, out, ham):
    half = near.shape[1]
    core, layer = at[0], at[1]

    @pl.when(pl.program_id(0) == 0)
    def _():
        for l in range(2):
            base = jnp.where(layer == l, 0, half)
            for j in range(SIDE // 2):
                mine = base + (2 * j + core) * TILE
                theirs = base + (2 * j + 1 - core) * TILE
                ham[pl.ds(pl.multiple_of(mine, TILE), TILE)] = own[l * 4 + j]
                ham[pl.ds(pl.multiple_of(theirs, TILE), TILE)] = other[l * 4 + j]

    total = jnp.dot(near[...], ham[:half], preferred_element_type=jnp.float32)
    total += jnp.dot(far[...], ham[half:], preferred_element_type=jnp.float32)
    out[...] = total.astype(jnp.bfloat16)


def product_of(at, near, far, own, other):
    rows, half = near.shape
    step = 256
    width = own.shape[2]
    return pl.pallas_call(
        product_kernel,
        out_shape=jax.ShapeDtypeStruct((rows, width), jnp.bfloat16),
        grid_spec=pltpu.PrefetchScalarGridSpec(
            num_scalar_prefetch=1,
            grid=(rows // step,),
            in_specs=[
                pl.BlockSpec((step, half), lambda i, at: (i, 0)),
                pl.BlockSpec((step, half), lambda i, at: (i, 0)),
                pl.BlockSpec(own.shape, lambda i, at: (0, 0, 0)),
                pl.BlockSpec(own.shape, lambda i, at: (0, 0, 0)),
            ],
            out_specs=pl.BlockSpec((step, width), lambda i, at: (i, 0)),
            scratch_shapes=[pltpu.VMEM((2 * half, width), jnp.bfloat16)],
        ),
        compiler_params=pltpu.CompilerParams(vmem_limit_bytes=24 * MIB),
        cost_estimate=pl.CostEstimate(
            flops=4 * rows * half * width, bytes_accessed=7 * MIB, transcendentals=0
        ),
        name="product",
    )(at, near, far, own, other)


def body(density, contributions, owners, slots, pattern):
    row_index = lax.axis_index(("rx", "rc"))
    col_index = lax.axis_index("col")
    layer_index = lax.axis_index(("lg", "lq"))
    core = lax.axis_index("rc")
    pair = lax.axis_index("lq")
    rows, inner = density.shape

    density_tiles = lax.dynamic_slice(
        pattern, (row_index * SIDE, col_index * SIDE + layer_index), (SIDE, 1)
    )
    sparse = (
        density.reshape(SIDE, TILE, inner) * density_tiles[:, :, None].astype(jnp.bfloat16)
    ).reshape(rows, inner)
    near = lax.all_gather(sparse, "col", axis=1, tiled=True)

    packed = pack(owners.reshape(-1), slots, contributions)
    got = lax.all_to_all(packed, ("rx", "rc"), split_axis=0, concat_axis=0, tiled=True)
    partial_ham = combine(got).reshape(rows, rows)
    far = lax.ppermute(near, "lq", [(0, 1), (1, 0)])
    ham = lax.psum_scatter(partial_ham, "col", scatter_dimension=0, tiled=True)

    halves = ham.reshape(inner, 2, rows // 2).transpose(1, 0, 2)
    spread = jnp.broadcast_to(halves[:, None], (2, 4, inner, rows // 2)).reshape(
        8, inner, rows // 2
    )
    own = lax.all_to_all(spread, ("lq", "rx"), split_axis=0, concat_axis=0, tiled=True)
    other = lax.ppermute(own, "rc", [(0, 1), (1, 0)])
    at = jnp.stack([core, pair]).astype(jnp.int32)
    term = product_of(at, near, far, own, other)

    terms = lax.all_to_all(
        term.reshape(SIDE, TILE, rows // 2), ("lg", "lq"), split_axis=0, concat_axis=0, tiled=True
    )
    summed = jnp.sum(terms.reshape(4, 2, TILE, rows // 2).astype(jnp.float32), axis=0)
    kept_tiles = lax.dynamic_slice(
        pattern, (row_index * SIDE + layer_index, col_index * SIDE), (1, SIDE)
    )
    mask = jnp.repeat(kept_tiles.reshape(2, 1, SIDE // 2).astype(jnp.float32), TILE, axis=2)
    kept = summed * mask
    return kept.astype(jnp.bfloat16).transpose(1, 0, 2).reshape(inner, rows)


def solution(mesh):
    layers, grid_rows, grid_cols = mesh.devices.shape
    split = Mesh(
        mesh.devices.reshape(layers // 2, 2, grid_rows // 2, 2, grid_cols),
        ("lg", "lq", "rx", "rc", "col"),
    )
    layer, row = ("lg", "lq"), ("rx", "rc")
    return jax.shard_map(
        body,
        mesh=split,
        in_specs=(
            P(row, ("col", *layer)),
            P((*layer, *row, "col"), None, None),
            P((*layer, *row, "col"), None),
            P((*layer, *row, "col")),
            P(),
        ),
        out_specs=P((*row, *layer), "col"),
        check_vma=False,
    )
```

time: 262 us -> 322 us (1.23)
  Pallas kernels: 0 us -> 73.4 us
  blocking collectives: 0 us -> 60.6 us
  waiting for transfers between devices: 180 us -> 142 us
  matrix products: 13.9 us -> 0 us
  local copies, waits for them, and re-layouts: 17.2 us -> 4.92 us
  other arithmetic: 8.09 us -> 2.84 us
  starting transfers between devices: 25.6 us -> 20.7 us
    all_to_all x2, waiting for transfers between devices: 111 us -> 24.2 us  [the longest x1 24.2 us: body(): lax.all_to_all(term.reshape(SIDE, TILE, rows // 2), ('lg', 'lq'), split_a...]
    pallas_call x0 -> x3, Pallas kernels: none -> 73.4 us  [the longest x1 65.3 us: pack(): pl.pallas_call(pack_kernel, out_shape=jax.ShapeDtypeStruct((SIDE, BODY +...]
    all_to_all x0 -> x1, blocking collectives: none -> 60.6 us  [body(): lax.all_to_all(packed, ('rx', 'rc'), split_axis=0, concat_axis=0, tiled=T...]
    ppermute x0 -> x2, waiting for transfers between devices: none -> 35.6 us  [the longest x1 35.6 us: body(): far = lax.ppermute(near, 'lq', [(0, 1), (1, 0)])]
    all_gather x2 -> x1, waiting for transfers between devices: 28.9 us -> 44.6 us  [body(): near = lax.all_gather(sparse, 'col', axis=1, tiled=True)]
    all_to_all x2, starting transfers between devices: 25.5 us -> 11.3 us  [the longest x1 6.46 us: body(): lax.all_to_all(term.reshape(SIDE, TILE, rows // 2), ('lg', 'lq'), split_a...]
    dot_general x3 -> x0, matrix products: 13.9 us -> none  [the longest x1 5.85 us: body(): jnp.dot(lax.all_gather(sparse, 'col', axis=1, tiled=True), ham_whole, pre...]
    reshape x2, local copies, waits for them, and re-layouts: 14.8 us -> 1.82 us  [the longest x1 0.97 us: body(): halves = ham.reshape(inner, 2, rows // 2).transpose(1, 0, 2)]
  transfers between devices with their start and end apart: 5 -> 6, of which waited for: 3 -> 4; matrix products, arithmetic and copies ran while one was open for 11% -> 2% of each run, Pallas kernels for 0% -> 0%
where the time goes in v1:
time: 322 us; the launch traced here: 318 us
  waiting for transfers between devices  142 us (44%)
  Pallas kernels  73.4 us (23%)
  blocking collectives  60.6 us (19%)
  starting transfers between devices  20.7 us (6%)
  between operations  13.5 us (4%)
  local copies, waits for them, and re-layouts  4.92 us (2%)
    pallas_call x1, Pallas kernels, pack(): pl.pallas_call(pack_kernel, out_shape=jax.ShapeDtypeStruct((SIDE, BODY +...  65.3 us
    all_to_all x1, blocking collectives, body(): lax.all_to_all(packed, ('rx', 'rc'), split_axis=0, concat_axis=0, tiled=T...  60.6 us
    all_gather x1, waiting for transfers between devices, body(): near = lax.all_gather(sparse, 'col', axis=1, tiled=True)  44.6 us
    reduce_scatter x1, waiting for transfers between devices, body(): ham = lax.psum_scatter(partial_ham, 'col', scatter_dimension=0, tiled=True)  37.6 us
    ppermute x1, waiting for transfers between devices, body(): far = lax.ppermute(near, 'lq', [(0, 1), (1, 0)])  35.6 us
    all_to_all x1, waiting for transfers between devices, body(): lax.all_to_all(term.reshape(SIDE, TILE, rows // 2), ('lg', 'lq'), split_a...  24.2 us
    all_to_all x1, starting transfers between devices, body(): lax.all_to_all(term.reshape(SIDE, TILE, rows // 2), ('lg', 'lq'), split_a...  6.46 us
  transfers between devices with their start and end apart: 6, of which 4 were waited for; matrix products, arithmetic and copies ran while one was open for 2% of the time, Pallas kernels for 0%

profile of v1, /device:TPU:1, one launch (start us, length us, event | category | flops | bytes accessed | tf_op | source)
XLA Modules:
  0.0 318.0 jit_solution(11582733833746023714)
XLA Ops:
  6.5 0.0 reduce-scatter.2.cloned.1.call-start
  6.5 65.3 %pack.1 = bf16[8,2064,128]{2,1,0:T(8,128)(2,1)} custom-call(s32[64]{0:T(128)} %bitcast.30, s32[64]{0:T(128)} %slots.1, bf16[64,128,128]{2,1,0:T(8,128)(2,1)} %contributions.1), custom_call_target="tpu_custom_call" | custom-call | bytes 4194304 | tf_op jit(solution)/shard_map/pack/pallas_call | solution.py:50
  71.9 60.6 %all_to_all.15.got = bf16[8,2064,128]{2,1,0:T(8,128)(2,1)S(1)} all-to-all(bf16[8,2064,128]{2,1,0:T(8,128)(2,1)} %pack.1), channel_id=1, replica_groups=mesh['lg'=4,'lq'=2,'rx'=4,'rc'=2,'col'=8] {'rx','rc'}, dimensions={0} | all-to-all | bytes 8454144 | tf_op jit(solution)/shard_map/all_to_all | solution.py:192
  132.5 3.7 %combine.1 = bf16[8,128,1024]{2,1,0:T(8,128)(2,1)} custom-call(bf16[8,2064,128]{2,1,0:T(8,128)(2,1)S(1)} %all_to_all.15.got), custom_call_target="tpu_custom_call" | custom-call | flops 4194304 | bytes 6291456 | tf_op jit(solution)/shard_map/combine/pallas_call | solution.py:106
  136.2 0.0 copy-start.1
  136.2 0.0 reduce-scatter.2.cloned.1.call-update
  136.2 0.0 all-gather.2.cloned.1.call-start
  136.3 0.9 fusion.1
  137.2 0.1 broadcast_bitcast_fusion.1
  137.3 0.9 broadcast_multiply_fusion
  138.2 0.0 all-gather.2.cloned.1.call-update
  138.2 37.6 %reduce-scatter.2.cloned.1.call-done = bf16[128,1024]{1,0:T(8,128)(2,1)} async-done(((bf16[1024,1024]{1,0:T(8,128)(2,1)}), bf16[128,1024]{1,0:T(8,128)(2,1)}) %reduce-scatter.2.cloned.1.call-update) | async-done | bytes 262160 | tf_op jit(solution)/shard_map/reduce_scatter | solution.py:195
  175.8 1.0 copy.15
  176.8 1.1 broadcast_in_dim.12
  177.9 4.8 %all-to-all-start.1 = ((bf16[8,128,512]{2,1,0:T(8,128)(2,1)}), bf16[8,128,512]{2,1,0:T(8,128)(2,1)S(1)}, u32[]{:S(2)}, u32[]{:S(2)}) async-start(bf16[8,128,512]{2,1,0:T(8,128)(2,1)} %bitcast.6), calls=%async_computation.2 | async-start | bytes 2097152 | tf_op jit(solution)/shard_map/all_to_all | solution.py:201
  182.7 44.6 %all-gather.2.cloned.1.call-done.near = bf16[1024,1024]{1,0:T(8,128)(2,1)} async-done(((bf16[1024,128]{1,0:T(8,128)(2,1)}), bf16[1024,1024]{1,0:T(8,128)(2,1)}) %all-gather.2.cloned.1.call-update) | async-done | bytes 2097168 | tf_op jit(solution)/shard_map/all_gather | solution.py:189
  227.3 3.1 collective-permute-start
  230.4 0.0 all-to-all-done.1.own
  230.4 6.3 %collective-permute-start.1 = (bf16[8,128,512]{2,1,0:T(8,128)(2,1)S(1)}, bf16[8,128,512]{2,1,0:T(8,128)(2,1)S(1)}, u32[]{:S(2)}, u32[]{:S(2)}) collective-permute-start(bf16[8,128,512]{2,1,0:T(8,128)(2,1)S(1)} %all-to-all-done.1.own), channel_id=1, source_target_pairs={{0,8},{8,0},{1,9},{9,1},{2,10},{10,2},{3,11},{11,3},{4,12},{12,4},... | collective-permute-start | bytes 3145736 | tf_op jit(solution)/shard_map/ppermute | solution.py:202
  236.7 0.1 pad_add_fusion.at
  236.8 35.6 %collective-permute-done.far = bf16[1024,1024]{1,0:T(8,128)(2,1)S(1)} collective-permute-done((bf16[1024,1024]{1,0:T(8,128)(2,1)}, bf16[1024,1024]{1,0:T(8,128)(2,1)S(1)}, u32[]{:S(2)}, u32[]{:S(2)}) %collective-permute-start) | collective-permute-done | bytes 2097184 | tf_op jit(solution)/shard_map/ppermute | solution.py:194
  272.4 0.0 collective-permute-done.1.other
  272.4 1.6 copy-done
  274.0 4.4 %product.1 = bf16[1024,512]{1,0:T(8,128)(2,1)} custom-call(s32[2]{0:T(128)S(1)} %pad_add_fusion.at, bf16[1024,1024]{1,0:T(8,128)(2,1)S(1)} %copy-done, bf16[1024,1024]{1,0:T(8,128)(2,1)S(1)} %collective-permute-done.far, bf16[8,128,512]{2,1,0:T(8,128)(2,1)S(1)} %all-to-all-done.1.own, bf16[8,128,512]{2,1,0:T(8,128)(2,1)S(1)} %collective-permute-done.1.other), custom_call_target="tpu_custom_call" | custom-call | flops 2147483648 | bytes 7340032 | tf_op jit(solution)/shard_map/product/pallas_call | solution.py:152
  278.4 6.5 %all-to-all-start.2 = ((bf16[8,128,512]{2,1,0:T(8,128)(2,1)}), bf16[8,128,512]{2,1,0:T(8,128)(2,1)S(1)}, u32[]{:S(2)}, u32[]{:S(2)}) async-start(bf16[8,128,512]{2,1,0:T(8,128)(2,1)} %bitcast.7), calls=%async_computation.3 | async-start | bytes 2097152 | tf_op jit(solution)/shard_map/all_to_all | solution.py:206
  284.8 0.8 convert_reduce_fusion.1
  285.6 0.1 convert_element_type.38
  285.7 0.1 broadcast_bitcast_fusion
  285.8 24.2 %all-to-all-done.2 = bf16[8,128,512]{2,1,0:T(8,128)(2,1)S(1)} async-done(((bf16[8,128,512]{2,1,0:T(8,128)(2,1)}), bf16[8,128,512]{2,1,0:T(8,128)(2,1)S(1)}, u32[]{:S(2)}, u32[]{:S(2)}) %all-to-all-start.2) | async-done | bytes 1048608 | tf_op jit(solution)/shard_map/all_to_all | solution.py:206
  309.9 0.1 convert_reduce_fusion
  310.1 0.2 copy.9
  310.3 0.9 copy.10
  (4 shorter events, 0.1 us)
Async XLA Ops:
  6.5 169.3 %reduce-scatter.2.cloned.1.call-start = ((), (), s32[]{:S(2)}) async-start(), calls=%async_computation.5 | async-start | bytes 2359296 | tf_op jit(solution)/shard_map/reduce_scatter | solution.py:195
  136.2 1.1 copy-start.1
  136.2 91.1 %all-gather.2.cloned.1.call-start = ((), (), s32[]{:S(2)}) async-start(), calls=%async_computation.4 | async-start | bytes 2359296 | tf_op jit(solution)/shard_map/all_gather | solution.py:189
  177.9 52.5 %all-to-all-start.1 = ((bf16[8,128,512]{2,1,0:T(8,128)(2,1)}), bf16[8,128,512]{2,1,0:T(8,128)(2,1)S(1)}, u32[]{:S(2)}, u32[]{:S(2)}) async-start(bf16[8,128,512]{2,1,0:T(8,128)(2,1)} %bitcast.6), calls=%async_computation.2 | async-start | bytes 2097152 | tf_op jit(solution)/shard_map/all_to_all | solution.py:201
  227.3 45.1 %collective-permute-start = (bf16[1024,1024]{1,0:T(8,128)(2,1)}, bf16[1024,1024]{1,0:T(8,128)(2,1)S(1)}, u32[]{:S(2)}, u32[]{:S(2)}) collective-permute-start(bf16[1024,1024]{1,0:T(8,128)(2,1)} %all-gather.2.cloned.1.call-done.near), channel_id=1, source_target_pairs={{0,64},{64,0},{1,65},{65,1},{2,66},{66,2},{3,67},{67,3},{4,68},{68... | collective-permute-start | bytes 6291464 | tf_op jit(solution)/shard_map/ppermute | solution.py:194
  230.4 42.0 %collective-permute-start.1 = (bf16[8,128,512]{2,1,0:T(8,128)(2,1)S(1)}, bf16[8,128,512]{2,1,0:T(8,128)(2,1)S(1)}, u32[]{:S(2)}, u32[]{:S(2)}) collective-permute-start(bf16[8,128,512]{2,1,0:T(8,128)(2,1)S(1)} %all-to-all-done.1.own), channel_id=1, source_target_pairs={{0,8},{8,0},{1,9},{9,1},{2,10},{10,2},{3,11},{11,3},{4,12},{12,4},... | collective-permute-start | bytes 3145736 | tf_op jit(solution)/shard_map/ppermute | solution.py:202
  272.4 1.6 copy-start
  278.4 31.6 %all-to-all-start.2 = ((bf16[8,128,512]{2,1,0:T(8,128)(2,1)}), bf16[8,128,512]{2,1,0:T(8,128)(2,1)S(1)}, u32[]{:S(2)}, u32[]{:S(2)}) async-start(bf16[8,128,512]{2,1,0:T(8,128)(2,1)} %bitcast.7), calls=%async_computation.3 | async-start | bytes 2097152 | tf_op jit(solution)/shard_map/all_to_all | solution.py:206
Sparse Core Ops, SparseCore 0:
  136.4 39.4 reduce-scatter.1
  177.8 49.4 all-gather.1

commit v2 on v1

v2 whole, which is shorter than its diff:
```python
import jax
import jax.numpy as jnp
from jax import lax
from jax.experimental import pallas as pl
from jax.experimental.pallas import tpu as pltpu
from jax.sharding import Mesh, PartitionSpec as P

TILE = 128
SIDE = 8
CAP = 16
BODY = CAP * TILE
META = 16
LAST = TILE - 1
MIB = 1 << 20
VMEM_MIB = 60


def pack_kernel(owners, slots, pattern, contributions, density, out, sparse, count, listed):
    step = pl.program_id(0)
    per = contributions.shape[0]

    @pl.when(step == 0)
    def _():
        for r in range(SIDE):
            count[r] = 0
        listed[...] = jnp.zeros_like(listed)

    row = lax.broadcasted_iota(jnp.int32, (SIDE, TILE), 0)
    lane = lax.broadcasted_iota(jnp.int32, (SIDE, TILE), 1)

    def one(i, places):
        index = step * per + i
        owner = owners[index]
        r = owner // SIDE
        c = owner - r * SIDE
        pos = count[r]
        count[r] = pos + 1
        out[r, pl.ds(pl.multiple_of(pos * TILE, TILE), TILE)] = contributions[i]
        here = (row == r) & (lane == pos)
        return jnp.where(here, c * SIDE + slots[index], places)

    listed[...] = lax.fori_loop(0, per, one, listed[...], unroll=True)
    tile_row = lax.axis_index(("rx", "rc")) * SIDE + step
    tile_col = lax.axis_index(("col", "lg", "lq"))
    keep = pattern[tile_row, tile_col].astype(jnp.float32)
    sparse[...] = (density[...].astype(jnp.float32) * keep).astype(jnp.bfloat16)

    @pl.when(step == pl.num_programs(0) - 1)
    def _():
        values = listed[...]
        for r in range(SIDE):
            values = jnp.where((row == r) & (lane == LAST), count[r], values)
        values = values.astype(jnp.float32)
        for r in range(SIDE):
            out[r, BODY:] = jnp.broadcast_to(values[r : r + 1], (META, TILE)).astype(jnp.bfloat16)


def pack(owners, slots, pattern, contributions, density):
    per = contributions.shape[0] // SIDE
    shape = (SIDE, BODY + META, TILE)
    return pl.pallas_call(
        pack_kernel,
        out_shape=(
            jax.ShapeDtypeStruct(shape, jnp.bfloat16),
            jax.ShapeDtypeStruct(density.shape, jnp.bfloat16),
        ),
        grid=(SIDE,),
        in_specs=[
            pl.BlockSpec(memory_space=pltpu.SMEM),
            pl.BlockSpec(memory_space=pltpu.SMEM),
            pl.BlockSpec(memory_space=pltpu.SMEM),
            pl.BlockSpec((per, TILE, TILE), lambda i: (i, 0, 0)),
            pl.BlockSpec((TILE, TILE), lambda i: (i, 0)),
        ],
        out_specs=(
            pl.BlockSpec(shape, lambda i: (0, 0, 0)),
            pl.BlockSpec((TILE, TILE), lambda i: (i, 0)),
        ),
        scratch_shapes=[pltpu.SMEM((SIDE,), jnp.int32), pltpu.VMEM((SIDE, TILE), jnp.int32)],
        compiler_params=pltpu.CompilerParams(vmem_limit_bytes=VMEM_MIB * MIB),
        cost_estimate=pl.CostEstimate(flops=0, bytes_accessed=7 * MIB, transcendentals=0),
        name="pack",
    )(owners, slots, pattern, contributions, density)


def combine_kernel(got, near, out, data, meta, places, table, total, sems, meta_sem, table_sem):
    head = pltpu.make_async_copy(got.at[:, pl.ds(BODY, META)], meta, meta_sem)
    head.start()
    loads = [
        pltpu.make_async_copy(got.at[r, pl.ds(0, BODY)], data.at[r], sems.at[r])
        for r in range(SIDE)
    ]
    for load in loads:
        load.start()
    total[...] = jnp.zeros_like(total)
    head.wait()
    for r in range(SIDE):
        places[r : r + 1] = meta[r].astype(jnp.float32)[:1].astype(jnp.int32)
    listing = pltpu.make_async_copy(places, table, table_sem)
    listing.start()
    listing.wait()
    for r in range(SIDE):
        loads[r].wait()

        def one(pos, carry, r=r):
            place = table[r, pos]
            rows = pl.ds(pl.multiple_of(pos * TILE, TILE), TILE)
            total[place] += data[r, rows].astype(jnp.float32)
            return carry

        lax.fori_loop(0, table[r, LAST], one, 0)

    def write(c, carry):
        for s in range(SIDE):
            columns = slice(s % 4 * TILE, (s % 4 + 1) * TILE)
            out[c, s // 4, :, columns] = total[c * SIDE + s].astype(jnp.bfloat16)
        return carry

    lax.fori_loop(0, SIDE, write, 0)


def combine(got, near):
    return pl.pallas_call(
        combine_kernel,
        out_shape=jax.ShapeDtypeStruct((SIDE, 2, TILE, SIDE * TILE // 2), jnp.bfloat16),
        in_specs=[pl.BlockSpec(memory_space=pl.ANY), pl.BlockSpec(memory_space=pl.ANY)],
        out_specs=pl.BlockSpec(memory_space=pltpu.VMEM),
        scratch_shapes=[
            pltpu.VMEM((SIDE, BODY, TILE), jnp.bfloat16),
            pltpu.VMEM((SIDE, META, TILE), jnp.bfloat16),
            pltpu.VMEM((SIDE, TILE), jnp.int32),
            pltpu.SMEM((SIDE, TILE), jnp.int32),
            pltpu.VMEM((SIDE * SIDE, TILE, TILE), jnp.float32),
            pltpu.SemaphoreType.DMA((SIDE,)),
            pltpu.SemaphoreType.DMA,
            pltpu.SemaphoreType.DMA,
        ],
        compiler_params=pltpu.CompilerParams(vmem_limit_bytes=VMEM_MIB * MIB),
        cost_estimate=pl.CostEstimate(
            flops=4 * MIB, bytes_accessed=6 * MIB, transcendentals=0
        ),
        name="combine",
    )(got, near)


def spread_kernel(ham, far, out):
    for half in range(2):
        rows = ham[half * TILE : (half + 1) * TILE]
        for chip in range(4):
            out[half * 4 + chip] = rows


def spread(ham, far):
    depth, width = ham.shape
    return pl.pallas_call(
        spread_kernel,
        out_shape=jax.ShapeDtypeStruct((SIDE, TILE, width), jnp.bfloat16),
        in_specs=[pl.BlockSpec(memory_space=pltpu.VMEM), pl.BlockSpec(memory_space=pl.ANY)],
        out_specs=pl.BlockSpec(memory_space=pltpu.VMEM),
        compiler_params=pltpu.CompilerParams(vmem_limit_bytes=VMEM_MIB * MIB),
        cost_estimate=pl.CostEstimate(flops=0, bytes_accessed=2 * MIB, transcendentals=0),
        name="spread",
    )(ham, far)


def product_kernel(near, far_top, far_bottom, own, other, out, ham):
    half = near.shape[1]
    core, layer = lax.axis_index("rc"), lax.axis_index("lq")
    step = pl.program_id(0)

    @pl.when(step == 0)
    def _():
        for l in range(2):
            base = jnp.where(layer == l, 0, half)
            for j in range(SIDE // 2):
                mine = base + (2 * j + core) * TILE
                theirs = base + (2 * j + 1 - core) * TILE
                ham[pl.ds(pl.multiple_of(mine, TILE), TILE)] = own[l * 4 + j]
                ham[pl.ds(pl.multiple_of(theirs, TILE), TILE)] = other[l * 4 + j]

    def both(far):
        total = jnp.dot(near[...], ham[:half], preferred_element_type=jnp.float32)
        total += jnp.dot(far[...], ham[half:], preferred_element_type=jnp.float32)
        out[...] = total.astype(jnp.bfloat16)

    @pl.when(step < pl.num_programs(0) // 2)
    def _():
        both(far_top)

    @pl.when(step >= pl.num_programs(0) // 2)
    def _():
        both(far_bottom)


def product_of(near, far_top, far_bottom, own, other):
    rows, half = near.shape
    step = 256
    turn = rows // step // 2
    width = own.shape[2]
    return pl.pallas_call(
        product_kernel,
        out_shape=jax.ShapeDtypeStruct((rows, width), jnp.bfloat16),
        grid=(rows // step,),
        in_specs=[
            pl.BlockSpec((step, half), lambda i: (i, 0)),
            pl.BlockSpec((step, half), lambda i: (jnp.minimum(i, turn - 1), 0)),
            pl.BlockSpec((step, half), lambda i: (jnp.maximum(i, turn) - turn, 0)),
            pl.BlockSpec(own.shape, lambda i: (0, 0, 0)),
            pl.BlockSpec(own.shape, lambda i: (0, 0, 0)),
        ],
        out_specs=pl.BlockSpec((step, width), lambda i: (i, 0)),
        scratch_shapes=[pltpu.VMEM((2 * half, width), jnp.bfloat16)],
        compiler_params=pltpu.CompilerParams(vmem_limit_bytes=VMEM_MIB * MIB),
        cost_estimate=pl.CostEstimate(
            flops=4 * rows * half * width, bytes_accessed=7 * MIB, transcendentals=0
        ),
        name="product",
    )(near, far_top, far_bottom, own, other)


def finish_kernel(pattern, terms, out):
    tile_row = lax.axis_index(("rx", "rc", "lg", "lq"))
    tile_col = lax.axis_index("col") * SIDE
    for t in range(SIDE):
        columns = slice(t % 4 * TILE, (t % 4 + 1) * TILE)
        total = jnp.zeros((TILE, TILE), jnp.float32)
        for group in range(4):
            total += terms[group * 2 + t // 4, :, columns].astype(jnp.float32)
        keep = pattern[tile_row, tile_col + t].astype(jnp.float32)
        out[:, t * TILE : (t + 1) * TILE] = (total * keep).astype(jnp.bfloat16)


def finish(pattern, terms):
    return pl.pallas_call(
        finish_kernel,
        out_shape=jax.ShapeDtypeStruct((TILE, SIDE * TILE), jnp.bfloat16),
        in_specs=[
            pl.BlockSpec(memory_space=pltpu.SMEM),
            pl.BlockSpec(memory_space=pltpu.VMEM),
        ],
        out_specs=pl.BlockSpec(memory_space=pltpu.VMEM),
        compiler_params=pltpu.CompilerParams(vmem_limit_bytes=VMEM_MIB * MIB),
        cost_estimate=pl.CostEstimate(flops=MIB, bytes_accessed=2 * MIB, transcendentals=0),
        name="finish",
    )(pattern, terms)


def body(density, contributions, owners, slots, pattern):
    packed, sparse = pack(owners.reshape(-1), slots, pattern, contributions, density)
    near = lax.all_gather(sparse, "col", axis=1, tiled=True)
    got = lax.all_to_all(packed, ("rx", "rc"), split_axis=0, concat_axis=0, tiled=True)
    partial_ham = combine(got, near)
    swap = [(0, 1), (1, 0)]
    rows = near.shape[0]
    far_top = lax.ppermute(near[: rows // 2], "lq", swap)
    far_bottom = lax.ppermute(near[rows // 2 :], "lq", swap)
    depth, width = partial_ham.shape[2:]
    ham = lax.psum_scatter(
        partial_ham.reshape(-1, width), "col", scatter_dimension=0, tiled=True
    )
    own = lax.all_to_all(
        spread(ham, far_top), ("lq", "rx"), split_axis=0, concat_axis=0, tiled=True
    )
    other = lax.ppermute(own, "rc", swap)
    term = product_of(near, far_top, far_bottom, own, other)
    terms = lax.all_to_all(
        term.reshape(SIDE, TILE, width), ("lg", "lq"), split_axis=0, concat_axis=0, tiled=True
    )
    return finish(pattern, terms)


def solution(mesh):
    layers, grid_rows, grid_cols = mesh.devices.shape
    split = Mesh(
        mesh.devices.reshape(layers // 2, 2, grid_rows // 2, 2, grid_cols),
        ("lg", "lq", "rx", "rc", "col"),
    )
    layer, row = ("lg", "lq"), ("rx", "rc")
    return jax.shard_map(
        body,
        mesh=split,
        in_specs=(
            P(row, ("col", *layer)),
            P((*layer, *row, "col"), None, None),
            P((*layer, *row, "col"), None),
            P((*layer, *row, "col")),
            P(),
        ),
        out_specs=P((*row, *layer), "col"),
        check_vma=False,
    )
```

time: 322 us -> 211 us (0.66)
  the two profiles are of different devices: /device:TPU:1 before, /device:TPU:6 now
where the time goes in v2:
time: 211 us
  waiting for transfers between devices  117 us (55%)
  blocking collectives  29.4 us (14%)
  starting transfers between devices  24.8 us (12%)
  Pallas kernels  23.1 us (11%)
  between operations  13.5 us (6%)
  local copies, waits for them, and re-layouts  2.7 us (1%)
    all_gather x1, waiting for transfers between devices, body(): near = lax.all_gather(sparse, 'col', axis=1, tiled=True)  51.3 us
    all_to_all x1, blocking collectives, body(): lax.all_to_all(term.reshape(SIDE, TILE, width), ('lg', 'lq'), split_axis=...  29.4 us
    ppermute x1, waiting for transfers between devices, body(): far_top = lax.ppermute(near[:rows // 2], 'lq', swap)  20 us
    reduce_scatter x1, waiting for transfers between devices, body(): lax.psum_scatter(partial_ham.reshape(-1, width), 'col', scatter_dimension...  19.1 us
    ppermute x1, waiting for transfers between devices, body(): far_bottom = lax.ppermute(near[rows // 2:], 'lq', swap)  15 us
    all_to_all x1, waiting for transfers between devices, body(): lax.all_to_all(spread(ham, far_top), ('lq', 'rx'), split_axis=0, concat_a...  11.1 us
    all_to_all x1, starting transfers between devices, body(): lax.all_to_all(packed, ('rx', 'rc'), split_axis=0, concat_axis=0, tiled=T...  10.3 us
    pallas_call x1, Pallas kernels, pack(): pl.pallas_call(pack_kernel, out_shape=(jax.ShapeDtypeStruct(shape, jnp.bf...  7.43 us
  transfers between devices with their start and end apart: 7, of which 5 were waited for; matrix products, arithmetic and copies ran while one was open for 0% of the time, Pallas kernels for 0%

profile of v2, /device:TPU:6, one launch (start us, length us, event | category | flops | bytes accessed | tf_op | source)
XLA Modules:
  0.0 210.8 jit_solution(4113314776219410483)
XLA Ops:
  6.5 7.4 %pack.1 = (bf16[8,2064,128]{2,1,0:T(8,128)(2,1)}, bf16[1024,128]{1,0:T(8,128)(2,1)}) custom-call(s32[64]{0:T(128)} %bitcast.5, s32[64]{0:T(128)} %slots.1, s32[64,64]{1,0:T(8,128)} %pattern.3, bf16[64,128,128]{2,1,0:T(8,128)(2,1)} %contributions.1, bf16[1024,128]{1,0:T(8,128)(2,1)} %density.1), custom_call_target="tpu_custom_call" | custom-call | bytes 7340032 | tf_op jit(solution)/shard_map/pack/pallas_call | solution.py:61
  14.0 10.3 %all-to-all-start = ((bf16[8,2064,128]{2,1,0:T(8,128)(2,1)}), bf16[8,2064,128]{2,1,0:T(8,128)(2,1)}, u32[]{:S(2)}, u32[]{:S(2)}) async-start(bf16[8,2064,128]{2,1,0:T(8,128)(2,1)} %get-tuple-element.8), calls=%async_computation | async-start | bytes 8454144 | tf_op jit(solution)/shard_map/all_to_all | solution.py:251
  24.3 0.0 all-gather.2.cloned.1.call-start
  24.3 0.7 all-gather.2.cloned.1.call-update
  25.0 0.0 reduce-scatter.2.cloned.1.call-start
  25.0 51.3 %all-gather.2.cloned.1.call-done.near = bf16[1024,1024]{1,0:T(8,128)(2,1)} async-done(((bf16[1024,128]{1,0:T(8,128)(2,1)}), bf16[1024,1024]{1,0:T(8,128)(2,1)}) %all-gather.2.cloned.1.call-update) | async-done | bytes 2097168 | tf_op jit(solution)/shard_map/all_gather | solution.py:250
  76.3 0.0 all-to-all-done.got
  76.3 5.0 %combine.1 = bf16[8,2,128,512]{3,2,1,0:T(8,128)(2,1)} custom-call(bf16[8,2064,128]{2,1,0:T(8,128)(2,1)} %all-to-all-done.got, bf16[1024,1024]{1,0:T(8,128)(2,1)} %all-gather.2.cloned.1.call-done.near), custom_call_target="tpu_custom_call" | custom-call | flops 4194304 | bytes 6291456 | tf_op jit(solution)/shard_map/combine/pallas_call | solution.py:123
  81.3 0.0 copy-start
  81.3 0.0 reduce-scatter.2.cloned.1.call-update
  81.4 1.6 copy-done
  82.9 0.2 fusion
  83.1 3.5 %collective-permute-start = (bf16[512,1024]{1,0:T(8,128)(2,1)S(1)}, bf16[512,1024]{1,0:T(8,128)(2,1)S(1)}, u32[]{:S(2)}, u32[]{:S(2)}) collective-permute-start(bf16[512,1024]{1,0:T(8,128)(2,1)S(1)} %get-tuple-element.10), channel_id=1, source_target_pairs={{0,64},{64,0},{1,65},{65,1},{2,66},{66,2},{3,67},{67,3},{4,68},{68... | collective-permute-start | bytes 3145736 | tf_op jit(solution)/shard_map/ppermute | solution.py:255
  86.6 20.0 %collective-permute-done.far.far_top = bf16[512,1024]{1,0:T(8,128)(2,1)S(1)} collective-permute-done((bf16[512,1024]{1,0:T(8,128)(2,1)S(1)}, bf16[512,1024]{1,0:T(8,128)(2,1)S(1)}, u32[]{:S(2)}, u32[]{:S(2)}) %collective-permute-start) | collective-permute-done | bytes 1048608 | tf_op jit(solution)/shard_map/ppermute | solution.py:255
  106.6 0.0 copy-start.1
  106.6 19.1 %reduce-scatter.2.cloned.1.call-done.ham = bf16[256,512]{1,0:T(8,128)(2,1)} async-done(((bf16[2048,512]{1,0:T(8,128)(2,1)}), bf16[256,512]{1,0:T(8,128)(2,1)}) %reduce-scatter.2.cloned.1.call-update) | async-done | bytes 262160 | tf_op jit(solution)/shard_map/reduce_scatter | solution.py:258
  125.7 0.0 copy-done.1
  125.7 2.0 spread.1
  127.7 5.7 %all-to-all-start.1 = ((bf16[8,128,512]{2,1,0:T(8,128)(2,1)}), bf16[8,128,512]{2,1,0:T(8,128)(2,1)S(1)}, u32[]{:S(2)}, u32[]{:S(2)}) async-start(bf16[8,128,512]{2,1,0:T(8,128)(2,1)} %spread.1), calls=%async_computation.2 | async-start | bytes 2097152 | tf_op jit(solution)/shard_map/all_to_all | solution.py:261
  133.4 3.4 %collective-permute-start.1 = (bf16[512,1024]{1,0:T(8,128)(2,1)S(1)}, bf16[512,1024]{1,0:T(8,128)(2,1)S(1)}, u32[]{:S(2)}, u32[]{:S(2)}) collective-permute-start(bf16[512,1024]{1,0:T(8,128)(2,1)S(1)} %get-tuple-element.9), channel_id=1, source_target_pairs={{0,64},{64,0},{1,65},{65,1},{2,66},{66,2},{3,67},{67,3},{4,68},{68... | collective-permute-start | bytes 3145736 | tf_op jit(solution)/shard_map/ppermute | solution.py:256
  136.8 11.1 %all-to-all-done.1.own = bf16[8,128,512]{2,1,0:T(8,128)(2,1)S(1)} async-done(((bf16[8,128,512]{2,1,0:T(8,128)(2,1)}), bf16[8,128,512]{2,1,0:T(8,128)(2,1)S(1)}, u32[]{:S(2)}, u32[]{:S(2)}) %all-to-all-start.1) | async-done | bytes 1048608 | tf_op jit(solution)/shard_map/all_to_all | solution.py:261
  148.0 0.0 copy-start.2
  148.0 1.9 collective-permute-start.2
  149.9 15.0 %collective-permute-done.1.far_bottom = bf16[512,1024]{1,0:T(8,128)(2,1)S(1)} collective-permute-done((bf16[512,1024]{1,0:T(8,128)(2,1)S(1)}, bf16[512,1024]{1,0:T(8,128)(2,1)S(1)}, u32[]{:S(2)}, u32[]{:S(2)}) %collective-permute-start.1) | collective-permute-done | bytes 1048608 | tf_op jit(solution)/shard_map/ppermute | solution.py:256
  164.8 0.0 copy-start.3
  164.8 0.0 collective-permute-done.2.other
  164.9 0.0 copy-done.2
  164.9 1.0 copy-done.3
  165.8 6.6 %product.1 = bf16[1024,512]{1,0:T(8,128)(2,1)} custom-call(bf16[1024,1024]{1,0:T(8,128)(2,1)} %all-gather.2.cloned.1.call-done.near, bf16[512,1024]{1,0:T(8,128)(2,1)} %copy-done.1, bf16[512,1024]{1,0:T(8,128)(2,1)} %copy-done.3, bf16[8,128,512]{2,1,0:T(8,128)(2,1)} %copy-done.2, bf16[8,128,512]{2,1,0:T(8,128)(2,1)} %collective-permute-done.2.other), custom_call_target="tpu_custom_call" | custom-call | flops 2147483648 | bytes 7340032 | tf_op jit(solution)/shard_map/product/pallas_call | solution.py:200
  172.4 29.4 %all_to_all.15.terms = bf16[8,128,512]{2,1,0:T(8,128)(2,1)} all-to-all(bf16[8,128,512]{2,1,0:T(8,128)(2,1)} %bitcast.4), channel_id=1, replica_groups=mesh['lg'=4,'lq'=2,'rx'=4,'rc'=2,'col'=8] {'lg','lq'}, dimensions={0} | all-to-all | bytes 2097152 | tf_op jit(solution)/shard_map/all_to_all | solution.py:266
  201.8 2.1 finish.1
Async XLA Ops:
  14.0 62.4 %all-to-all-start = ((bf16[8,2064,128]{2,1,0:T(8,128)(2,1)}), bf16[8,2064,128]{2,1,0:T(8,128)(2,1)}, u32[]{:S(2)}, u32[]{:S(2)}) async-start(bf16[8,2064,128]{2,1,0:T(8,128)(2,1)} %get-tuple-element.8), calls=%async_computation | async-start | bytes 8454144 | tf_op jit(solution)/shard_map/all_to_all | solution.py:251
  24.3 52.1 %all-gather.2.cloned.1.call-start = ((), (), s32[]{:S(2)}) async-start(), calls=%async_computation.4 | async-start | bytes 2359296 | tf_op jit(solution)/shard_map/all_gather | solution.py:250
  25.0 100.7 %reduce-scatter.2.cloned.1.call-start = ((), (), s32[]{:S(2)}) async-start(), calls=%async_computation.5 | async-start | bytes 2359296 | tf_op jit(solution)/shard_map/reduce_scatter | solution.py:258
  81.3 1.6 copy-start
  83.1 23.5 %collective-permute-start = (bf16[512,1024]{1,0:T(8,128)(2,1)S(1)}, bf16[512,1024]{1,0:T(8,128)(2,1)S(1)}, u32[]{:S(2)}, u32[]{:S(2)}) collective-permute-start(bf16[512,1024]{1,0:T(8,128)(2,1)S(1)} %get-tuple-element.10), channel_id=1, source_target_pairs={{0,64},{64,0},{1,65},{65,1},{2,66},{66,2},{3,67},{67,3},{4,68},{68... | collective-permute-start | bytes 3145736 | tf_op jit(solution)/shard_map/ppermute | solution.py:255
  106.6 19.1 %copy-start.1 = (bf16[512,1024]{1,0:T(8,128)(2,1)}, bf16[512,1024]{1,0:T(8,128)(2,1)S(1)}, u32[]{:S(2)}) copy-start(bf16[512,1024]{1,0:T(8,128)(2,1)S(1)} %collective-permute-done.far.far_top) | copy-start | bytes 3145732
  127.7 20.2 %all-to-all-start.1 = ((bf16[8,128,512]{2,1,0:T(8,128)(2,1)}), bf16[8,128,512]{2,1,0:T(8,128)(2,1)S(1)}, u32[]{:S(2)}, u32[]{:S(2)}) async-start(bf16[8,128,512]{2,1,0:T(8,128)(2,1)} %spread.1), calls=%async_computation.2 | async-start | bytes 2097152 | tf_op jit(solution)/shard_map/all_to_all | solution.py:261
  133.4 31.4 %collective-permute-start.1 = (bf16[512,1024]{1,0:T(8,128)(2,1)S(1)}, bf16[512,1024]{1,0:T(8,128)(2,1)S(1)}, u32[]{:S(2)}, u32[]{:S(2)}) collective-permute-start(bf16[512,1024]{1,0:T(8,128)(2,1)S(1)} %get-tuple-element.9), channel_id=1, source_target_pairs={{0,64},{64,0},{1,65},{65,1},{2,66},{66,2},{3,67},{67,3},{4,68},{68... | collective-permute-start | bytes 3145736 | tf_op jit(solution)/shard_map/ppermute | solution.py:256
  148.0 16.9 %copy-start.2 = (bf16[8,128,512]{2,1,0:T(8,128)(2,1)}, bf16[8,128,512]{2,1,0:T(8,128)(2,1)S(1)}, u32[]{:S(2)}) copy-start(bf16[8,128,512]{2,1,0:T(8,128)(2,1)S(1)} %all-to-all-done.1.own) | copy-start | bytes 3145732
  148.0 16.9 %collective-permute-start.2 = (bf16[8,128,512]{2,1,0:T(8,128)(2,1)S(1)}, bf16[8,128,512]{2,1,0:T(8,128)(2,1)}, u32[]{:S(2)}, u32[]{:S(2)}) collective-permute-start(bf16[8,128,512]{2,1,0:T(8,128)(2,1)S(1)} %all-to-all-done.1.own), channel_id=1, source_target_pairs={{0,8},{8,0},{1,9},{9,1},{2,10},{10,2},{3,11},{11,3},{4,12},{12,4},... | collective-permute-start | bytes 3145736 | tf_op jit(solution)/shard_map/ppermute | solution.py:264
  164.8 1.0 copy-start.3
Sparse Core Ops, SparseCore 0:
  27.1 49.1 all-gather.1
  81.5 44.1 reduce-scatter.1

commit v3 on v2

v3 whole, which is shorter than its diff:
```python
import jax
import jax.numpy as jnp
from jax import lax
from jax.experimental import pallas as pl
from jax.experimental.pallas import tpu as pltpu
from jax.sharding import Mesh, PartitionSpec as P

TILE = 128
SIDE = 8
CAP = 16
BODY = CAP * TILE
META = 16
LAST = TILE - 1
MIB = 1 << 20
VMEM_MIB = 60
SMALL_MIB = 20


def pack_kernel(
    owners, slots, pattern, contributions, density, out, masked, data, meta, count, sems, sem, meta_sem
):
    per = contributions.shape[0] // SIDE
    loads = [
        pltpu.make_async_copy(
            contributions.at[pl.ds(k * per, per)], data.at[pl.ds(k * per, per)], sems.at[k]
        )
        for k in range(SIDE)
    ]
    for load in loads:
        load.start()
    tile_row = lax.axis_index(("rx", "rc")) * SIDE
    tile_col = lax.axis_index(("ch", "cl", "lg", "lq"))
    for t in range(SIDE):
        rows = slice(t * TILE, (t + 1) * TILE)
        keep = pattern[tile_row + t, tile_col].astype(jnp.float32)
        masked[rows] = (density[rows].astype(jnp.float32) * keep).astype(jnp.bfloat16)
        count[t] = 0
    row = lax.broadcasted_iota(jnp.int32, (SIDE, TILE), 0)
    lane = lax.broadcasted_iota(jnp.int32, (SIDE, TILE), 1)
    places = jnp.zeros((SIDE, TILE), jnp.int32)
    for k in range(SIDE):
        loads[k].wait()

        def one(i, places, k=k):
            index = k * per + i
            owner = owners[index]
            r = owner // SIDE
            c = owner - r * SIDE
            pos = count[r]
            count[r] = pos + 1
            pltpu.make_async_copy(
                data.at[index], out.at[r, pl.ds(pl.multiple_of(pos * TILE, TILE), TILE)], sem
            ).start()
            here = (row == r) & (lane == pos)
            return jnp.where(here, c * SIDE + slots[index], places)

        places = lax.fori_loop(0, per, one, places, unroll=True)
    for r in range(SIDE):
        places = jnp.where((row == r) & (lane == LAST), count[r], places)
    values = places.astype(jnp.float32)
    for r in range(SIDE):
        meta[r] = jnp.broadcast_to(values[r : r + 1], (META, TILE)).astype(jnp.bfloat16)
    tail = pltpu.make_async_copy(meta, out.at[:, pl.ds(BODY, META)], meta_sem)
    tail.start()
    tail.wait()
    pltpu.make_async_copy(data, data, sem).wait()


def pack(owners, slots, pattern, contributions, density):
    return pl.pallas_call(
        pack_kernel,
        out_shape=(
            jax.ShapeDtypeStruct((SIDE, BODY + META, TILE), jnp.bfloat16),
            jax.ShapeDtypeStruct(density.shape, jnp.bfloat16),
        ),
        in_specs=[
            pl.BlockSpec(memory_space=pltpu.SMEM),
            pl.BlockSpec(memory_space=pltpu.SMEM),
            pl.BlockSpec(memory_space=pltpu.SMEM),
            pl.BlockSpec(memory_space=pl.ANY),
            pl.BlockSpec(memory_space=pltpu.VMEM),
        ],
        out_specs=(pl.BlockSpec(memory_space=pl.ANY), pl.BlockSpec(memory_space=pltpu.VMEM)),
        scratch_shapes=[
            pltpu.VMEM(contributions.shape, jnp.bfloat16),
            pltpu.VMEM((SIDE, META, TILE), jnp.bfloat16),
            pltpu.SMEM((SIDE,), jnp.int32),
            pltpu.SemaphoreType.DMA((SIDE,)),
            pltpu.SemaphoreType.DMA,
            pltpu.SemaphoreType.DMA,
        ],
        compiler_params=pltpu.CompilerParams(vmem_limit_bytes=VMEM_MIB * MIB),
        cost_estimate=pl.CostEstimate(flops=0, bytes_accessed=7 * MIB, transcendentals=0),
        name="pack",
    )(owners, slots, pattern, contributions, density)


def combine_kernel(got, near, keep, send, data, meta, places, table, total, sems, meta_sem, table_sem):
    head = pltpu.make_async_copy(got.at[:, pl.ds(BODY, META)], meta, meta_sem)
    head.start()
    loads = [
        pltpu.make_async_copy(got.at[r, pl.ds(0, BODY)], data.at[r], sems.at[r])
        for r in range(SIDE)
    ]
    for load in loads:
        load.start()
    total[...] = jnp.zeros_like(total)
    head.wait()
    for r in range(SIDE):
        places[r : r + 1] = meta[r].astype(jnp.float32)[:1].astype(jnp.int32)
    listing = pltpu.make_async_copy(places, table, table_sem)
    listing.start()
    listing.wait()
    for r in range(SIDE):
        loads[r].wait()

        def one(pos, carry, r=r):
            place = table[r, pos]
            rows = pl.ds(pl.multiple_of(pos * TILE, TILE), TILE)
            total[place] += data[r, rows].astype(jnp.float32)
            return carry

        lax.fori_loop(0, table[r, LAST], one, 0)

    parity = lax.axis_index("cl")

    def write(j, carry):
        for s in range(SIDE):
            columns = slice(s % 4 * TILE, (s % 4 + 1) * TILE)
            mine = total[(2 * j + parity) * SIDE + s]
            keep[j, s // 4, :, columns] = mine.astype(jnp.bfloat16)
            theirs = total[(2 * j + 1 - parity) * SIDE + s]
            send[j, s // 4, :, columns] = theirs.astype(jnp.bfloat16)
        return carry

    lax.fori_loop(0, SIDE // 2, write, 0)


def combine(got, near):
    half = jax.ShapeDtypeStruct((SIDE // 2, 2, TILE, SIDE * TILE // 2), jnp.bfloat16)
    return pl.pallas_call(
        combine_kernel,
        out_shape=(half, half),
        in_specs=[pl.BlockSpec(memory_space=pl.ANY), pl.BlockSpec(memory_space=pl.ANY)],
        out_specs=(pl.BlockSpec(memory_space=pltpu.VMEM), pl.BlockSpec(memory_space=pltpu.VMEM)),
        scratch_shapes=[
            pltpu.VMEM((SIDE, BODY, TILE), jnp.bfloat16),
            pltpu.VMEM((SIDE, META, TILE), jnp.bfloat16),
            pltpu.VMEM((SIDE, TILE), jnp.int32),
            pltpu.SMEM((SIDE, TILE), jnp.int32),
            pltpu.VMEM((SIDE * SIDE, TILE, TILE), jnp.float32),
            pltpu.SemaphoreType.DMA((SIDE,)),
            pltpu.SemaphoreType.DMA,
            pltpu.SemaphoreType.DMA,
        ],
        compiler_params=pltpu.CompilerParams(vmem_limit_bytes=VMEM_MIB * MIB),
        cost_estimate=pl.CostEstimate(
            flops=4 * MIB, bytes_accessed=6 * MIB, transcendentals=0
        ),
        name="combine",
    )(got, near)


def spread_kernel(parts, far, out):
    for half in range(2):
        rows = parts[0, half].astype(jnp.float32)
        for part in range(1, parts.shape[0]):
            rows += parts[part, half].astype(jnp.float32)
        rows = rows.astype(jnp.bfloat16)
        for chip in range(4):
            out[half * 4 + chip] = rows


def spread(parts, far):
    depth, width = parts.shape[2:]
    return pl.pallas_call(
        spread_kernel,
        out_shape=jax.ShapeDtypeStruct((SIDE, depth, width), jnp.bfloat16),
        in_specs=[pl.BlockSpec(memory_space=pltpu.VMEM), pl.BlockSpec(memory_space=pl.ANY)],
        out_specs=pl.BlockSpec(memory_space=pltpu.VMEM),
        compiler_params=pltpu.CompilerParams(vmem_limit_bytes=SMALL_MIB * MIB),
        cost_estimate=pl.CostEstimate(flops=MIB, bytes_accessed=2 * MIB, transcendentals=0),
        name="spread",
    )(parts, far)


def product_kernel(near, far, own, other, out, ham):
    half = SIDE * TILE
    core, layer = lax.axis_index("rc"), lax.axis_index("lq")
    column = lax.axis_index(("ch", "cl"))

    @pl.when(pl.program_id(0) == 0)
    def _():
        for l in range(2):
            base = jnp.where(layer == l, 0, half)
            for j in range(SIDE // 2):
                mine = base + (2 * j + core - column + SIDE) % SIDE * TILE
                theirs = base + (2 * j + 1 - core - column + SIDE) % SIDE * TILE
                ham[pl.ds(pl.multiple_of(mine, TILE), TILE)] = own[l * 4 + j]
                ham[pl.ds(pl.multiple_of(theirs, TILE), TILE)] = other[l * 4 + j]

    blocks = [near[c] for c in range(SIDE)] + [far[c] for c in range(SIDE)]
    rows = jnp.concatenate(blocks, axis=1)
    total = jnp.dot(rows, ham[...], preferred_element_type=jnp.float32)
    out[...] = total.astype(jnp.bfloat16)


def product_of(near, far, own, other):
    rows = near.shape[1]
    step = 256
    width = own.shape[2]
    return pl.pallas_call(
        product_kernel,
        out_shape=jax.ShapeDtypeStruct((rows, width), jnp.bfloat16),
        grid=(rows // step,),
        in_specs=[
            pl.BlockSpec((SIDE, step, TILE), lambda i: (0, i, 0)),
            pl.BlockSpec((SIDE, step, TILE), lambda i: (0, i, 0)),
            pl.BlockSpec(own.shape, lambda i: (0, 0, 0)),
            pl.BlockSpec(own.shape, lambda i: (0, 0, 0)),
        ],
        out_specs=pl.BlockSpec((step, width), lambda i: (i, 0)),
        scratch_shapes=[pltpu.VMEM((2 * SIDE * TILE, width), jnp.bfloat16)],
        compiler_params=pltpu.CompilerParams(vmem_limit_bytes=SMALL_MIB * MIB),
        cost_estimate=pl.CostEstimate(
            flops=4 * rows * rows * width, bytes_accessed=7 * MIB, transcendentals=0
        ),
        name="product",
    )(near, far, own, other)


def finish_kernel(pattern, terms, out):
    tile_row = lax.axis_index(("rx", "rc", "lg", "lq"))
    tile_col = lax.axis_index(("ch", "cl")) * SIDE
    for t in range(SIDE):
        columns = slice(t % 4 * TILE, (t % 4 + 1) * TILE)
        total = jnp.zeros((TILE, TILE), jnp.float32)
        for group in range(4):
            total += terms[group * 2 + t // 4, :, columns].astype(jnp.float32)
        keep = pattern[tile_row, tile_col + t].astype(jnp.float32)
        out[:, t * TILE : (t + 1) * TILE] = (total * keep).astype(jnp.bfloat16)


def finish(pattern, terms):
    return pl.pallas_call(
        finish_kernel,
        out_shape=jax.ShapeDtypeStruct((TILE, SIDE * TILE), jnp.bfloat16),
        in_specs=[
            pl.BlockSpec(memory_space=pltpu.SMEM),
            pl.BlockSpec(memory_space=pltpu.VMEM),
        ],
        out_specs=pl.BlockSpec(memory_space=pltpu.VMEM),
        compiler_params=pltpu.CompilerParams(vmem_limit_bytes=SMALL_MIB * MIB),
        cost_estimate=pl.CostEstimate(flops=MIB, bytes_accessed=2 * MIB, transcendentals=0),
        name="finish",
    )(pattern, terms)


def exchange(values, axes):
    return lax.all_to_all(values, axes, split_axis=0, concat_axis=0, tiled=True)


def body(density, contributions, owners, slots, pattern):
    packed, sparse = pack(owners.reshape(-1), slots, pattern, contributions, density)
    got = exchange(packed, ("rx", "rc"))

    def ahead(block, distance):
        return lax.ppermute(
            block, ("ch", "cl"), [(c, (c - distance) % SIDE) for c in range(SIDE)]
        )

    one, last, two, sixth = (ahead(sparse, distance) for distance in (1, -1, 2, -2))
    three, fifth, four = ahead(two, 1), ahead(sixth, -1), ahead(two, 2)
    near = jnp.stack([sparse, one, two, three, four, fifth, sixth, last])
    swap = [(0, 1), (1, 0)]
    far = lax.ppermute(near, "lq", swap)

    keep, send = combine(got, near)
    count = SIDE
    even = [(c, c ^ 1) for c in range(count)]
    odd = [(count + c, count + (c + (1 if c % 2 else -1)) % count) for c in range(count)]
    taken = lax.ppermute(send, ("rc", "ch", "cl"), even + odd)
    parts = exchange(
        (keep.astype(jnp.float32) + taken.astype(jnp.float32)).astype(jnp.bfloat16), "ch"
    )

    own = exchange(spread(parts, far), ("lq", "rx"))
    other = lax.ppermute(own, "rc", swap)
    term = product_of(near, far, own, other)
    terms = exchange(term.reshape(SIDE, TILE, -1), ("lg", "lq"))
    return finish(pattern, terms)


def solution(mesh):
    layers, grid_rows, grid_cols = mesh.devices.shape
    split = Mesh(
        mesh.devices.reshape(layers // 2, 2, grid_rows // 2, 2, grid_cols // 2, 2),
        ("lg", "lq", "rx", "rc", "ch", "cl"),
    )
    layer, row, col = ("lg", "lq"), ("rx", "rc"), ("ch", "cl")
    return jax.shard_map(
        body,
        mesh=split,
        in_specs=(
            P(row, (*col, *layer)),
            P((*layer, *row, *col), None, None),
            P((*layer, *row, *col), None),
            P((*layer, *row, *col)),
            P(),
        ),
        out_specs=P((*row, *layer), col),
        check_vma=False,
    )
```

time: 211 us -> 185 us (0.88)
  the two profiles are of different devices: /device:TPU:6 before, /device:TPU:1 now
where the time goes in v3:
time: 185 us; the launch traced here: 182 us
  waiting for transfers between devices  62.7 us (34%)
  starting transfers between devices  52.2 us (28%)
  blocking collectives  49.1 us (27%)
  Pallas kernels  14.8 us (8%)
  other arithmetic  2.51 us (1%)
    all_to_all x2, blocking collectives, exchange(): return lax.all_to_all(values, axes, split_axis=0, concat_axis=0, tiled=True)  49.1 us
    ppermute x1, waiting for transfers between devices, body(): far = lax.ppermute(near, 'lq', swap)  28.5 us
    ppermute x7, starting transfers between devices, ahead(): lax.ppermute(block, ('ch', 'cl'), [(c, (c - distance) % SIDE) for c in ra...  26.5 us
    all_to_all x2, starting transfers between devices, exchange(): return lax.all_to_all(values, axes, split_axis=0, concat_axis=0, tiled=True)  15.4 us
    ppermute x7, waiting for transfers between devices, ahead(): lax.ppermute(block, ('ch', 'cl'), [(c, (c - distance) % SIDE) for c in ra...  13.3 us
    ppermute x1, waiting for transfers between devices, body(): taken = lax.ppermute(send, ('rc', 'ch', 'cl'), even + odd)  9.21 us
    all_to_all x2, waiting for transfers between devices, exchange(): return lax.all_to_all(values, axes, split_axis=0, concat_axis=0, tiled=True)  9.08 us
    ppermute x1, starting transfers between devices, body(): taken = lax.ppermute(send, ('rc', 'ch', 'cl'), even + odd)  5.27 us
  transfers between devices with their start and end apart: 12, of which 6 were waited for; matrix products, arithmetic and copies ran while one was open for 2% of the time, Pallas kernels for 0%

profile of v3, /device:TPU:1, one launch (start us, length us, event | category | flops | bytes accessed | tf_op | source)
XLA Modules:
  0.0 181.9 jit_solution(14211147574309030774)
XLA Ops:
  0.0 4.3 %pack.1 = (bf16[8,2064,128]{2,1,0:T(8,128)(2,1)}, bf16[1024,128]{1,0:T(8,128)(2,1)}) custom-call(s32[64]{0:T(128)} %bitcast.19, s32[64]{0:T(128)} %slots.1, s32[64,64]{1,0:T(8,128)} %pattern.3, bf16[64,128,128]{2,1,0:T(8,128)(2,1)} %contributions.1, bf16[1024,128]{1,0:T(8,128)(2,1)} %density.1), custom_call_target="tpu_custom_call" | custom-call | bytes 7340032 | tf_op jit(solution)/shard_map/pack/pallas_call | solution.py:70
  4.3 0.0 copy-start.3
  4.3 11.4 %all-to-all-start = ((bf16[8,2064,128]{2,1,0:T(8,128)(2,1)}), bf16[8,2064,128]{2,1,0:T(8,128)(2,1)}, u32[]{:S(2)}, u32[]{:S(2)}) async-start(bf16[8,2064,128]{2,1,0:T(8,128)(2,1)} %get-tuple-element.10), calls=%async_computation | async-start | bytes 8454144 | tf_op jit(solution)/shard_map/all_to_all | solution.py:260
  15.8 5.3 %collective-permute-start.1 = (bf16[1024,128]{1,0:T(8,128)(2,1)S(1)}, bf16[1024,128]{1,0:T(8,128)(2,1)S(1)}, u32[]{:S(2)}, u32[]{:S(2)}) collective-permute-start(bf16[1024,128]{1,0:T(8,128)(2,1)S(1)} %copy-done.3), channel_id=1, source_target_pairs={{0,6},{1,7},{2,0},{3,1},{4,2},{5,3},{6,4},{7,5},{8,14},{9,15},{10,... | collective-permute-start | bytes 786440 | tf_op jit(solution)/shard_map/ppermute | solution.py:268
  21.1 1.9 %collective-permute-start.4 = (bf16[1024,128]{1,0:T(8,128)(2,1)S(1)}, bf16[1024,128]{1,0:T(8,128)(2,1)S(1)}, u32[]{:S(2)}, u32[]{:S(2)}) collective-permute-start(bf16[1024,128]{1,0:T(8,128)(2,1)S(1)} %copy-done.3), channel_id=1, source_target_pairs={{0,2},{1,3},{2,4},{3,5},{4,6},{5,7},{6,0},{7,1},{8,10},{9,11},{10,... | collective-permute-start | bytes 786440 | tf_op jit(solution)/shard_map/ppermute | solution.py:268
  23.0 5.5 %collective-permute-start = (bf16[1024,128]{1,0:T(8,128)(2,1)S(1)}, bf16[1024,128]{1,0:T(8,128)(2,1)S(1)}, u32[]{:S(2)}, u32[]{:S(2)}) collective-permute-start(bf16[1024,128]{1,0:T(8,128)(2,1)S(1)} %copy-done.3), channel_id=1, source_target_pairs={{0,7},{1,0},{2,1},{3,2},{4,3},{5,4},{6,5},{7,6},{8,15},{9,8},{10,9... | collective-permute-start | bytes 786440 | tf_op jit(solution)/shard_map/ppermute | solution.py:268
  28.5 1.9 %collective-permute-start.6 = (bf16[1024,128]{1,0:T(8,128)(2,1)S(1)}, bf16[1024,128]{1,0:T(8,128)(2,1)S(1)}, u32[]{:S(2)}, u32[]{:S(2)}) collective-permute-start(bf16[1024,128]{1,0:T(8,128)(2,1)S(1)} %copy-done.3), channel_id=1, source_target_pairs={{0,1},{1,2},{2,3},{3,4},{4,5},{5,6},{6,7},{7,0},{8,9},{9,10},{10,1... | collective-permute-start | bytes 786440 | tf_op jit(solution)/shard_map/ppermute | solution.py:268
  30.4 0.2 collective-permute-done.1
  30.6 4.9 %collective-permute-start.3 = (bf16[1024,128]{1,0:T(8,128)(2,1)S(1)}, bf16[1024,128]{1,0:T(8,128)(2,1)S(1)}, u32[]{:S(2)}, u32[]{:S(2)}) collective-permute-start(bf16[1024,128]{1,0:T(8,128)(2,1)S(1)} %collective-permute-done.1), channel_id=1, source_target_pairs={{0,6},{1,7},{2,0},{3,1},{4,2},{5,3},{6,4},{7,5},{8,14},{9,15},{10,... | collective-permute-start | bytes 786440 | tf_op jit(solution)/shard_map/ppermute | solution.py:268
  35.5 3.9 %collective-permute-start.2 = (bf16[1024,128]{1,0:T(8,128)(2,1)S(1)}, bf16[1024,128]{1,0:T(8,128)(2,1)S(1)}, u32[]{:S(2)}, u32[]{:S(2)}) collective-permute-start(bf16[1024,128]{1,0:T(8,128)(2,1)S(1)} %collective-permute-done.1), channel_id=1, source_target_pairs={{0,7},{1,0},{2,1},{3,2},{4,3},{5,4},{6,5},{7,6},{8,15},{9,8},{10,9... | collective-permute-start | bytes 786440 | tf_op jit(solution)/shard_map/ppermute | solution.py:268
  39.4 0.0 collective-permute-done.4
  39.4 3.1 %collective-permute-start.5 = (bf16[1024,128]{1,0:T(8,128)(2,1)S(1)}, bf16[1024,128]{1,0:T(8,128)(2,1)S(1)}, u32[]{:S(2)}, u32[]{:S(2)}) collective-permute-start(bf16[1024,128]{1,0:T(8,128)(2,1)S(1)} %collective-permute-done.4), channel_id=1, source_target_pairs={{0,1},{1,2},{2,3},{3,4},{4,5},{5,6},{6,7},{7,0},{8,9},{9,10},{10,1... | collective-permute-start | bytes 786440 | tf_op jit(solution)/shard_map/ppermute | solution.py:268
  42.5 0.0 collective-permute-done
  42.6 13.1 %collective-permute-done.2 = bf16[1024,128]{1,0:T(8,128)(2,1)S(1)} collective-permute-done((bf16[1024,128]{1,0:T(8,128)(2,1)S(1)}, bf16[1024,128]{1,0:T(8,128)(2,1)S(1)}, u32[]{:S(2)}, u32[]{:S(2)}) %collective-permute-start.2) | collective-permute-done | bytes 262176 | tf_op jit(solution)/shard_map/ppermute | solution.py:268
  55.8 0.0 collective-permute-done.3
  55.8 0.0 collective-permute-done.5
  56.0 9.1 %all-to-all-done.got = bf16[8,2064,128]{2,1,0:T(8,128)(2,1)} async-done(((bf16[8,2064,128]{2,1,0:T(8,128)(2,1)}), bf16[8,2064,128]{2,1,0:T(8,128)(2,1)}, u32[]{:S(2)}, u32[]{:S(2)}) %all-to-all-start) | async-done | bytes 4227104 | tf_op jit(solution)/shard_map/all_to_all | solution.py:260
  65.0 5.0 %combine.1 = (bf16[4,2,128,512]{3,2,1,0:T(8,128)(2,1)}, bf16[4,2,128,512]{3,2,1,0:T(8,128)(2,1)}) custom-call(bf16[8,2064,128]{2,1,0:T(8,128)(2,1)} %all-to-all-done.got, bf16[8,1024,128]{2,1,0:T(8,128)(2,1)} %copy-done), custom_call_target="tpu_custom_call" | custom-call | flops 4194304 | bytes 6291456 | tf_op jit(solution)/shard_map/combine/pallas_call | solution.py:141
  70.1 5.3 %collective-permute-start.8 = (bf16[4,2,128,512]{3,2,1,0:T(8,128)(2,1)}, bf16[4,2,128,512]{3,2,1,0:T(8,128)(2,1)S(1)}, u32[]{:S(2)}, u32[]{:S(2)}) collective-permute-start(bf16[4,2,128,512]{3,2,1,0:T(8,128)(2,1)} %get-tuple-element.12), channel_id=1, source_target_pairs={{0,1},{1,0},{2,3},{3,2},{4,5},{5,4},{6,7},{7,6},{8,15},{9,10},{10,... | collective-permute-start | bytes 3145736 | tf_op jit(solution)/shard_map/ppermute | solution.py:282
  75.4 3.2 %collective-permute-start.7 = (bf16[8,1024,128]{2,1,0:T(8,128)(2,1)}, bf16[8,1024,128]{2,1,0:T(8,128)(2,1)S(1)}, u32[]{:S(2)}, u32[]{:S(2)}) collective-permute-start(bf16[8,1024,128]{2,1,0:T(8,128)(2,1)} %copy-done), channel_id=1, source_target_pairs={{0,64},{64,0},{1,65},{65,1},{2,66},{66,2},{3,67},{67,3},{4,68},{68... | collective-permute-start | bytes 6291464 | tf_op jit(solution)/shard_map/ppermute | solution.py:276
  78.5 9.2 %collective-permute-done.8 = bf16[4,2,128,512]{3,2,1,0:T(8,128)(2,1)S(1)} collective-permute-done((bf16[4,2,128,512]{3,2,1,0:T(8,128)(2,1)}, bf16[4,2,128,512]{3,2,1,0:T(8,128)(2,1)S(1)}, u32[]{:S(2)}, u32[]{:S(2)}) %collective-permute-start.8) | collective-permute-done | bytes 1048608 | tf_op jit(solution)/shard_map/ppermute | solution.py:282
  87.7 2.5 %add_convert_fusion = bf16[4,2,128,512]{3,2,1,0:T(8,128)(2,1)} fusion(bf16[4,2,128,512]{3,2,1,0:T(8,128)(2,1)S(1)} %collective-permute-done.8, bf16[4,2,128,512]{3,2,1,0:T(8,128)(2,1)} %get-tuple-element.11), kind=kLoop, calls=%fused_computation | loop fusion | flops 2097152 | bytes 3145728 | tf_op jit(solution)/shard_map/convert_element_type | solution.py:284
  90.3 3.9 %all-to-all-start.1 = ((bf16[4,2,128,512]{3,2,1,0:T(8,128)(2,1)}), bf16[4,2,128,512]{3,2,1,0:T(8,128)(2,1)S(1)}, u32[]{:S(2)}, u32[]{:S(2)}) async-start(bf16[4,2,128,512]{3,2,1,0:T(8,128)(2,1)} %add_convert_fusion), calls=%async_computation.1 | async-start | bytes 2097152 | tf_op jit(solution)/shard_map/all_to_all | solution.py:260
  94.2 28.5 %collective-permute-done.7.far = bf16[8,1024,128]{2,1,0:T(8,128)(2,1)S(1)} collective-permute-done((bf16[8,1024,128]{2,1,0:T(8,128)(2,1)}, bf16[8,1024,128]{2,1,0:T(8,128)(2,1)S(1)}, u32[]{:S(2)}, u32[]{:S(2)}) %collective-permute-start.7) | collective-permute-done | bytes 2097184 | tf_op jit(solution)/shard_map/ppermute | solution.py:276
  122.7 0.1 spread.1
  122.8 17.4 %all_to_all.20.own = bf16[8,128,512]{2,1,0:T(8,128)(2,1)S(1)} all-to-all(bf16[8,128,512]{2,1,0:T(8,128)(2,1)S(1)} %spread.1), channel_id=1, replica_groups=mesh['lg'=4,'lq'=2,'rx'=4,'rc'=2,'ch'=4,'cl'=2] {'lq','rx'}, dimensions={0} | all-to-all | bytes 2097152 | tf_op jit(solution)/shard_map/all_to_all | solution.py:260
  140.3 1.9 %collective-permute-start.9 = (bf16[8,128,512]{2,1,0:T(8,128)(2,1)S(1)}, bf16[8,128,512]{2,1,0:T(8,128)(2,1)S(1)}, u32[]{:S(2)}, u32[]{:S(2)}) collective-permute-start(bf16[8,128,512]{2,1,0:T(8,128)(2,1)S(1)} %all_to_all.20.own), channel_id=1, source_target_pairs={{0,8},{8,0},{1,9},{9,1},{2,10},{10,2},{3,11},{11,3},{4,12},{12,4},... | collective-permute-start | bytes 3145736 | tf_op jit(solution)/shard_map/ppermute | solution.py:288
  142.2 2.6 %collective-permute-done.9.other = bf16[8,128,512]{2,1,0:T(8,128)(2,1)S(1)} collective-permute-done((bf16[8,128,512]{2,1,0:T(8,128)(2,1)S(1)}, bf16[8,128,512]{2,1,0:T(8,128)(2,1)S(1)}, u32[]{:S(2)}, u32[]{:S(2)}) %collective-permute-start.9) | collective-permute-done | bytes 1048608 | tf_op jit(solution)/shard_map/ppermute | solution.py:288
  144.8 3.5 %product.1 = bf16[1024,512]{1,0:T(8,128)(2,1)S(1)} custom-call(bf16[8,1024,128]{2,1,0:T(8,128)(2,1)S(1)} %copy-done.1, bf16[8,1024,128]{2,1,0:T(8,128)(2,1)S(1)} %collective-permute-done.7.far, bf16[8,128,512]{2,1,0:T(8,128)(2,1)S(1)} %all_to_all.20.own, bf16[8,128,512]{2,1,0:T(8,128)(2,1)S(1)} %collective-permute-done.9.other), custom_call_target="tpu_custom_call" | custom-call | flops 2147483648 | bytes 7340032 | tf_op jit(solution)/shard_map/product/pallas_call | solution.py:212
  148.3 0.0 copy-start.2
  148.3 31.6 %all_to_all.21.terms = bf16[8,128,512]{2,1,0:T(8,128)(2,1)S(1)} all-to-all(bf16[8,128,512]{2,1,0:T(8,128)(2,1)S(1)} %bitcast.18), channel_id=1, replica_groups=mesh['lg'=4,'lq'=2,'rx'=4,'rc'=2,'ch'=4,'cl'=2] {'lg','lq'}, dimensions={0} | all-to-all | bytes 2097152 | tf_op jit(solution)/shard_map/all_to_all | solution.py:260
  179.9 1.9 %finish.1 = bf16[128,1024]{1,0:T(8,128)(2,1)} custom-call(s32[64,64]{1,0:T(8,128)S(1)} %copy-done.2, bf16[8,128,512]{2,1,0:T(8,128)(2,1)S(1)} %all_to_all.21.terms), custom_call_target="tpu_custom_call" | custom-call | flops 1048576 | bytes 2097152 | tf_op jit(solution)/shard_map/finish/pallas_call | solution.py:245
  (16 shorter events, 0.3 us)
Async XLA Ops:
  4.3 11.5 %copy-start.3 = (bf16[1024,128]{1,0:T(8,128)(2,1)S(1)}, bf16[1024,128]{1,0:T(8,128)(2,1)}, u32[]{:S(2)}) copy-start(bf16[1024,128]{1,0:T(8,128)(2,1)} %get-tuple-element.9) | copy-start | bytes 786436
  4.3 60.7 %all-to-all-start = ((bf16[8,2064,128]{2,1,0:T(8,128)(2,1)}), bf16[8,2064,128]{2,1,0:T(8,128)(2,1)}, u32[]{:S(2)}, u32[]{:S(2)}) async-start(bf16[8,2064,128]{2,1,0:T(8,128)(2,1)} %get-tuple-element.10), calls=%async_computation | async-start | bytes 8454144 | tf_op jit(solution)/shard_map/all_to_all | solution.py:260
  15.8 14.8 %collective-permute-start.1 = (bf16[1024,128]{1,0:T(8,128)(2,1)S(1)}, bf16[1024,128]{1,0:T(8,128)(2,1)S(1)}, u32[]{:S(2)}, u32[]{:S(2)}) collective-permute-start(bf16[1024,128]{1,0:T(8,128)(2,1)S(1)} %copy-done.3), channel_id=1, source_target_pairs={{0,6},{1,7},{2,0},{3,1},{4,2},{5,3},{6,4},{7,5},{8,14},{9,15},{10,... | collective-permute-start | bytes 786440 | tf_op jit(solution)/shard_map/ppermute | solution.py:268
  21.1 18.3 %collective-permute-start.4 = (bf16[1024,128]{1,0:T(8,128)(2,1)S(1)}, bf16[1024,128]{1,0:T(8,128)(2,1)S(1)}, u32[]{:S(2)}, u32[]{:S(2)}) collective-permute-start(bf16[1024,128]{1,0:T(8,128)(2,1)S(1)} %copy-done.3), channel_id=1, source_target_pairs={{0,2},{1,3},{2,4},{3,5},{4,6},{5,7},{6,0},{7,1},{8,10},{9,11},{10,... | collective-permute-start | bytes 786440 | tf_op jit(solution)/shard_map/ppermute | solution.py:268
  23.0 19.5 %collective-permute-start = (bf16[1024,128]{1,0:T(8,128)(2,1)S(1)}, bf16[1024,128]{1,0:T(8,128)(2,1)S(1)}, u32[]{:S(2)}, u32[]{:S(2)}) collective-permute-start(bf16[1024,128]{1,0:T(8,128)(2,1)S(1)} %copy-done.3), channel_id=1, source_target_pairs={{0,7},{1,0},{2,1},{3,2},{4,3},{5,4},{6,5},{7,6},{8,15},{9,8},{10,9... | collective-permute-start | bytes 786440 | tf_op jit(solution)/shard_map/ppermute | solution.py:268
  28.5 27.4 %collective-permute-start.6 = (bf16[1024,128]{1,0:T(8,128)(2,1)S(1)}, bf16[1024,128]{1,0:T(8,128)(2,1)S(1)}, u32[]{:S(2)}, u32[]{:S(2)}) collective-permute-start(bf16[1024,128]{1,0:T(8,128)(2,1)S(1)} %copy-done.3), channel_id=1, source_target_pairs={{0,1},{1,2},{2,3},{3,4},{4,5},{5,6},{6,7},{7,0},{8,9},{9,10},{10,1... | collective-permute-start | bytes 786440 | tf_op jit(solution)/shard_map/ppermute | solution.py:268
  30.6 25.2 %collective-permute-start.3 = (bf16[1024,128]{1,0:T(8,128)(2,1)S(1)}, bf16[1024,128]{1,0:T(8,128)(2,1)S(1)}, u32[]{:S(2)}, u32[]{:S(2)}) collective-permute-start(bf16[1024,128]{1,0:T(8,128)(2,1)S(1)} %collective-permute-done.1), channel_id=1, source_target_pairs={{0,6},{1,7},{2,0},{3,1},{4,2},{5,3},{6,4},{7,5},{8,14},{9,15},{10,... | collective-permute-start | bytes 786440 | tf_op jit(solution)/shard_map/ppermute | solution.py:268
  35.5 20.2 %collective-permute-start.2 = (bf16[1024,128]{1,0:T(8,128)(2,1)S(1)}, bf16[1024,128]{1,0:T(8,128)(2,1)S(1)}, u32[]{:S(2)}, u32[]{:S(2)}) collective-permute-start(bf16[1024,128]{1,0:T(8,128)(2,1)S(1)} %collective-permute-done.1), channel_id=1, source_target_pairs={{0,7},{1,0},{2,1},{3,2},{4,3},{5,4},{6,5},{7,6},{8,15},{9,8},{10,9... | collective-permute-start | bytes 786440 | tf_op jit(solution)/shard_map/ppermute | solution.py:268
  39.4 16.4 %collective-permute-start.5 = (bf16[1024,128]{1,0:T(8,128)(2,1)S(1)}, bf16[1024,128]{1,0:T(8,128)(2,1)S(1)}, u32[]{:S(2)}, u32[]{:S(2)}) collective-permute-start(bf16[1024,128]{1,0:T(8,128)(2,1)S(1)} %collective-permute-done.4), channel_id=1, source_target_pairs={{0,1},{1,2},{2,3},{3,4},{4,5},{5,6},{6,7},{7,0},{8,9},{9,10},{10,1... | collective-permute-start | bytes 786440 | tf_op jit(solution)/shard_map/ppermute | solution.py:268
  56.0 9.1 %copy-start = (bf16[8,1024,128]{2,1,0:T(8,128)(2,1)}, bf16[8,1024,128]{2,1,0:T(8,128)(2,1)S(1)}, u32[]{:S(2)}) copy-start(bf16[8,1024,128]{2,1,0:T(8,128)(2,1)S(1)} %bitcast_dynamic-update-slice_fusion.near) | copy-start | bytes 6291460
  70.1 17.7 %collective-permute-start.8 = (bf16[4,2,128,512]{3,2,1,0:T(8,128)(2,1)}, bf16[4,2,128,512]{3,2,1,0:T(8,128)(2,1)S(1)}, u32[]{:S(2)}, u32[]{:S(2)}) collective-permute-start(bf16[4,2,128,512]{3,2,1,0:T(8,128)(2,1)} %get-tuple-element.12), channel_id=1, source_target_pairs={{0,1},{1,0},{2,3},{3,2},{4,5},{5,4},{6,7},{7,6},{8,15},{9,10},{10,... | collective-permute-start | bytes 3145736 | tf_op jit(solution)/shard_map/ppermute | solution.py:282
  75.4 47.3 %collective-permute-start.7 = (bf16[8,1024,128]{2,1,0:T(8,128)(2,1)}, bf16[8,1024,128]{2,1,0:T(8,128)(2,1)S(1)}, u32[]{:S(2)}, u32[]{:S(2)}) collective-permute-start(bf16[8,1024,128]{2,1,0:T(8,128)(2,1)} %copy-done), channel_id=1, source_target_pairs={{0,64},{64,0},{1,65},{65,1},{2,66},{66,2},{3,67},{67,3},{4,68},{68... | collective-permute-start | bytes 6291464 | tf_op jit(solution)/shard_map/ppermute | solution.py:276
  90.3 32.4 %all-to-all-start.1 = ((bf16[4,2,128,512]{3,2,1,0:T(8,128)(2,1)}), bf16[4,2,128,512]{3,2,1,0:T(8,128)(2,1)S(1)}, u32[]{:S(2)}, u32[]{:S(2)}) async-start(bf16[4,2,128,512]{3,2,1,0:T(8,128)(2,1)} %add_convert_fusion), calls=%async_computation.1 | async-start | bytes 2097152 | tf_op jit(solution)/shard_map/all_to_all | solution.py:260
  122.8 22.0 %copy-start.1 = (bf16[8,1024,128]{2,1,0:T(8,128)(2,1)S(1)}, bf16[8,1024,128]{2,1,0:T(8,128)(2,1)}, u32[]{:S(2)}) copy-start(bf16[8,1024,128]{2,1,0:T(8,128)(2,1)} %copy-done) | copy-start | bytes 6291460
  140.3 4.5 %collective-permute-start.9 = (bf16[8,128,512]{2,1,0:T(8,128)(2,1)S(1)}, bf16[8,128,512]{2,1,0:T(8,128)(2,1)S(1)}, u32[]{:S(2)}, u32[]{:S(2)}) collective-permute-start(bf16[8,128,512]{2,1,0:T(8,128)(2,1)S(1)} %all_to_all.20.own), channel_id=1, source_target_pairs={{0,8},{8,0},{1,9},{9,1},{2,10},{10,2},{3,11},{11,3},{4,12},{12,4},... | collective-permute-start | bytes 3145736 | tf_op jit(solution)/shard_map/ppermute | solution.py:288
  148.3 31.7 %copy-start.2 = (s32[64,64]{1,0:T(8,128)S(1)}, s32[64,64]{1,0:T(8,128)}, u32[]{:S(2)}) copy-start(s32[64,64]{1,0:T(8,128)} %pattern.3) | copy-start | bytes 49156

commit v4 on v3

--- a/solution.py
+++ b/solution.py
@@ -7,17 +7,19 @@
 
 TILE = 128
 SIDE = 8
-CAP = 16
+CAP = 12
+REST = 4
 BODY = CAP * TILE
 META = 16
 LAST = TILE - 1
+FLAG = TILE - 2
 MIB = 1 << 20
 VMEM_MIB = 60
 SMALL_MIB = 20
 
 
 def pack_kernel(
-    owners, slots, pattern, contributions, density, out, masked, data, meta, count, sems, sem, meta_sem
+    owners, slots, pattern, contributions, density, out, rest, masked, data, meta, count, sems, sem, meta_sem
 ):
     per = contributions.shape[0] // SIDE
     loads = [
@@ -48,13 +50,25 @@
             c = owner - r * SIDE
             pos = count[r]
             count[r] = pos + 1
-            pltpu.make_async_copy(
-                data.at[index], out.at[r, pl.ds(pl.multiple_of(pos * TILE, TILE), TILE)], sem
-            ).start()
+
+            @pl.when(pos < CAP)
+            def _():
+                at = pl.ds(pl.multiple_of(pos * TILE, TILE), TILE)
+                pltpu.make_async_copy(data.at[index], out.at[r, at], sem).start()
+
+            @pl.when(pos >= CAP)
+            def _():
+                at = pl.ds(pl.multiple_of((pos - CAP) * TILE, TILE), TILE)
+                pltpu.make_async_copy(data.at[index], rest.at[r, at], sem).start()
+
             here = (row == r) & (lane == pos)
             return jnp.where(here, c * SIDE + slots[index], places)
 
         places = lax.fori_loop(0, per, one, places, unroll=True)
+    most = count[0]
+    for r in range(1, SIDE):
+        most = jnp.maximum(most, count[r])
+    places = jnp.where(lane == FLAG, (most > CAP).astype(jnp.int32), places)
     for r in range(SIDE):
         places = jnp.where((row == r) & (lane == LAST), count[r], places)
     values = places.astype(jnp.float32)
@@ -71,6 +85,7 @@
         pack_kernel,
         out_shape=(
             jax.ShapeDtypeStruct((SIDE, BODY + META, TILE), jnp.bfloat16),
+            jax.ShapeDtypeStruct((SIDE, REST * TILE, TILE), jnp.bfloat16),
             jax.ShapeDtypeStruct(density.shape, jnp.bfloat16),
         ),
         in_specs=[
@@ -80,7 +95,11 @@
             pl.BlockSpec(memory_space=pl.ANY),
             pl.BlockSpec(memory_space=pltpu.VMEM),
         ],
-        out_specs=(pl.BlockSpec(memory_space=pl.ANY), pl.BlockSpec(memory_space=pltpu.VMEM)),
+        out_specs=(
+            pl.BlockSpec(memory_space=pl.ANY),
+            pl.BlockSpec(memory_space=pl.ANY),
+            pl.BlockSpec(memory_space=pltpu.VMEM),
+        ),
         scratch_shapes=[
             pltpu.VMEM(contributions.shape, jnp.bfloat16),
             pltpu.VMEM((SIDE, META, TILE), jnp.bfloat16),
@@ -95,7 +114,9 @@
     )(owners, slots, pattern, contributions, density)
 
 
-def combine_kernel(got, near, keep, send, data, meta, places, table, total, sems, meta_sem, table_sem):
+def combine_kernel(
+    got, more, near, keep, send, data, extra, meta, places, table, total, sems, meta_sem, table_sem, extra_sem
+):
     head = pltpu.make_async_copy(got.at[:, pl.ds(BODY, META)], meta, meta_sem)
     head.start()
     loads = [
@@ -120,7 +141,23 @@
             total[place] += data[r, rows].astype(jnp.float32)
             return carry
 
-        lax.fori_loop(0, table[r, LAST], one, 0)
+        held = table[r, LAST]
+        lax.fori_loop(0, jnp.minimum(held, CAP), one, 0)
+
+        @pl.when(held > CAP)
+        def _(r=r, held=held):
+            load = pltpu.make_async_copy(more.at[r], extra, extra_sem)
+            load.start()
+            load.wait()
+
+            def late(pos, carry):
+                place = table[r, CAP + pos]
+                rows = pl.ds(pl.multiple_of(pos * TILE, TILE), TILE)
+                total[place] += extra[rows].astype(jnp.float32)
+                return carry
+
+            lax.fori_loop(0, held - CAP, late, 0)
+
 
     parity = lax.axis_index("cl")
 
@@ -136,15 +173,16 @@
     lax.fori_loop(0, SIDE // 2, write, 0)
 
 
-def combine(got, near):
+def combine(got, more, near):
     half = jax.ShapeDtypeStruct((SIDE // 2, 2, TILE, SIDE * TILE // 2), jnp.bfloat16)
     return pl.pallas_call(
         combine_kernel,
         out_shape=(half, half),
-        in_specs=[pl.BlockSpec(memory_space=pl.ANY), pl.BlockSpec(memory_space=pl.ANY)],
+        in_specs=[pl.BlockSpec(memory_space=pl.ANY)] * 3,
         out_specs=(pl.BlockSpec(memory_space=pltpu.VMEM), pl.BlockSpec(memory_space=pltpu.VMEM)),
         scratch_shapes=[
             pltpu.VMEM((SIDE, BODY, TILE), jnp.bfloat16),
+            pltpu.VMEM((REST * TILE, TILE), jnp.bfloat16),
             pltpu.VMEM((SIDE, META, TILE), jnp.bfloat16),
             pltpu.VMEM((SIDE, TILE), jnp.int32),
             pltpu.SMEM((SIDE, TILE), jnp.int32),
@@ -152,13 +190,14 @@
             pltpu.SemaphoreType.DMA((SIDE,)),
             pltpu.SemaphoreType.DMA,
             pltpu.SemaphoreType.DMA,
+            pltpu.SemaphoreType.DMA,
         ],
         compiler_params=pltpu.CompilerParams(vmem_limit_bytes=VMEM_MIB * MIB),
         cost_estimate=pl.CostEstimate(
             flops=4 * MIB, bytes_accessed=6 * MIB, transcendentals=0
         ),
         name="combine",
-    )(got, near)
+    )(got, more, near)
 
 
 def spread_kernel(parts, far, out):
@@ -261,7 +300,7 @@
 
 
 def body(density, contributions, owners, slots, pattern):
-    packed, sparse = pack(owners.reshape(-1), slots, pattern, contributions, density)
+    packed, rest, sparse = pack(owners.reshape(-1), slots, pattern, contributions, density)
     got = exchange(packed, ("rx", "rc"))
 
     def ahead(block, distance):
@@ -275,7 +314,9 @@
     swap = [(0, 1), (1, 0)]
     far = lax.ppermute(near, "lq", swap)
 
-    keep, send = combine(got, near)
+    anyone = jnp.max(got[:, BODY, FLAG].astype(jnp.float32)) > 0
+    more = lax.cond(anyone, lambda v: exchange(v, ("rx", "rc")), lambda v: v, rest)
+    keep, send = combine(got, more, near)
     count = SIDE
     even = [(c, c ^ 1) for c in range(count)]
     odd = [(count + c, count + (c + (1 if c % 2 else -1)) % count) for c in range(count)]

time: 185 us -> 182 us (0.984); the launches traced: 182 us -> 181 us
  waiting for transfers between devices: 62.7 us -> 55.6 us
  blocking collectives: 49.1 us -> 52.7 us
    all_to_all x2, waiting for transfers between devices: 9.08 us -> 2.53 us  [exchange(): return lax.all_to_all(values, axes, split_axis=0, concat_axis=0, tiled=True)]
    all_to_all x2, blocking collectives: 49.1 us -> 52.7 us  [exchange(): return lax.all_to_all(values, axes, split_axis=0, concat_axis=0, tiled=True)]
    ppermute x7, waiting for transfers between devices: 13.3 us -> 10.9 us  [ahead(): lax.ppermute(block, ('ch', 'cl'), [(c, (c - distance) % SIDE) for c in ra...]
    ppermute x7, starting transfers between devices: 26.5 us -> 24.2 us  [ahead(): lax.ppermute(block, ('ch', 'cl'), [(c, (c - distance) % SIDE) for c in ra...]
    ppermute x1, starting transfers between devices: 1.91 us -> 4.09 us  [body(): other = lax.ppermute(own, 'rc', swap)]
  transfers between devices with their start and end apart: 12 -> 12, of which waited for: 6 -> 8; matrix products, arithmetic and copies ran while one was open for 2% -> 2% of each run, Pallas kernels for 0% -> 0%
where the time goes in v4:
time: 182 us; the launch traced here: 181 us
  waiting for transfers between devices  55.6 us (31%)
  blocking collectives  52.7 us (29%)
  starting transfers between devices  51.6 us (28%)
  Pallas kernels  16.3 us (9%)
  other arithmetic  3.91 us (2%)
    all_to_all x2, blocking collectives, exchange(): return lax.all_to_all(values, axes, split_axis=0, concat_axis=0, tiled=True)  52.7 us
    ppermute x1, waiting for transfers between devices, body(): far = lax.ppermute(near, 'lq', swap)  29.5 us
    ppermute x7, starting transfers between devices, ahead(): lax.ppermute(block, ('ch', 'cl'), [(c, (c - distance) % SIDE) for c in ra...  24.2 us
    all_to_all x2, starting transfers between devices, exchange(): return lax.all_to_all(values, axes, split_axis=0, concat_axis=0, tiled=True)  14.9 us
    ppermute x7, waiting for transfers between devices, ahead(): lax.ppermute(block, ('ch', 'cl'), [(c, (c - distance) % SIDE) for c in ra...  10.9 us
    ppermute x1, waiting for transfers between devices, body(): taken = lax.ppermute(send, ('rc', 'ch', 'cl'), even + odd)  10.3 us
    ppermute x1, starting transfers between devices, body(): taken = lax.ppermute(send, ('rc', 'ch', 'cl'), even + odd)  6.4 us
    pallas_call x1, Pallas kernels, combine(): pl.pallas_call(combine_kernel, out_shape=(half, half), in_specs=[pl.Block...  4.86 us
  transfers between devices with their start and end apart: 12, of which 8 were waited for; matrix products, arithmetic and copies ran while one was open for 2% of the time, Pallas kernels for 0%

profile of v4, /device:TPU:1, one launch (start us, length us, event | category | flops | bytes accessed | tf_op | source)
XLA Modules:
  0.0 181.3 jit_solution(12710961051751032350)
XLA Ops:
  0.0 4.7 %pack.1 = (bf16[8,1552,128]{2,1,0:T(8,128)(2,1)}, bf16[8,512,128]{2,1,0:T(8,128)(2,1)S(1)}, bf16[1024,128]{1,0:T(8,128)(2,1)}) custom-call(s32[64]{0:T(128)} %bitcast.19, s32[64]{0:T(128)} %slots.1, s32[64,64]{1,0:T(8,128)} %pattern.3, bf16[64,128,128]{2,1,0:T(8,128)(2,1)} %contributions.1, bf16[1024,128]{1,0:T(8,128)(2,1)} %density.1), custom_call_target="tpu_custom_call" | custom-call | bytes 7340032 | tf_op jit(solution)/shard_map/pack/pallas_call | solution.py:84
  4.7 0.0 copy-start.3
  4.7 11.4 %all-to-all-start.1 = ((bf16[8,1552,128]{2,1,0:T(8,128)(2,1)}), bf16[8,1552,128]{2,1,0:T(8,128)(2,1)}, u32[]{:S(2)}, u32[]{:S(2)}) async-start(bf16[8,1552,128]{2,1,0:T(8,128)(2,1)} %get-tuple-element.16), calls=%async_computation.1 | async-start | bytes 6356992 | tf_op jit(solution)/shard_map/all_to_all | solution.py:299
  16.1 5.3 %collective-permute-start.1 = (bf16[1024,128]{1,0:T(8,128)(2,1)S(1)}, bf16[1024,128]{1,0:T(8,128)(2,1)S(1)}, u32[]{:S(2)}, u32[]{:S(2)}) collective-permute-start(bf16[1024,128]{1,0:T(8,128)(2,1)S(1)} %copy-done.3), channel_id=1, source_target_pairs={{0,6},{1,7},{2,0},{3,1},{4,2},{5,3},{6,4},{7,5},{8,14},{9,15},{10,... | collective-permute-start | bytes 786440 | tf_op jit(solution)/shard_map/ppermute | solution.py:307
  21.4 2.2 %collective-permute-start = (bf16[1024,128]{1,0:T(8,128)(2,1)S(1)}, bf16[1024,128]{1,0:T(8,128)(2,1)S(1)}, u32[]{:S(2)}, u32[]{:S(2)}) collective-permute-start(bf16[1024,128]{1,0:T(8,128)(2,1)S(1)} %copy-done.3), channel_id=1, source_target_pairs={{0,7},{1,0},{2,1},{3,2},{4,3},{5,4},{6,5},{7,6},{8,15},{9,8},{10,9... | collective-permute-start | bytes 786440 | tf_op jit(solution)/shard_map/ppermute | solution.py:307
  23.6 4.0 %collective-permute-start.4 = (bf16[1024,128]{1,0:T(8,128)(2,1)S(1)}, bf16[1024,128]{1,0:T(8,128)(2,1)S(1)}, u32[]{:S(2)}, u32[]{:S(2)}) collective-permute-start(bf16[1024,128]{1,0:T(8,128)(2,1)S(1)} %copy-done.3), channel_id=1, source_target_pairs={{0,2},{1,3},{2,4},{3,5},{4,6},{5,7},{6,0},{7,1},{8,10},{9,11},{10,... | collective-permute-start | bytes 786440 | tf_op jit(solution)/shard_map/ppermute | solution.py:307
  27.6 1.9 %collective-permute-start.6 = (bf16[1024,128]{1,0:T(8,128)(2,1)S(1)}, bf16[1024,128]{1,0:T(8,128)(2,1)S(1)}, u32[]{:S(2)}, u32[]{:S(2)}) collective-permute-start(bf16[1024,128]{1,0:T(8,128)(2,1)S(1)} %copy-done.3), channel_id=1, source_target_pairs={{0,1},{1,2},{2,3},{3,4},{4,5},{5,6},{6,7},{7,0},{8,9},{9,10},{10,1... | collective-permute-start | bytes 786440 | tf_op jit(solution)/shard_map/ppermute | solution.py:307
  29.6 1.2 collective-permute-done.1
  30.8 7.0 %collective-permute-start.2 = (bf16[1024,128]{1,0:T(8,128)(2,1)S(1)}, bf16[1024,128]{1,0:T(8,128)(2,1)S(1)}, u32[]{:S(2)}, u32[]{:S(2)}) collective-permute-start(bf16[1024,128]{1,0:T(8,128)(2,1)S(1)} %collective-permute-done.1), channel_id=1, source_target_pairs={{0,7},{1,0},{2,1},{3,2},{4,3},{5,4},{6,5},{7,6},{8,15},{9,8},{10,9... | collective-permute-start | bytes 786440 | tf_op jit(solution)/shard_map/ppermute | solution.py:307
  37.8 1.9 %collective-permute-start.3 = (bf16[1024,128]{1,0:T(8,128)(2,1)S(1)}, bf16[1024,128]{1,0:T(8,128)(2,1)S(1)}, u32[]{:S(2)}, u32[]{:S(2)}) collective-permute-start(bf16[1024,128]{1,0:T(8,128)(2,1)S(1)} %collective-permute-done.1), channel_id=1, source_target_pairs={{0,6},{1,7},{2,0},{3,1},{4,2},{5,3},{6,4},{7,5},{8,14},{9,15},{10,... | collective-permute-start | bytes 786440 | tf_op jit(solution)/shard_map/ppermute | solution.py:307
  39.7 0.0 collective-permute-done
  39.8 1.5 collective-permute-done.4
  41.3 1.9 %collective-permute-start.5 = (bf16[1024,128]{1,0:T(8,128)(2,1)S(1)}, bf16[1024,128]{1,0:T(8,128)(2,1)S(1)}, u32[]{:S(2)}, u32[]{:S(2)}) collective-permute-start(bf16[1024,128]{1,0:T(8,128)(2,1)S(1)} %collective-permute-done.4), channel_id=1, source_target_pairs={{0,1},{1,2},{2,3},{3,4},{4,5},{5,6},{6,7},{7,0},{8,9},{9,10},{10,1... | collective-permute-start | bytes 786440 | tf_op jit(solution)/shard_map/ppermute | solution.py:307
  43.2 4.4 %collective-permute-done.2 = bf16[1024,128]{1,0:T(8,128)(2,1)S(1)} collective-permute-done((bf16[1024,128]{1,0:T(8,128)(2,1)S(1)}, bf16[1024,128]{1,0:T(8,128)(2,1)S(1)}, u32[]{:S(2)}, u32[]{:S(2)}) %collective-permute-start.2) | collective-permute-done | bytes 262176 | tf_op jit(solution)/shard_map/ppermute | solution.py:307
  47.6 3.8 %collective-permute-done.3 = bf16[1024,128]{1,0:T(8,128)(2,1)S(1)} collective-permute-done((bf16[1024,128]{1,0:T(8,128)(2,1)S(1)}, bf16[1024,128]{1,0:T(8,128)(2,1)S(1)}, u32[]{:S(2)}, u32[]{:S(2)}) %collective-permute-start.3) | collective-permute-done | bytes 262176 | tf_op jit(solution)/shard_map/ppermute | solution.py:307
  51.6 2.5 %all-to-all-done.1.got = bf16[8,1552,128]{2,1,0:T(8,128)(2,1)} async-done(((bf16[8,1552,128]{2,1,0:T(8,128)(2,1)}), bf16[8,1552,128]{2,1,0:T(8,128)(2,1)}, u32[]{:S(2)}, u32[]{:S(2)}) %all-to-all-start.1) | async-done | bytes 3178528 | tf_op jit(solution)/shard_map/all_to_all | solution.py:299
  54.1 1.4 slice_reduce_fusion
  56.2 4.9 %combine.1 = (bf16[4,2,128,512]{3,2,1,0:T(8,128)(2,1)}, bf16[4,2,128,512]{3,2,1,0:T(8,128)(2,1)}) custom-call(bf16[8,1552,128]{2,1,0:T(8,128)(2,1)} %all-to-all-done.1.got, bf16[8,512,128]{2,1,0:T(8,128)(2,1)S(1)} %get-tuple-element.20.more, bf16[8,1024,128]{2,1,0:T(8,128)(2,1)} %copy-done), custom_call_target="tpu_custom_call" | custom-call | flops 4194304 | bytes 6291456 | tf_op jit(solution)/shard_map/combine/pallas_call | solution.py:178
  61.1 6.4 %collective-permute-start.8 = (bf16[4,2,128,512]{3,2,1,0:T(8,128)(2,1)}, bf16[4,2,128,512]{3,2,1,0:T(8,128)(2,1)S(1)}, u32[]{:S(2)}, u32[]{:S(2)}) collective-permute-start(bf16[4,2,128,512]{3,2,1,0:T(8,128)(2,1)} %get-tuple-element.19), channel_id=1, source_target_pairs={{0,1},{1,0},{2,3},{3,2},{4,5},{5,4},{6,7},{7,6},{8,15},{9,10},{10,... | collective-permute-start | bytes 3145736 | tf_op jit(solution)/shard_map/ppermute | solution.py:323
  67.5 2.0 %collective-permute-start.7 = (bf16[8,1024,128]{2,1,0:T(8,128)(2,1)S(1)}, bf16[8,1024,128]{2,1,0:T(8,128)(2,1)}, u32[]{:S(2)}, u32[]{:S(2)}) collective-permute-start(bf16[8,1024,128]{2,1,0:T(8,128)(2,1)S(1)} %copy-done.1), channel_id=1, source_target_pairs={{0,64},{64,0},{1,65},{65,1},{2,66},{66,2},{3,67},{67,3},{4,68},{68... | collective-permute-start | bytes 6291464 | tf_op jit(solution)/shard_map/ppermute | solution.py:315
  69.6 10.3 %collective-permute-done.8 = bf16[4,2,128,512]{3,2,1,0:T(8,128)(2,1)S(1)} collective-permute-done((bf16[4,2,128,512]{3,2,1,0:T(8,128)(2,1)}, bf16[4,2,128,512]{3,2,1,0:T(8,128)(2,1)S(1)}, u32[]{:S(2)}, u32[]{:S(2)}) %collective-permute-start.8) | collective-permute-done | bytes 1048608 | tf_op jit(solution)/shard_map/ppermute | solution.py:323
  79.9 2.5 %add_convert_fusion = bf16[4,2,128,512]{3,2,1,0:T(8,128)(2,1)} fusion(bf16[4,2,128,512]{3,2,1,0:T(8,128)(2,1)S(1)} %collective-permute-done.8, bf16[4,2,128,512]{3,2,1,0:T(8,128)(2,1)} %get-tuple-element.18), kind=kLoop, calls=%fused_computation | loop fusion | flops 2097152 | bytes 3145728 | tf_op jit(solution)/shard_map/convert_element_type | solution.py:325
  82.4 3.5 %all-to-all-start.2 = ((bf16[4,2,128,512]{3,2,1,0:T(8,128)(2,1)}), bf16[4,2,128,512]{3,2,1,0:T(8,128)(2,1)S(1)}, u32[]{:S(2)}, u32[]{:S(2)}) async-start(bf16[4,2,128,512]{3,2,1,0:T(8,128)(2,1)} %add_convert_fusion), calls=%async_computation.2 | async-start | bytes 2097152 | tf_op jit(solution)/shard_map/all_to_all | solution.py:299
  85.9 29.5 %collective-permute-done.7.far = bf16[8,1024,128]{2,1,0:T(8,128)(2,1)} collective-permute-done((bf16[8,1024,128]{2,1,0:T(8,128)(2,1)S(1)}, bf16[8,1024,128]{2,1,0:T(8,128)(2,1)}, u32[]{:S(2)}, u32[]{:S(2)}) %collective-permute-start.7) | collective-permute-done | bytes 2097184 | tf_op jit(solution)/shard_map/ppermute | solution.py:315
  115.5 0.1 spread.1
  115.6 18.9 %all_to_all.25.own = bf16[8,128,512]{2,1,0:T(8,128)(2,1)S(1)} all-to-all(bf16[8,128,512]{2,1,0:T(8,128)(2,1)S(1)} %spread.1), channel_id=1, replica_groups=mesh['lg'=4,'lq'=2,'rx'=4,'rc'=2,'ch'=4,'cl'=2] {'lq','rx'}, dimensions={0} | all-to-all | bytes 2097152 | tf_op jit(solution)/shard_map/all_to_all | solution.py:299
  134.6 4.1 %collective-permute-start.9 = (bf16[8,128,512]{2,1,0:T(8,128)(2,1)S(1)}, bf16[8,128,512]{2,1,0:T(8,128)(2,1)S(1)}, u32[]{:S(2)}, u32[]{:S(2)}) collective-permute-start(bf16[8,128,512]{2,1,0:T(8,128)(2,1)S(1)} %all_to_all.25.own), channel_id=1, source_target_pairs={{0,8},{8,0},{1,9},{9,1},{2,10},{10,2},{3,11},{11,3},{4,12},{12,4},... | collective-permute-start | bytes 3145736 | tf_op jit(solution)/shard_map/ppermute | solution.py:329
  138.7 2.3 %collective-permute-done.9.other = bf16[8,128,512]{2,1,0:T(8,128)(2,1)S(1)} collective-permute-done((bf16[8,128,512]{2,1,0:T(8,128)(2,1)S(1)}, bf16[8,128,512]{2,1,0:T(8,128)(2,1)S(1)}, u32[]{:S(2)}, u32[]{:S(2)}) %collective-permute-start.9) | collective-permute-done | bytes 1048608 | tf_op jit(solution)/shard_map/ppermute | solution.py:329
  140.9 4.6 %product.1 = bf16[1024,512]{1,0:T(8,128)(2,1)S(1)} custom-call(bf16[8,1024,128]{2,1,0:T(8,128)(2,1)S(1)} %copy-done.1, bf16[8,1024,128]{2,1,0:T(8,128)(2,1)} %collective-permute-done.7.far, bf16[8,128,512]{2,1,0:T(8,128)(2,1)S(1)} %all_to_all.25.own, bf16[8,128,512]{2,1,0:T(8,128)(2,1)S(1)} %collective-permute-done.9.other), custom_call_target="tpu_custom_call" | custom-call | flops 2147483648 | bytes 7340032 | tf_op jit(solution)/shard_map/product/pallas_call | solution.py:251
  145.5 0.0 copy-start.2
  145.6 33.8 %all_to_all.26.terms = bf16[8,128,512]{2,1,0:T(8,128)(2,1)S(1)} all-to-all(bf16[8,128,512]{2,1,0:T(8,128)(2,1)S(1)} %bitcast.18), channel_id=1, replica_groups=mesh['lg'=4,'lq'=2,'rx'=4,'rc'=2,'ch'=4,'cl'=2] {'lg','lq'}, dimensions={0} | all-to-all | bytes 2097152 | tf_op jit(solution)/shard_map/all_to_all | solution.py:299
  179.4 1.9 %finish.1 = bf16[128,1024]{1,0:T(8,128)(2,1)} custom-call(s32[64,64]{1,0:T(8,128)S(1)} %copy-done.2, bf16[8,128,512]{2,1,0:T(8,128)(2,1)S(1)} %all_to_all.26.terms), custom_call_target="tpu_custom_call" | custom-call | flops 1048576 | bytes 2097152 | tf_op jit(solution)/shard_map/finish/pallas_call | solution.py:284
  (18 shorter events, 0.3 us)
Async XLA Ops:
  4.7 11.4 %copy-start.3 = (bf16[1024,128]{1,0:T(8,128)(2,1)S(1)}, bf16[1024,128]{1,0:T(8,128)(2,1)}, u32[]{:S(2)}) copy-start(bf16[1024,128]{1,0:T(8,128)(2,1)} %get-tuple-element.15) | copy-start | bytes 786436
  4.7 49.4 %all-to-all-start.1 = ((bf16[8,1552,128]{2,1,0:T(8,128)(2,1)}), bf16[8,1552,128]{2,1,0:T(8,128)(2,1)}, u32[]{:S(2)}, u32[]{:S(2)}) async-start(bf16[8,1552,128]{2,1,0:T(8,128)(2,1)} %get-tuple-element.16), calls=%async_computation.1 | async-start | bytes 6356992 | tf_op jit(solution)/shard_map/all_to_all | solution.py:299
  16.1 14.7 %collective-permute-start.1 = (bf16[1024,128]{1,0:T(8,128)(2,1)S(1)}, bf16[1024,128]{1,0:T(8,128)(2,1)S(1)}, u32[]{:S(2)}, u32[]{:S(2)}) collective-permute-start(bf16[1024,128]{1,0:T(8,128)(2,1)S(1)} %copy-done.3), channel_id=1, source_target_pairs={{0,6},{1,7},{2,0},{3,1},{4,2},{5,3},{6,4},{7,5},{8,14},{9,15},{10,... | collective-permute-start | bytes 786440 | tf_op jit(solution)/shard_map/ppermute | solution.py:307
  21.4 18.3 %collective-permute-start = (bf16[1024,128]{1,0:T(8,128)(2,1)S(1)}, bf16[1024,128]{1,0:T(8,128)(2,1)S(1)}, u32[]{:S(2)}, u32[]{:S(2)}) collective-permute-start(bf16[1024,128]{1,0:T(8,128)(2,1)S(1)} %copy-done.3), channel_id=1, source_target_pairs={{0,7},{1,0},{2,1},{3,2},{4,3},{5,4},{6,5},{7,6},{8,15},{9,8},{10,9... | collective-permute-start | bytes 786440 | tf_op jit(solution)/shard_map/ppermute | solution.py:307
  23.6 17.7 %collective-permute-start.4 = (bf16[1024,128]{1,0:T(8,128)(2,1)S(1)}, bf16[1024,128]{1,0:T(8,128)(2,1)S(1)}, u32[]{:S(2)}, u32[]{:S(2)}) collective-permute-start(bf16[1024,128]{1,0:T(8,128)(2,1)S(1)} %copy-done.3), channel_id=1, source_target_pairs={{0,2},{1,3},{2,4},{3,5},{4,6},{5,7},{6,0},{7,1},{8,10},{9,11},{10,... | collective-permute-start | bytes 786440 | tf_op jit(solution)/shard_map/ppermute | solution.py:307
  27.6 24.0 %collective-permute-start.6 = (bf16[1024,128]{1,0:T(8,128)(2,1)S(1)}, bf16[1024,128]{1,0:T(8,128)(2,1)S(1)}, u32[]{:S(2)}, u32[]{:S(2)}) collective-permute-start(bf16[1024,128]{1,0:T(8,128)(2,1)S(1)} %copy-done.3), channel_id=1, source_target_pairs={{0,1},{1,2},{2,3},{3,4},{4,5},{5,6},{6,7},{7,0},{8,9},{9,10},{10,1... | collective-permute-start | bytes 786440 | tf_op jit(solution)/shard_map/ppermute | solution.py:307
  30.8 16.8 %collective-permute-start.2 = (bf16[1024,128]{1,0:T(8,128)(2,1)S(1)}, bf16[1024,128]{1,0:T(8,128)(2,1)S(1)}, u32[]{:S(2)}, u32[]{:S(2)}) collective-permute-start(bf16[1024,128]{1,0:T(8,128)(2,1)S(1)} %collective-permute-done.1), channel_id=1, source_target_pairs={{0,7},{1,0},{2,1},{3,2},{4,3},{5,4},{6,5},{7,6},{8,15},{9,8},{10,9... | collective-permute-start | bytes 786440 | tf_op jit(solution)/shard_map/ppermute | solution.py:307
  37.8 13.6 %collective-permute-start.3 = (bf16[1024,128]{1,0:T(8,128)(2,1)S(1)}, bf16[1024,128]{1,0:T(8,128)(2,1)S(1)}, u32[]{:S(2)}, u32[]{:S(2)}) collective-permute-start(bf16[1024,128]{1,0:T(8,128)(2,1)S(1)} %collective-permute-done.1), channel_id=1, source_target_pairs={{0,6},{1,7},{2,0},{3,1},{4,2},{5,3},{6,4},{7,5},{8,14},{9,15},{10,... | collective-permute-start | bytes 786440 | tf_op jit(solution)/shard_map/ppermute | solution.py:307
  41.3 10.2 %collective-permute-start.5 = (bf16[1024,128]{1,0:T(8,128)(2,1)S(1)}, bf16[1024,128]{1,0:T(8,128)(2,1)S(1)}, u32[]{:S(2)}, u32[]{:S(2)}) collective-permute-start(bf16[1024,128]{1,0:T(8,128)(2,1)S(1)} %collective-permute-done.4), channel_id=1, source_target_pairs={{0,1},{1,2},{2,3},{3,4},{4,5},{5,6},{6,7},{7,0},{8,9},{9,10},{10,1... | collective-permute-start | bytes 786440 | tf_op jit(solution)/shard_map/ppermute | solution.py:307
  51.6 4.6 %copy-start = (bf16[8,1024,128]{2,1,0:T(8,128)(2,1)}, bf16[8,1024,128]{2,1,0:T(8,128)(2,1)S(1)}, u32[]{:S(2)}) copy-start(bf16[8,1024,128]{2,1,0:T(8,128)(2,1)S(1)} %bitcast_dynamic-update-slice_fusion.near) | copy-start | bytes 6291460
  56.2 11.3 %copy-start.1 = (bf16[8,1024,128]{2,1,0:T(8,128)(2,1)S(1)}, bf16[8,1024,128]{2,1,0:T(8,128)(2,1)}, u32[]{:S(2)}) copy-start(bf16[8,1024,128]{2,1,0:T(8,128)(2,1)} %copy-done) | copy-start | bytes 6291460
  61.1 18.8 %collective-permute-start.8 = (bf16[4,2,128,512]{3,2,1,0:T(8,128)(2,1)}, bf16[4,2,128,512]{3,2,1,0:T(8,128)(2,1)S(1)}, u32[]{:S(2)}, u32[]{:S(2)}) collective-permute-start(bf16[4,2,128,512]{3,2,1,0:T(8,128)(2,1)} %get-tuple-element.19), channel_id=1, source_target_pairs={{0,1},{1,0},{2,3},{3,2},{4,5},{5,4},{6,7},{7,6},{8,15},{9,10},{10,... | collective-permute-start | bytes 3145736 | tf_op jit(solution)/shard_map/ppermute | solution.py:323
  67.5 48.0 %collective-permute-start.7 = (bf16[8,1024,128]{2,1,0:T(8,128)(2,1)S(1)}, bf16[8,1024,128]{2,1,0:T(8,128)(2,1)}, u32[]{:S(2)}, u32[]{:S(2)}) collective-permute-start(bf16[8,1024,128]{2,1,0:T(8,128)(2,1)S(1)} %copy-done.1), channel_id=1, source_target_pairs={{0,64},{64,0},{1,65},{65,1},{2,66},{66,2},{3,67},{67,3},{4,68},{68... | collective-permute-start | bytes 6291464 | tf_op jit(solution)/shard_map/ppermute | solution.py:315
  82.4 33.1 %all-to-all-start.2 = ((bf16[4,2,128,512]{3,2,1,0:T(8,128)(2,1)}), bf16[4,2,128,512]{3,2,1,0:T(8,128)(2,1)S(1)}, u32[]{:S(2)}, u32[]{:S(2)}) async-start(bf16[4,2,128,512]{3,2,1,0:T(8,128)(2,1)} %add_convert_fusion), calls=%async_computation.2 | async-start | bytes 2097152 | tf_op jit(solution)/shard_map/all_to_all | solution.py:299
  134.6 6.4 %collective-permute-start.9 = (bf16[8,128,512]{2,1,0:T(8,128)(2,1)S(1)}, bf16[8,128,512]{2,1,0:T(8,128)(2,1)S(1)}, u32[]{:S(2)}, u32[]{:S(2)}) collective-permute-start(bf16[8,128,512]{2,1,0:T(8,128)(2,1)S(1)} %all_to_all.25.own), channel_id=1, source_target_pairs={{0,8},{8,0},{1,9},{9,1},{2,10},{10,2},{3,11},{11,3},{4,12},{12,4},... | collective-permute-start | bytes 3145736 | tf_op jit(solution)/shard_map/ppermute | solution.py:329
  145.5 33.8 %copy-start.2 = (s32[64,64]{1,0:T(8,128)S(1)}, s32[64,64]{1,0:T(8,128)}, u32[]{:S(2)}) copy-start(s32[64,64]{1,0:T(8,128)} %pattern.3) | copy-start | bytes 49156

commit v5 on v4

--- a/solution.py
+++ b/solution.py
@@ -1,3 +1,5 @@
+import functools
+
 import jax
 import jax.numpy as jnp
 from jax import lax
@@ -115,7 +117,7 @@
 
 
 def combine_kernel(
-    got, more, near, keep, send, data, extra, meta, places, table, total, sems, meta_sem, table_sem, extra_sem
+    keeps, got, more, first, out, data, extra, meta, places, table, total, sems, meta_sem, table_sem, extra_sem
 ):
     head = pltpu.make_async_copy(got.at[:, pl.ds(BODY, META)], meta, meta_sem)
     head.start()
@@ -126,22 +128,33 @@
     for load in loads:
         load.start()
     total[...] = jnp.zeros_like(total)
+    parity = lax.axis_index("cl")
+    if not keeps:
+        parity = 1 - parity
     head.wait()
     for r in range(SIDE):
         places[r : r + 1] = meta[r].astype(jnp.float32)[:1].astype(jnp.int32)
     listing = pltpu.make_async_copy(places, table, table_sem)
     listing.start()
     listing.wait()
+
+    def put(place, values):
+        column = place // SIDE
+
+        @pl.when(column % 2 == parity)
+        def _():
+            at = column // 2 * SIDE + place % SIDE
+            total[at] += values().astype(jnp.float32)
+
     for r in range(SIDE):
         loads[r].wait()
+        held = table[r, LAST]
 
         def one(pos, carry, r=r):
-            place = table[r, pos]
             rows = pl.ds(pl.multiple_of(pos * TILE, TILE), TILE)
-            total[place] += data[r, rows].astype(jnp.float32)
+            put(table[r, pos], lambda: data[r, rows])
             return carry
 
-        held = table[r, LAST]
         lax.fori_loop(0, jnp.minimum(held, CAP), one, 0)
 
         @pl.when(held > CAP)
@@ -151,53 +164,45 @@
             load.wait()
 
             def late(pos, carry):
-                place = table[r, CAP + pos]
                 rows = pl.ds(pl.multiple_of(pos * TILE, TILE), TILE)
-                total[place] += extra[rows].astype(jnp.float32)
+                put(table[r, CAP + pos], lambda: extra[rows])
                 return carry
 
             lax.fori_loop(0, held - CAP, late, 0)
-
-
-    parity = lax.axis_index("cl")
 
     def write(j, carry):
         for s in range(SIDE):
             columns = slice(s % 4 * TILE, (s % 4 + 1) * TILE)
-            mine = total[(2 * j + parity) * SIDE + s]
-            keep[j, s // 4, :, columns] = mine.astype(jnp.bfloat16)
-            theirs = total[(2 * j + 1 - parity) * SIDE + s]
-            send[j, s // 4, :, columns] = theirs.astype(jnp.bfloat16)
+            out[j, s // 4, :, columns] = total[j * SIDE + s].astype(jnp.bfloat16)
         return carry
 
     lax.fori_loop(0, SIDE // 2, write, 0)
 
 
-def combine(got, more, near):
-    half = jax.ShapeDtypeStruct((SIDE // 2, 2, TILE, SIDE * TILE // 2), jnp.bfloat16)
-    return pl.pallas_call(
-        combine_kernel,
-        out_shape=(half, half),
+def combine(keeps, got, more, first):
+    return pl.pallas_call(
+        functools.partial(combine_kernel, keeps),
+        out_shape=jax.ShapeDtypeStruct((SIDE // 2, 2, TILE, SIDE * TILE // 2), jnp.bfloat16),
         in_specs=[pl.BlockSpec(memory_space=pl.ANY)] * 3,
-        out_specs=(pl.BlockSpec(memory_space=pltpu.VMEM), pl.BlockSpec(memory_space=pltpu.VMEM)),
+        out_specs=pl.BlockSpec(memory_space=pltpu.VMEM),
         scratch_shapes=[
             pltpu.VMEM((SIDE, BODY, TILE), jnp.bfloat16),
             pltpu.VMEM((REST * TILE, TILE), jnp.bfloat16),
             pltpu.VMEM((SIDE, META, TILE), jnp.bfloat16),
             pltpu.VMEM((SIDE, TILE), jnp.int32),
             pltpu.SMEM((SIDE, TILE), jnp.int32),
-            pltpu.VMEM((SIDE * SIDE, TILE, TILE), jnp.float32),
+            pltpu.VMEM((SIDE * SIDE // 2, TILE, TILE), jnp.float32),
             pltpu.SemaphoreType.DMA((SIDE,)),
             pltpu.SemaphoreType.DMA,
             pltpu.SemaphoreType.DMA,
             pltpu.SemaphoreType.DMA,
         ],
-        compiler_params=pltpu.CompilerParams(vmem_limit_bytes=VMEM_MIB * MIB),
+        compiler_params=pltpu.CompilerParams(vmem_limit_bytes=SMALL_MIB * MIB),
         cost_estimate=pl.CostEstimate(
-            flops=4 * MIB, bytes_accessed=6 * MIB, transcendentals=0
+            flops=2 * MIB, bytes_accessed=4 * MIB, transcendentals=0
         ),
         name="combine",
-    )(got, more, near)
+    )(got, more, first)
 
 
 def spread_kernel(parts, far, out):
@@ -316,14 +321,13 @@
 
     anyone = jnp.max(got[:, BODY, FLAG].astype(jnp.float32)) > 0
     more = lax.cond(anyone, lambda v: exchange(v, ("rx", "rc")), lambda v: v, rest)
-    keep, send = combine(got, more, near)
+    send = combine(False, got, more, three)
     count = SIDE
     even = [(c, c ^ 1) for c in range(count)]
     odd = [(count + c, count + (c + (1 if c % 2 else -1)) % count) for c in range(count)]
     taken = lax.ppermute(send, ("rc", "ch", "cl"), even + odd)
-    parts = exchange(
-        (keep.astype(jnp.float32) + taken.astype(jnp.float32)).astype(jnp.bfloat16), "ch"
-    )
+    keep = combine(True, got, more, near)
+    parts = exchange(keep + taken, "ch")
 
     own = exchange(spread(parts, far), ("lq", "rx"))
     other = lax.ppermute(own, "rc", swap)

time: 182 us -> 187 us (1.027)
  waiting for transfers between devices: 55.6 us -> 45.9 us
  local copies, waits for them, and re-layouts: 0.29 us -> 9.59 us
  Pallas kernels: 16.3 us -> 20.5 us
  starting transfers between devices: 51.6 us -> 54.2 us
  other arithmetic: 3.91 us -> 1.98 us
    ppermute x1, waiting for transfers between devices: 10.3 us -> 0.58 us  [body(): taken = lax.ppermute(send, ('rc', 'ch', 'cl'), even + odd)]
    unnamed x15 -> x11, local copies, waits for them, and re-layouts: 0.26 us -> 7.91 us
    ppermute x1, waiting for transfers between devices: 29.5 us -> 35.8 us  [body(): far = lax.ppermute(near, 'lq', swap)]
    pallas_call x1 -> x2, Pallas kernels: 4.86 us -> 9.17 us  [combine(): pl.pallas_call(functools.partial(combine_kernel, keeps), out_shape=jax.Sh...]
    ppermute x7, waiting for transfers between devices: 10.9 us -> 6.83 us  [ahead(): lax.ppermute(block, ('ch', 'cl'), [(c, (c - distance) % SIDE) for c in ra...]
    convert_element_type x1 -> x0, other arithmetic: 2.51 us -> none  [body(): (keep.astype(jnp.float32) + taken.astype(jnp.float32)).astype(jnp.bfloat16)]
    all_to_all x2, waiting for transfers between devices: 2.53 us -> 0.45 us  [exchange(): return lax.all_to_all(values, axes, split_axis=0, concat_axis=0, tiled=True)]
  transfers between devices with their start and end apart: 12 -> 12, of which waited for: 8 -> 6; matrix products, arithmetic and copies ran while one was open for 2% -> 6% of each run, Pallas kernels for 0% -> 5%
where the time goes in v5:
time: 187 us; the launch traced here: 186 us
  starting transfers between devices  54.2 us (29%)
  blocking collectives  52.7 us (28%)
  waiting for transfers between devices  45.9 us (25%)
  Pallas kernels  20.5 us (11%)
  local copies, waits for them, and re-layouts  9.59 us (5%)
  other arithmetic  1.98 us (1%)
    all_to_all x2, blocking collectives, exchange(): return lax.all_to_all(values, axes, split_axis=0, concat_axis=0, tiled=True)  52.7 us
    ppermute x1, waiting for transfers between devices, body(): far = lax.ppermute(near, 'lq', swap)  35.8 us
    ppermute x7, starting transfers between devices, ahead(): lax.ppermute(block, ('ch', 'cl'), [(c, (c - distance) % SIDE) for c in ra...  26 us
    all_to_all x2, starting transfers between devices, exchange(): return lax.all_to_all(values, axes, split_axis=0, concat_axis=0, tiled=True)  14 us
    pallas_call x2, Pallas kernels, combine(): pl.pallas_call(functools.partial(combine_kernel, keeps), out_shape=jax.Sh...  9.17 us
    ppermute x1, starting transfers between devices, body(): taken = lax.ppermute(send, ('rc', 'ch', 'cl'), even + odd)  8.18 us
    unnamed x11, local copies, waits for them, and re-layouts  7.91 us
    ppermute x7, waiting for transfers between devices, ahead(): lax.ppermute(block, ('ch', 'cl'), [(c, (c - distance) % SIDE) for c in ra...  6.83 us
  transfers between devices with their start and end apart: 12, of which 6 were waited for; matrix products, arithmetic and copies ran while one was open for 6% of the time, Pallas kernels for 5%

profile of v5, /device:TPU:1, one launch (start us, length us, event | category | flops | bytes accessed | tf_op | source)
XLA Modules:
  0.0 185.8 jit_solution(1580066605399881873)
XLA Ops:
  0.0 4.4 %pack.1 = (bf16[8,1552,128]{2,1,0:T(8,128)(2,1)}, bf16[8,512,128]{2,1,0:T(8,128)(2,1)}, bf16[1024,128]{1,0:T(8,128)(2,1)}) custom-call(s32[64]{0:T(128)} %bitcast.19, s32[64]{0:T(128)} %slots.1, s32[64,64]{1,0:T(8,128)} %pattern.3, bf16[64,128,128]{2,1,0:T(8,128)(2,1)} %contributions.1, bf16[1024,128]{1,0:T(8,128)(2,1)} %density.1), custom_call_target="tpu_custom_call" | custom-call | bytes 7340032 | tf_op jit(solution)/shard_map/pack/pallas_call | solution.py:86
  4.4 10.4 %all-to-all-start.1 = ((bf16[8,1552,128]{2,1,0:T(8,128)(2,1)}), bf16[8,1552,128]{2,1,0:T(8,128)(2,1)S(1)}, u32[]{:S(2)}, u32[]{:S(2)}) async-start(bf16[8,1552,128]{2,1,0:T(8,128)(2,1)} %get-tuple-element.14), calls=%async_computation.1 | async-start | bytes 6356992 | tf_op jit(solution)/shard_map/all_to_all | solution.py:304
  14.9 6.0 %collective-permute-start.1 = (bf16[1024,128]{1,0:T(8,128)(2,1)}, bf16[1024,128]{1,0:T(8,128)(2,1)S(1)}, u32[]{:S(2)}, u32[]{:S(2)}) collective-permute-start(bf16[1024,128]{1,0:T(8,128)(2,1)} %get-tuple-element.13), channel_id=1, source_target_pairs={{0,6},{1,7},{2,0},{3,1},{4,2},{5,3},{6,4},{7,5},{8,14},{9,15},{10,... | collective-permute-start | bytes 786440 | tf_op jit(solution)/shard_map/ppermute | solution.py:312
  20.9 2.2 %collective-permute-start = (bf16[1024,128]{1,0:T(8,128)(2,1)}, bf16[1024,128]{1,0:T(8,128)(2,1)S(1)}, u32[]{:S(2)}, u32[]{:S(2)}) collective-permute-start(bf16[1024,128]{1,0:T(8,128)(2,1)} %get-tuple-element.13), channel_id=1, source_target_pairs={{0,7},{1,0},{2,1},{3,2},{4,3},{5,4},{6,5},{7,6},{8,15},{9,8},{10,9... | collective-permute-start | bytes 786440 | tf_op jit(solution)/shard_map/ppermute | solution.py:312
  23.1 4.0 %collective-permute-start.4 = (bf16[1024,128]{1,0:T(8,128)(2,1)}, bf16[1024,128]{1,0:T(8,128)(2,1)}, u32[]{:S(2)}, u32[]{:S(2)}) collective-permute-start(bf16[1024,128]{1,0:T(8,128)(2,1)} %get-tuple-element.13), channel_id=1, source_target_pairs={{0,2},{1,3},{2,4},{3,5},{4,6},{5,7},{6,0},{7,1},{8,10},{9,11},{10,... | collective-permute-start | bytes 786440 | tf_op jit(solution)/shard_map/ppermute | solution.py:312
  27.1 1.9 %collective-permute-start.6 = (bf16[1024,128]{1,0:T(8,128)(2,1)}, bf16[1024,128]{1,0:T(8,128)(2,1)}, u32[]{:S(2)}, u32[]{:S(2)}) collective-permute-start(bf16[1024,128]{1,0:T(8,128)(2,1)} %get-tuple-element.13), channel_id=1, source_target_pairs={{0,1},{1,2},{2,3},{3,4},{4,5},{5,6},{6,7},{7,0},{8,9},{9,10},{10,1... | collective-permute-start | bytes 786440 | tf_op jit(solution)/shard_map/ppermute | solution.py:312
  29.0 1.7 bitcast_dynamic-update-slice_fusion.7
  30.7 6.9 %collective-permute-start.2 = (bf16[1024,128]{1,0:T(8,128)(2,1)S(1)}, bf16[1024,128]{1,0:T(8,128)(2,1)S(1)}, u32[]{:S(2)}, u32[]{:S(2)}) collective-permute-start(bf16[1024,128]{1,0:T(8,128)(2,1)S(1)} %collective-permute-done.1), channel_id=1, source_target_pairs={{0,7},{1,0},{2,1},{3,2},{4,3},{5,4},{6,5},{7,6},{8,15},{9,8},{10,9... | collective-permute-start | bytes 786440 | tf_op jit(solution)/shard_map/ppermute | solution.py:312
  37.7 2.0 %collective-permute-start.3 = (bf16[1024,128]{1,0:T(8,128)(2,1)S(1)}, bf16[1024,128]{1,0:T(8,128)(2,1)S(1)}, u32[]{:S(2)}, u32[]{:S(2)}) collective-permute-start(bf16[1024,128]{1,0:T(8,128)(2,1)S(1)} %collective-permute-done.1), channel_id=1, source_target_pairs={{0,6},{1,7},{2,0},{3,1},{4,2},{5,3},{6,4},{7,5},{8,14},{9,15},{10,... | collective-permute-start | bytes 786440 | tf_op jit(solution)/shard_map/ppermute | solution.py:312
  39.6 0.7 bitcast_dynamic-update-slice_fusion.6
  40.4 0.7 bitcast_dynamic-update-slice_fusion.5
  41.1 3.0 %collective-permute-start.5 = (bf16[1024,128]{1,0:T(8,128)(2,1)}, bf16[1024,128]{1,0:T(8,128)(2,1)}, u32[]{:S(2)}, u32[]{:S(2)}) collective-permute-start(bf16[1024,128]{1,0:T(8,128)(2,1)} %collective-permute-done.4), channel_id=1, source_target_pairs={{0,1},{1,2},{2,3},{3,4},{4,5},{5,6},{6,7},{7,0},{8,9},{9,10},{10,1... | collective-permute-start | bytes 786440 | tf_op jit(solution)/shard_map/ppermute | solution.py:312
  44.2 3.0 %collective-permute-done.2.first = bf16[1024,128]{1,0:T(8,128)(2,1)S(1)} collective-permute-done((bf16[1024,128]{1,0:T(8,128)(2,1)S(1)}, bf16[1024,128]{1,0:T(8,128)(2,1)S(1)}, u32[]{:S(2)}, u32[]{:S(2)}) %collective-permute-start.2) | collective-permute-done | bytes 262176 | tf_op jit(solution)/shard_map/ppermute | solution.py:312
  47.2 0.7 bitcast_dynamic-update-slice_fusion.4
  47.9 3.8 %collective-permute-done.3 = bf16[1024,128]{1,0:T(8,128)(2,1)S(1)} collective-permute-done((bf16[1024,128]{1,0:T(8,128)(2,1)S(1)}, bf16[1024,128]{1,0:T(8,128)(2,1)S(1)}, u32[]{:S(2)}, u32[]{:S(2)}) %collective-permute-start.3) | collective-permute-done | bytes 262176 | tf_op jit(solution)/shard_map/ppermute | solution.py:312
  51.6 0.7 bitcast_dynamic-update-slice_fusion.3
  54.2 4.5 %combine.3 = bf16[4,2,128,512]{3,2,1,0:T(8,128)(2,1)S(1)} custom-call(bf16[8,1552,128]{2,1,0:T(8,128)(2,1)S(1)} %all-to-all-done.1.got, bf16[8,512,128]{2,1,0:T(8,128)(2,1)} %get-tuple-element.16.more, bf16[1024,128]{1,0:T(8,128)(2,1)S(1)} %collective-permute-done.2.first), custom_call_target="tpu_custom_call" | custom-call | flops 2097152 | bytes 4194304 | tf_op jit(solution)/shard_map/combine/pallas_call | solution.py:183
  58.7 8.2 %collective-permute-start.8 = (bf16[4,2,128,512]{3,2,1,0:T(8,128)(2,1)S(1)}, bf16[4,2,128,512]{3,2,1,0:T(8,128)(2,1)S(1)}, u32[]{:S(2)}, u32[]{:S(2)}) collective-permute-start(bf16[4,2,128,512]{3,2,1,0:T(8,128)(2,1)S(1)} %combine.3), channel_id=1, source_target_pairs={{0,1},{1,0},{2,3},{3,2},{4,5},{5,4},{6,7},{7,6},{8,15},{9,10},{10,... | collective-permute-start | bytes 3145736 | tf_op jit(solution)/shard_map/ppermute | solution.py:328
  66.9 1.7 bitcast_dynamic-update-slice_fusion.2
  68.6 1.7 bitcast_dynamic-update-slice_fusion.1
  70.3 1.7 bitcast_dynamic-update-slice_fusion.first.near
  71.9 1.9 %collective-permute-start.7 = (bf16[8,1024,128]{2,1,0:T(8,128)(2,1)}, bf16[8,1024,128]{2,1,0:T(8,128)(2,1)}, u32[]{:S(2)}, u32[]{:S(2)}) collective-permute-start(bf16[8,1024,128]{2,1,0:T(8,128)(2,1)} %bitcast_dynamic-update-slice_fusion.first.near), channel_id=1, source_target_pairs={{0,64},{64,0},{1,65},{65,1},{2,66},{66,2},{3,67},{67,3},{4,68},{68... | collective-permute-start | bytes 6291464 | tf_op jit(solution)/shard_map/ppermute | solution.py:320
  73.9 4.6 %combine.2 = bf16[4,2,128,512]{3,2,1,0:T(8,128)(2,1)S(1)} custom-call(bf16[8,1552,128]{2,1,0:T(8,128)(2,1)S(1)} %all-to-all-done.1.got, bf16[8,512,128]{2,1,0:T(8,128)(2,1)S(1)} %copy-done.1, bf16[8,1024,128]{2,1,0:T(8,128)(2,1)} %bitcast_dynamic-update-slice_fusion.first.near), custom_call_target="tpu_custom_call" | custom-call | flops 2097152 | bytes 4194304 | tf_op jit(solution)/shard_map/combine/pallas_call | solution.py:183
  79.1 1.3 add.3
  80.4 3.5 %all-to-all-start.2 = ((bf16[4,2,128,512]{3,2,1,0:T(8,128)(2,1)}), bf16[4,2,128,512]{3,2,1,0:T(8,128)(2,1)S(1)}, u32[]{:S(2)}, u32[]{:S(2)}) async-start(bf16[4,2,128,512]{3,2,1,0:T(8,128)(2,1)} %add.3), calls=%async_computation.2 | async-start | bytes 2097152 | tf_op jit(solution)/shard_map/all_to_all | solution.py:304
  83.9 35.8 %collective-permute-done.7.far = bf16[8,1024,128]{2,1,0:T(8,128)(2,1)} collective-permute-done((bf16[8,1024,128]{2,1,0:T(8,128)(2,1)}, bf16[8,1024,128]{2,1,0:T(8,128)(2,1)}, u32[]{:S(2)}, u32[]{:S(2)}) %collective-permute-start.7) | collective-permute-done | bytes 2097184 | tf_op jit(solution)/shard_map/ppermute | solution.py:320
  119.8 19.1 %all_to_all.25.own = bf16[8,128,512]{2,1,0:T(8,128)(2,1)S(1)} all-to-all(bf16[8,128,512]{2,1,0:T(8,128)(2,1)S(1)} %spread.1), channel_id=1, replica_groups=mesh['lg'=4,'lq'=2,'rx'=4,'rc'=2,'ch'=4,'cl'=2] {'lq','rx'}, dimensions={0} | all-to-all | bytes 2097152 | tf_op jit(solution)/shard_map/all_to_all | solution.py:304
  138.9 4.2 %collective-permute-start.9 = (bf16[8,128,512]{2,1,0:T(8,128)(2,1)S(1)}, bf16[8,128,512]{2,1,0:T(8,128)(2,1)S(1)}, u32[]{:S(2)}, u32[]{:S(2)}) collective-permute-start(bf16[8,128,512]{2,1,0:T(8,128)(2,1)S(1)} %all_to_all.25.own), channel_id=1, source_target_pairs={{0,8},{8,0},{1,9},{9,1},{2,10},{10,2},{3,11},{11,3},{4,12},{12,4},... | collective-permute-start | bytes 3145736 | tf_op jit(solution)/shard_map/ppermute | solution.py:333
  143.1 2.3 %collective-permute-done.9.other = bf16[8,128,512]{2,1,0:T(8,128)(2,1)S(1)} collective-permute-done((bf16[8,128,512]{2,1,0:T(8,128)(2,1)S(1)}, bf16[8,128,512]{2,1,0:T(8,128)(2,1)S(1)}, u32[]{:S(2)}, u32[]{:S(2)}) %collective-permute-start.9) | collective-permute-done | bytes 1048608 | tf_op jit(solution)/shard_map/ppermute | solution.py:333
  145.3 4.9 %product.1 = bf16[1024,512]{1,0:T(8,128)(2,1)S(1)} custom-call(bf16[8,1024,128]{2,1,0:T(8,128)(2,1)} %bitcast_dynamic-update-slice_fusion.first.near, bf16[8,1024,128]{2,1,0:T(8,128)(2,1)} %collective-permute-done.7.far, bf16[8,128,512]{2,1,0:T(8,128)(2,1)S(1)} %all_to_all.25.own, bf16[8,128,512]{2,1,0:T(8,128)(2,1)S(1)} %collective-permute-done.9.other), custom_call_target="tpu_custom_call" | custom-call | flops 2147483648 | bytes 7340032 | tf_op jit(solution)/shard_map/product/pallas_call | solution.py:256
  150.2 33.6 %all_to_all.26.terms = bf16[8,128,512]{2,1,0:T(8,128)(2,1)S(1)} all-to-all(bf16[8,128,512]{2,1,0:T(8,128)(2,1)S(1)} %bitcast.18), channel_id=1, replica_groups=mesh['lg'=4,'lq'=2,'rx'=4,'rc'=2,'ch'=4,'cl'=2] {'lg','lq'}, dimensions={0} | all-to-all | bytes 2097152 | tf_op jit(solution)/shard_map/all_to_all | solution.py:304
  183.9 1.9 %finish.1 = bf16[128,1024]{1,0:T(8,128)(2,1)} custom-call(s32[64,64]{1,0:T(8,128)S(1)} %copy-done, bf16[8,128,512]{2,1,0:T(8,128)(2,1)S(1)} %all_to_all.26.terms), custom_call_target="tpu_custom_call" | custom-call | flops 1048576 | bytes 2097152 | tf_op jit(solution)/shard_map/finish/pallas_call | solution.py:289
  (15 shorter events, 1.9 us)
Async XLA Ops:
  4.4 48.4 %all-to-all-start.1 = ((bf16[8,1552,128]{2,1,0:T(8,128)(2,1)}), bf16[8,1552,128]{2,1,0:T(8,128)(2,1)S(1)}, u32[]{:S(2)}, u32[]{:S(2)}) async-start(bf16[8,1552,128]{2,1,0:T(8,128)(2,1)} %get-tuple-element.14), calls=%async_computation.1 | async-start | bytes 6356992 | tf_op jit(solution)/shard_map/all_to_all | solution.py:304
  14.9 15.9 %collective-permute-start.1 = (bf16[1024,128]{1,0:T(8,128)(2,1)}, bf16[1024,128]{1,0:T(8,128)(2,1)S(1)}, u32[]{:S(2)}, u32[]{:S(2)}) collective-permute-start(bf16[1024,128]{1,0:T(8,128)(2,1)} %get-tuple-element.13), channel_id=1, source_target_pairs={{0,6},{1,7},{2,0},{3,1},{4,2},{5,3},{6,4},{7,5},{8,14},{9,15},{10,... | collective-permute-start | bytes 786440 | tf_op jit(solution)/shard_map/ppermute | solution.py:312
  20.9 18.7 %collective-permute-start = (bf16[1024,128]{1,0:T(8,128)(2,1)}, bf16[1024,128]{1,0:T(8,128)(2,1)S(1)}, u32[]{:S(2)}, u32[]{:S(2)}) collective-permute-start(bf16[1024,128]{1,0:T(8,128)(2,1)} %get-tuple-element.13), channel_id=1, source_target_pairs={{0,7},{1,0},{2,1},{3,2},{4,3},{5,4},{6,5},{7,6},{8,15},{9,8},{10,9... | collective-permute-start | bytes 786440 | tf_op jit(solution)/shard_map/ppermute | solution.py:312
  23.1 18.0 %collective-permute-start.4 = (bf16[1024,128]{1,0:T(8,128)(2,1)}, bf16[1024,128]{1,0:T(8,128)(2,1)}, u32[]{:S(2)}, u32[]{:S(2)}) collective-permute-start(bf16[1024,128]{1,0:T(8,128)(2,1)} %get-tuple-element.13), channel_id=1, source_target_pairs={{0,2},{1,3},{2,4},{3,5},{4,6},{5,7},{6,0},{7,1},{8,10},{9,11},{10,... | collective-permute-start | bytes 786440 | tf_op jit(solution)/shard_map/ppermute | solution.py:312
  27.1 43.2 %collective-permute-start.6 = (bf16[1024,128]{1,0:T(8,128)(2,1)}, bf16[1024,128]{1,0:T(8,128)(2,1)}, u32[]{:S(2)}, u32[]{:S(2)}) collective-permute-start(bf16[1024,128]{1,0:T(8,128)(2,1)} %get-tuple-element.13), channel_id=1, source_target_pairs={{0,1},{1,2},{2,3},{3,4},{4,5},{5,6},{6,7},{7,0},{8,9},{9,10},{10,1... | collective-permute-start | bytes 786440 | tf_op jit(solution)/shard_map/ppermute | solution.py:312
  30.7 16.4 %collective-permute-start.2 = (bf16[1024,128]{1,0:T(8,128)(2,1)S(1)}, bf16[1024,128]{1,0:T(8,128)(2,1)S(1)}, u32[]{:S(2)}, u32[]{:S(2)}) collective-permute-start(bf16[1024,128]{1,0:T(8,128)(2,1)S(1)} %collective-permute-done.1), channel_id=1, source_target_pairs={{0,7},{1,0},{2,1},{3,2},{4,3},{5,4},{6,5},{7,6},{8,15},{9,8},{10,9... | collective-permute-start | bytes 786440 | tf_op jit(solution)/shard_map/ppermute | solution.py:312
  37.7 14.0 %collective-permute-start.3 = (bf16[1024,128]{1,0:T(8,128)(2,1)S(1)}, bf16[1024,128]{1,0:T(8,128)(2,1)S(1)}, u32[]{:S(2)}, u32[]{:S(2)}) collective-permute-start(bf16[1024,128]{1,0:T(8,128)(2,1)S(1)} %collective-permute-done.1), channel_id=1, source_target_pairs={{0,6},{1,7},{2,0},{3,1},{4,2},{5,3},{6,4},{7,5},{8,14},{9,15},{10,... | collective-permute-start | bytes 786440 | tf_op jit(solution)/shard_map/ppermute | solution.py:312
  41.1 25.8 %collective-permute-start.5 = (bf16[1024,128]{1,0:T(8,128)(2,1)}, bf16[1024,128]{1,0:T(8,128)(2,1)}, u32[]{:S(2)}, u32[]{:S(2)}) collective-permute-start(bf16[1024,128]{1,0:T(8,128)(2,1)} %collective-permute-done.4), channel_id=1, source_target_pairs={{0,1},{1,2},{2,3},{3,4},{4,5},{5,6},{6,7},{7,0},{8,9},{9,10},{10,1... | collective-permute-start | bytes 786440 | tf_op jit(solution)/shard_map/ppermute | solution.py:312
  58.7 15.1 %copy-start.1 = (bf16[8,512,128]{2,1,0:T(8,128)(2,1)S(1)}, bf16[8,512,128]{2,1,0:T(8,128)(2,1)}, u32[]{:S(2)}) copy-start(bf16[8,512,128]{2,1,0:T(8,128)(2,1)} %get-tuple-element.16.more) | copy-start | bytes 3145732
  58.7 20.4 %collective-permute-start.8 = (bf16[4,2,128,512]{3,2,1,0:T(8,128)(2,1)S(1)}, bf16[4,2,128,512]{3,2,1,0:T(8,128)(2,1)S(1)}, u32[]{:S(2)}, u32[]{:S(2)}) collective-permute-start(bf16[4,2,128,512]{3,2,1,0:T(8,128)(2,1)S(1)} %combine.3), channel_id=1, source_target_pairs={{0,1},{1,0},{2,3},{3,2},{4,5},{5,4},{6,7},{7,6},{8,15},{9,10},{10,... | collective-permute-start | bytes 3145736 | tf_op jit(solution)/shard_map/ppermute | solution.py:328
  71.9 47.7 %collective-permute-start.7 = (bf16[8,1024,128]{2,1,0:T(8,128)(2,1)}, bf16[8,1024,128]{2,1,0:T(8,128)(2,1)}, u32[]{:S(2)}, u32[]{:S(2)}) collective-permute-start(bf16[8,1024,128]{2,1,0:T(8,128)(2,1)} %bitcast_dynamic-update-slice_fusion.first.near), channel_id=1, source_target_pairs={{0,64},{64,0},{1,65},{65,1},{2,66},{66,2},{3,67},{67,3},{4,68},{68... | collective-permute-start | bytes 6291464 | tf_op jit(solution)/shard_map/ppermute | solution.py:320
  80.4 39.3 %all-to-all-start.2 = ((bf16[4,2,128,512]{3,2,1,0:T(8,128)(2,1)}), bf16[4,2,128,512]{3,2,1,0:T(8,128)(2,1)S(1)}, u32[]{:S(2)}, u32[]{:S(2)}) async-start(bf16[4,2,128,512]{3,2,1,0:T(8,128)(2,1)} %add.3), calls=%async_computation.2 | async-start | bytes 2097152 | tf_op jit(solution)/shard_map/all_to_all | solution.py:304
  138.9 6.4 %collective-permute-start.9 = (bf16[8,128,512]{2,1,0:T(8,128)(2,1)S(1)}, bf16[8,128,512]{2,1,0:T(8,128)(2,1)S(1)}, u32[]{:S(2)}, u32[]{:S(2)}) collective-permute-start(bf16[8,128,512]{2,1,0:T(8,128)(2,1)S(1)} %all_to_all.25.own), channel_id=1, source_target_pairs={{0,8},{8,0},{1,9},{9,1},{2,10},{10,2},{3,11},{11,3},{4,12},{12,4},... | collective-permute-start | bytes 3145736 | tf_op jit(solution)/shard_map/ppermute | solution.py:333
  150.2 33.6 %copy-start = (s32[64,64]{1,0:T(8,128)S(1)}, s32[64,64]{1,0:T(8,128)}, u32[]{:S(2)}) copy-start(s32[64,64]{1,0:T(8,128)} %pattern.3) | copy-start | bytes 49156

commit v6 on v5

--- a/solution.py
+++ b/solution.py
@@ -228,41 +228,42 @@
     )(parts, far)
 
 
-def product_kernel(near, far, own, other, out, ham):
+def product_kernel(near, near_late, far, far_late, own, other, out, ham):
     half = SIDE * TILE
     core, layer = lax.axis_index("rc"), lax.axis_index("lq")
     column = lax.axis_index(("ch", "cl"))
+
+    def slot(block):
+        distance = (block - column + SIDE) % SIDE
+        return jnp.where(distance == 7, 3, jnp.where(distance < 3, distance, distance + 1))
 
     @pl.when(pl.program_id(0) == 0)
     def _():
         for l in range(2):
             base = jnp.where(layer == l, 0, half)
             for j in range(SIDE // 2):
-                mine = base + (2 * j + core - column + SIDE) % SIDE * TILE
-                theirs = base + (2 * j + 1 - core - column + SIDE) % SIDE * TILE
+                mine = base + slot(2 * j + core) * TILE
+                theirs = base + slot(2 * j + 1 - core) * TILE
                 ham[pl.ds(pl.multiple_of(mine, TILE), TILE)] = own[l * 4 + j]
                 ham[pl.ds(pl.multiple_of(theirs, TILE), TILE)] = other[l * 4 + j]
 
-    blocks = [near[c] for c in range(SIDE)] + [far[c] for c in range(SIDE)]
-    rows = jnp.concatenate(blocks, axis=1)
+    parts = (near, near_late, far, far_late)
+    rows = jnp.concatenate([part[c] for part in parts for c in range(SIDE // 2)], axis=1)
     total = jnp.dot(rows, ham[...], preferred_element_type=jnp.float32)
     out[...] = total.astype(jnp.bfloat16)
 
 
-def product_of(near, far, own, other):
+def product_of(near, near_late, far, far_late, own, other):
     rows = near.shape[1]
     step = 256
     width = own.shape[2]
+    block = pl.BlockSpec((SIDE // 2, step, TILE), lambda i: (0, i, 0))
+    whole = pl.BlockSpec(own.shape, lambda i: (0, 0, 0))
     return pl.pallas_call(
         product_kernel,
         out_shape=jax.ShapeDtypeStruct((rows, width), jnp.bfloat16),
         grid=(rows // step,),
-        in_specs=[
-            pl.BlockSpec((SIDE, step, TILE), lambda i: (0, i, 0)),
-            pl.BlockSpec((SIDE, step, TILE), lambda i: (0, i, 0)),
-            pl.BlockSpec(own.shape, lambda i: (0, 0, 0)),
-            pl.BlockSpec(own.shape, lambda i: (0, 0, 0)),
-        ],
+        in_specs=[block, block, block, block, whole, whole],
         out_specs=pl.BlockSpec((step, width), lambda i: (i, 0)),
         scratch_shapes=[pltpu.VMEM((2 * SIDE * TILE, width), jnp.bfloat16)],
         compiler_params=pltpu.CompilerParams(vmem_limit_bytes=SMALL_MIB * MIB),
@@ -270,7 +271,7 @@
             flops=4 * rows * rows * width, bytes_accessed=7 * MIB, transcendentals=0
         ),
         name="product",
-    )(near, far, own, other)
+    )(near, near_late, far, far_late, own, other)
 
 
 def finish_kernel(pattern, terms, out):
@@ -315,23 +316,25 @@
 
     one, last, two, sixth = (ahead(sparse, distance) for distance in (1, -1, 2, -2))
     three, fifth, four = ahead(two, 1), ahead(sixth, -1), ahead(two, 2)
-    near = jnp.stack([sparse, one, two, three, four, fifth, sixth, last])
     swap = [(0, 1), (1, 0)]
+    near = jnp.stack([sparse, one, two, last])
     far = lax.ppermute(near, "lq", swap)
+    near_late = jnp.stack([three, four, fifth, sixth])
+    far_late = lax.ppermute(near_late, "lq", swap)
 
     anyone = jnp.max(got[:, BODY, FLAG].astype(jnp.float32)) > 0
     more = lax.cond(anyone, lambda v: exchange(v, ("rx", "rc")), lambda v: v, rest)
-    send = combine(False, got, more, three)
+    send = combine(False, got, more, near_late)
     count = SIDE
     even = [(c, c ^ 1) for c in range(count)]
     odd = [(count + c, count + (c + (1 if c % 2 else -1)) % count) for c in range(count)]
     taken = lax.ppermute(send, ("rc", "ch", "cl"), even + odd)
-    keep = combine(True, got, more, near)
+    keep = combine(True, got, more, far)
     parts = exchange(keep + taken, "ch")
 
-    own = exchange(spread(parts, far), ("lq", "rx"))
+    own = exchange(spread(parts, far_late), ("lq", "rx"))
     other = lax.ppermute(own, "rc", swap)
-    term = product_of(near, far, own, other)
+    term = product_of(near, near_late, far, far_late, own, other)
     terms = exchange(term.reshape(SIDE, TILE, -1), ("lg", "lq"))
     return finish(pattern, terms)
 

time: 187 us -> 182 us (0.973)
  local copies, waits for them, and re-layouts: 9.59 us -> 1.24 us
  starting transfers between devices: 54.2 us -> 60.1 us
  blocking collectives: 52.7 us -> 49.7 us
  other arithmetic: 1.98 us -> 4.2 us
    ppermute x1, waiting for transfers between devices: 35.8 us -> 0.49 us  [body(): far = lax.ppermute(near, 'lq', swap)]
    ppermute x0 -> x1, waiting for transfers between devices: none -> 23 us  [body(): far_late = lax.ppermute(near_late, 'lq', swap)]
    ppermute x1, waiting for transfers between devices: 0.58 us -> 8.3 us  [body(): taken = lax.ppermute(send, ('rc', 'ch', 'cl'), even + odd)]
    unnamed x11 -> x10, local copies, waits for them, and re-layouts: 7.91 us -> 1.24 us
    ppermute x1, starting transfers between devices: 8.18 us -> 3.2 us  [body(): taken = lax.ppermute(send, ('rc', 'ch', 'cl'), even + odd)]
    ppermute x7, waiting for transfers between devices: 6.83 us -> 10.1 us  [ahead(): lax.ppermute(block, ('ch', 'cl'), [(c, (c - distance) % SIDE) for c in ra...]
    ppermute x0 -> x1, starting transfers between devices: none -> 3.27 us  [body(): far_late = lax.ppermute(near_late, 'lq', swap)]
    all_to_all x2, blocking collectives: 52.7 us -> 49.7 us  [exchange(): return lax.all_to_all(values, axes, split_axis=0, concat_axis=0, tiled=True)]
  transfers between devices with their start and end apart: 12 -> 13, of which waited for: 6 -> 6; matrix products, arithmetic and copies ran while one was open for 6% -> 2% of each run, Pallas kernels for 5% -> 5%
where the time goes in v6:
time: 182 us; the launch traced here: 181 us
  starting transfers between devices  60.1 us (33%)
  blocking collectives  49.7 us (27%)
  waiting for transfers between devices  44.2 us (24%)
  Pallas kernels  20.5 us (11%)
  other arithmetic  4.2 us (2%)
    all_to_all x2, blocking collectives, exchange(): return lax.all_to_all(values, axes, split_axis=0, concat_axis=0, tiled=True)  49.7 us
    ppermute x7, starting transfers between devices, ahead(): lax.ppermute(block, ('ch', 'cl'), [(c, (c - distance) % SIDE) for c in ra...  28.6 us
    ppermute x1, waiting for transfers between devices, body(): far_late = lax.ppermute(near_late, 'lq', swap)  23 us
    all_to_all x2, starting transfers between devices, exchange(): return lax.all_to_all(values, axes, split_axis=0, concat_axis=0, tiled=True)  16 us
    ppermute x7, waiting for transfers between devices, ahead(): lax.ppermute(block, ('ch', 'cl'), [(c, (c - distance) % SIDE) for c in ra...  10.1 us
    pallas_call x2, Pallas kernels, combine(): pl.pallas_call(functools.partial(combine_kernel, keeps), out_shape=jax.Sh...  9.52 us
    ppermute x1, waiting for transfers between devices, body(): taken = lax.ppermute(send, ('rc', 'ch', 'cl'), even + odd)  8.3 us
    ppermute x1, starting transfers between devices, body(): other = lax.ppermute(own, 'rc', swap)  5.77 us
  transfers between devices with their start and end apart: 13, of which 6 were waited for; matrix products, arithmetic and copies ran while one was open for 2% of the time, Pallas kernels for 5%

profile of v6, /device:TPU:1, one launch (start us, length us, event | category | flops | bytes accessed | tf_op | source)
XLA Modules:
  0.0 180.8 jit_solution(6673814900147372222)
XLA Ops:
  0.0 4.4 %pack.1 = (bf16[8,1552,128]{2,1,0:T(8,128)(2,1)}, bf16[8,512,128]{2,1,0:T(8,128)(2,1)}, bf16[1024,128]{1,0:T(8,128)(2,1)}) custom-call(s32[64]{0:T(128)} %bitcast.19, s32[64]{0:T(128)} %slots.1, s32[64,64]{1,0:T(8,128)} %pattern.3, bf16[64,128,128]{2,1,0:T(8,128)(2,1)} %contributions.1, bf16[1024,128]{1,0:T(8,128)(2,1)} %density.1), custom_call_target="tpu_custom_call" | custom-call | bytes 7340032 | tf_op jit(solution)/shard_map/pack/pallas_call | solution.py:86
  4.4 10.6 %all-to-all-start.1 = ((bf16[8,1552,128]{2,1,0:T(8,128)(2,1)}), bf16[8,1552,128]{2,1,0:T(8,128)(2,1)S(1)}, u32[]{:S(2)}, u32[]{:S(2)}) async-start(bf16[8,1552,128]{2,1,0:T(8,128)(2,1)} %get-tuple-element.14), calls=%async_computation.1 | async-start | bytes 6356992 | tf_op jit(solution)/shard_map/all_to_all | solution.py:305
  15.0 1.9 %collective-permute-start.5 = (bf16[1024,128]{1,0:T(8,128)(2,1)S(1)}, bf16[1024,128]{1,0:T(8,128)(2,1)S(1)}, u32[]{:S(2)}, u32[]{:S(2)}) collective-permute-start(bf16[1024,128]{1,0:T(8,128)(2,1)S(1)} %copy-done.4), channel_id=1, source_target_pairs={{0,2},{1,3},{2,4},{3,5},{4,6},{5,7},{6,0},{7,1},{8,10},{9,11},{10,... | collective-permute-start | bytes 786440 | tf_op jit(solution)/shard_map/ppermute | solution.py:313
  16.9 6.0 %collective-permute-start.1 = (bf16[1024,128]{1,0:T(8,128)(2,1)S(1)}, bf16[1024,128]{1,0:T(8,128)(2,1)S(1)}, u32[]{:S(2)}, u32[]{:S(2)}) collective-permute-start(bf16[1024,128]{1,0:T(8,128)(2,1)S(1)} %copy-done.4), channel_id=1, source_target_pairs={{0,6},{1,7},{2,0},{3,1},{4,2},{5,3},{6,4},{7,5},{8,14},{9,15},{10,... | collective-permute-start | bytes 786440 | tf_op jit(solution)/shard_map/ppermute | solution.py:313
  23.0 3.1 %collective-permute-start.2 = (bf16[1024,128]{1,0:T(8,128)(2,1)S(1)}, bf16[1024,128]{1,0:T(8,128)(2,1)S(1)}, u32[]{:S(2)}, u32[]{:S(2)}) collective-permute-start(bf16[1024,128]{1,0:T(8,128)(2,1)S(1)} %copy-done.4), channel_id=1, source_target_pairs={{0,1},{1,2},{2,3},{3,4},{4,5},{5,6},{6,7},{7,0},{8,9},{9,10},{10,1... | collective-permute-start | bytes 786440 | tf_op jit(solution)/shard_map/ppermute | solution.py:313
  26.1 3.4 %collective-permute-start = (bf16[1024,128]{1,0:T(8,128)(2,1)S(1)}, bf16[1024,128]{1,0:T(8,128)(2,1)S(1)}, u32[]{:S(2)}, u32[]{:S(2)}) collective-permute-start(bf16[1024,128]{1,0:T(8,128)(2,1)S(1)} %copy-done.4), channel_id=1, source_target_pairs={{0,7},{1,0},{2,1},{3,2},{4,3},{5,4},{6,5},{7,6},{8,15},{9,8},{10,9... | collective-permute-start | bytes 786440 | tf_op jit(solution)/shard_map/ppermute | solution.py:313
  29.5 7.0 %collective-permute-start.6 = (bf16[1024,128]{1,0:T(8,128)(2,1)S(1)}, bf16[1024,128]{1,0:T(8,128)(2,1)S(1)}, u32[]{:S(2)}, u32[]{:S(2)}) collective-permute-start(bf16[1024,128]{1,0:T(8,128)(2,1)S(1)} %collective-permute-done.5), channel_id=1, source_target_pairs={{0,1},{1,2},{2,3},{3,4},{4,5},{5,6},{6,7},{7,0},{8,9},{9,10},{10,1... | collective-permute-start | bytes 786440 | tf_op jit(solution)/shard_map/ppermute | solution.py:313
  36.5 3.4 %collective-permute-start.4 = (bf16[1024,128]{1,0:T(8,128)(2,1)S(1)}, bf16[1024,128]{1,0:T(8,128)(2,1)S(1)}, u32[]{:S(2)}, u32[]{:S(2)}) collective-permute-start(bf16[1024,128]{1,0:T(8,128)(2,1)S(1)} %collective-permute-done.1), channel_id=1, source_target_pairs={{0,6},{1,7},{2,0},{3,1},{4,2},{5,3},{6,4},{7,5},{8,14},{9,15},{10,... | collective-permute-start | bytes 786440 | tf_op jit(solution)/shard_map/ppermute | solution.py:313
  39.9 3.8 %collective-permute-start.3 = (bf16[1024,128]{1,0:T(8,128)(2,1)S(1)}, bf16[1024,128]{1,0:T(8,128)(2,1)S(1)}, u32[]{:S(2)}, u32[]{:S(2)}) collective-permute-start(bf16[1024,128]{1,0:T(8,128)(2,1)S(1)} %collective-permute-done.1), channel_id=1, source_target_pairs={{0,7},{1,0},{2,1},{3,2},{4,3},{5,4},{6,5},{7,6},{8,15},{9,8},{10,9... | collective-permute-start | bytes 786440 | tf_op jit(solution)/shard_map/ppermute | solution.py:313
  43.7 1.1 pad_maximum_fusion.near
  44.8 3.2 %collective-permute-start.7 = (bf16[4,1024,128]{2,1,0:T(8,128)(2,1)}, bf16[4,1024,128]{2,1,0:T(8,128)(2,1)}, u32[]{:S(2)}, u32[]{:S(2)}) collective-permute-start(bf16[4,1024,128]{2,1,0:T(8,128)(2,1)} %pad_maximum_fusion.near), channel_id=1, source_target_pairs={{0,64},{64,0},{1,65},{65,1},{2,66},{66,2},{3,67},{67,3},{4,68},{68... | collective-permute-start | bytes 3145736 | tf_op jit(solution)/shard_map/ppermute | solution.py:321
  48.1 3.4 %collective-permute-done.4 = bf16[1024,128]{1,0:T(8,128)(2,1)S(1)} collective-permute-done((bf16[1024,128]{1,0:T(8,128)(2,1)S(1)}, bf16[1024,128]{1,0:T(8,128)(2,1)S(1)}, u32[]{:S(2)}, u32[]{:S(2)}) %collective-permute-start.4) | collective-permute-done | bytes 262176 | tf_op jit(solution)/shard_map/ppermute | solution.py:313
  51.5 6.7 %collective-permute-done.3 = bf16[1024,128]{1,0:T(8,128)(2,1)S(1)} collective-permute-done((bf16[1024,128]{1,0:T(8,128)(2,1)S(1)}, bf16[1024,128]{1,0:T(8,128)(2,1)S(1)}, u32[]{:S(2)}, u32[]{:S(2)}) %collective-permute-start.3) | collective-permute-done | bytes 262176 | tf_op jit(solution)/shard_map/ppermute | solution.py:313
  58.2 1.1 pad_maximum_fusion.1.first.near_late
  59.3 0.7 slice_reduce_fusion
  60.7 1.2 copy-done
  61.9 4.8 %combine.3 = bf16[4,2,128,512]{3,2,1,0:T(8,128)(2,1)S(1)} custom-call(bf16[8,1552,128]{2,1,0:T(8,128)(2,1)S(1)} %all-to-all-done.1.got, bf16[8,512,128]{2,1,0:T(8,128)(2,1)} %get-tuple-element.16.more, bf16[4,1024,128]{2,1,0:T(8,128)(2,1)S(1)} %copy-done), custom_call_target="tpu_custom_call" | custom-call | flops 2097152 | bytes 4194304 | tf_op jit(solution)/shard_map/combine/pallas_call | solution.py:183
  66.7 3.2 %collective-permute-start.9 = (bf16[4,2,128,512]{3,2,1,0:T(8,128)(2,1)S(1)}, bf16[4,2,128,512]{3,2,1,0:T(8,128)(2,1)S(1)}, u32[]{:S(2)}, u32[]{:S(2)}) collective-permute-start(bf16[4,2,128,512]{3,2,1,0:T(8,128)(2,1)S(1)} %combine.3), channel_id=1, source_target_pairs={{0,1},{1,0},{2,3},{3,2},{4,5},{5,4},{6,7},{7,6},{8,15},{9,10},{10,... | collective-permute-start | bytes 3145736 | tf_op jit(solution)/shard_map/ppermute | solution.py:331
  69.9 0.5 collective-permute-done.7.first.far
  70.4 4.7 %combine.2 = bf16[4,2,128,512]{3,2,1,0:T(8,128)(2,1)S(1)} custom-call(bf16[8,1552,128]{2,1,0:T(8,128)(2,1)S(1)} %all-to-all-done.1.got, bf16[8,512,128]{2,1,0:T(8,128)(2,1)S(1)} %copy-done.3, bf16[4,1024,128]{2,1,0:T(8,128)(2,1)} %collective-permute-done.7.first.far), custom_call_target="tpu_custom_call" | custom-call | flops 2097152 | bytes 4194304 | tf_op jit(solution)/shard_map/combine/pallas_call | solution.py:183
  75.1 8.3 %collective-permute-done.9 = bf16[4,2,128,512]{3,2,1,0:T(8,128)(2,1)S(1)} collective-permute-done((bf16[4,2,128,512]{3,2,1,0:T(8,128)(2,1)S(1)}, bf16[4,2,128,512]{3,2,1,0:T(8,128)(2,1)S(1)}, u32[]{:S(2)}, u32[]{:S(2)}) %collective-permute-start.9) | collective-permute-done | bytes 1048608 | tf_op jit(solution)/shard_map/ppermute | solution.py:331
  83.4 1.3 add.3
  84.7 5.5 %all-to-all-start.2 = ((bf16[4,2,128,512]{3,2,1,0:T(8,128)(2,1)}), bf16[4,2,128,512]{3,2,1,0:T(8,128)(2,1)S(1)}, u32[]{:S(2)}, u32[]{:S(2)}) async-start(bf16[4,2,128,512]{3,2,1,0:T(8,128)(2,1)} %add.3), calls=%async_computation.2 | async-start | bytes 2097152 | tf_op jit(solution)/shard_map/all_to_all | solution.py:305
  90.2 3.3 %collective-permute-start.8 = (bf16[4,1024,128]{2,1,0:T(8,128)(2,1)S(1)}, bf16[4,1024,128]{2,1,0:T(8,128)(2,1)S(1)}, u32[]{:S(2)}, u32[]{:S(2)}) collective-permute-start(bf16[4,1024,128]{2,1,0:T(8,128)(2,1)S(1)} %copy-done.1), channel_id=1, source_target_pairs={{0,64},{64,0},{1,65},{65,1},{2,66},{66,2},{3,67},{67,3},{4,68},{68... | collective-permute-start | bytes 3145736 | tf_op jit(solution)/shard_map/ppermute | solution.py:323
  93.4 23.0 %collective-permute-done.8.far.far_late = bf16[4,1024,128]{2,1,0:T(8,128)(2,1)S(1)} collective-permute-done((bf16[4,1024,128]{2,1,0:T(8,128)(2,1)S(1)}, bf16[4,1024,128]{2,1,0:T(8,128)(2,1)S(1)}, u32[]{:S(2)}, u32[]{:S(2)}) %collective-permute-start.8) | collective-permute-done | bytes 1048608 | tf_op jit(solution)/shard_map/ppermute | solution.py:323
  116.5 0.1 spread.1
  116.6 15.7 %all_to_all.25.own = bf16[8,128,512]{2,1,0:T(8,128)(2,1)S(1)} all-to-all(bf16[8,128,512]{2,1,0:T(8,128)(2,1)S(1)} %spread.1), channel_id=1, replica_groups=mesh['lg'=4,'lq'=2,'rx'=4,'rc'=2,'ch'=4,'cl'=2] {'lq','rx'}, dimensions={0} | all-to-all | bytes 2097152 | tf_op jit(solution)/shard_map/all_to_all | solution.py:305
  132.3 5.8 %collective-permute-start.10 = (bf16[8,128,512]{2,1,0:T(8,128)(2,1)S(1)}, bf16[8,128,512]{2,1,0:T(8,128)(2,1)S(1)}, u32[]{:S(2)}, u32[]{:S(2)}) collective-permute-start(bf16[8,128,512]{2,1,0:T(8,128)(2,1)S(1)} %all_to_all.25.own), channel_id=1, source_target_pairs={{0,8},{8,0},{1,9},{9,1},{2,10},{10,2},{3,11},{11,3},{4,12},{12,4},... | collective-permute-start | bytes 3145736 | tf_op jit(solution)/shard_map/ppermute | solution.py:336
  138.1 2.3 %collective-permute-done.10.other = bf16[8,128,512]{2,1,0:T(8,128)(2,1)S(1)} collective-permute-done((bf16[8,128,512]{2,1,0:T(8,128)(2,1)S(1)}, bf16[8,128,512]{2,1,0:T(8,128)(2,1)S(1)}, u32[]{:S(2)}, u32[]{:S(2)}) %collective-permute-start.10) | collective-permute-done | bytes 1048608 | tf_op jit(solution)/shard_map/ppermute | solution.py:336
  140.3 4.5 %product.1 = bf16[1024,512]{1,0:T(8,128)(2,1)S(1)} custom-call(bf16[4,1024,128]{2,1,0:T(8,128)(2,1)} %pad_maximum_fusion.near, bf16[4,1024,128]{2,1,0:T(8,128)(2,1)S(1)} %copy-done.1, bf16[4,1024,128]{2,1,0:T(8,128)(2,1)} %collective-permute-done.7.first.far, bf16[4,1024,128]{2,1,0:T(8,128)(2,1)S(1)} %collective-permute-done.8.far.far_late, ...), custom_call_target="tpu_custom_call" | custom-call | flops 2147483648 | bytes 7340032 | tf_op jit(solution)/shard_map/product/pallas_call | solution.py:262
  144.9 34.0 %all_to_all.26.terms = bf16[8,128,512]{2,1,0:T(8,128)(2,1)S(1)} all-to-all(bf16[8,128,512]{2,1,0:T(8,128)(2,1)S(1)} %bitcast.10), channel_id=1, replica_groups=mesh['lg'=4,'lq'=2,'rx'=4,'rc'=2,'ch'=4,'cl'=2] {'lg','lq'}, dimensions={0} | all-to-all | bytes 2097152 | tf_op jit(solution)/shard_map/all_to_all | solution.py:305
  178.9 1.9 %finish.1 = bf16[128,1024]{1,0:T(8,128)(2,1)} custom-call(s32[64,64]{1,0:T(8,128)S(1)} %copy-done.2, bf16[8,128,512]{2,1,0:T(8,128)(2,1)S(1)} %all_to_all.26.terms), custom_call_target="tpu_custom_call" | custom-call | flops 1048576 | bytes 2097152 | tf_op jit(solution)/shard_map/finish/pallas_call | solution.py:290
  (17 shorter events, 0.0 us)
Async XLA Ops:
  4.4 10.6 %copy-start.4 = (bf16[1024,128]{1,0:T(8,128)(2,1)S(1)}, bf16[1024,128]{1,0:T(8,128)(2,1)}, u32[]{:S(2)}) copy-start(bf16[1024,128]{1,0:T(8,128)(2,1)} %get-tuple-element.13) | copy-start | bytes 786436
  4.4 54.9 %all-to-all-start.1 = ((bf16[8,1552,128]{2,1,0:T(8,128)(2,1)}), bf16[8,1552,128]{2,1,0:T(8,128)(2,1)S(1)}, u32[]{:S(2)}, u32[]{:S(2)}) async-start(bf16[8,1552,128]{2,1,0:T(8,128)(2,1)} %get-tuple-element.14), calls=%async_computation.1 | async-start | bytes 6356992 | tf_op jit(solution)/shard_map/all_to_all | solution.py:305
  15.0 14.5 %collective-permute-start.5 = (bf16[1024,128]{1,0:T(8,128)(2,1)S(1)}, bf16[1024,128]{1,0:T(8,128)(2,1)S(1)}, u32[]{:S(2)}, u32[]{:S(2)}) collective-permute-start(bf16[1024,128]{1,0:T(8,128)(2,1)S(1)} %copy-done.4), channel_id=1, source_target_pairs={{0,2},{1,3},{2,4},{3,5},{4,6},{5,7},{6,0},{7,1},{8,10},{9,11},{10,... | collective-permute-start | bytes 786440 | tf_op jit(solution)/shard_map/ppermute | solution.py:313
  16.9 19.6 %collective-permute-start.1 = (bf16[1024,128]{1,0:T(8,128)(2,1)S(1)}, bf16[1024,128]{1,0:T(8,128)(2,1)S(1)}, u32[]{:S(2)}, u32[]{:S(2)}) collective-permute-start(bf16[1024,128]{1,0:T(8,128)(2,1)S(1)} %copy-done.4), channel_id=1, source_target_pairs={{0,6},{1,7},{2,0},{3,1},{4,2},{5,3},{6,4},{7,5},{8,14},{9,15},{10,... | collective-permute-start | bytes 786440 | tf_op jit(solution)/shard_map/ppermute | solution.py:313
  23.0 20.7 %collective-permute-start.2 = (bf16[1024,128]{1,0:T(8,128)(2,1)S(1)}, bf16[1024,128]{1,0:T(8,128)(2,1)S(1)}, u32[]{:S(2)}, u32[]{:S(2)}) collective-permute-start(bf16[1024,128]{1,0:T(8,128)(2,1)S(1)} %copy-done.4), channel_id=1, source_target_pairs={{0,1},{1,2},{2,3},{3,4},{4,5},{5,6},{6,7},{7,0},{8,9},{9,10},{10,1... | collective-permute-start | bytes 786440 | tf_op jit(solution)/shard_map/ppermute | solution.py:313
  26.1 17.7 %collective-permute-start = (bf16[1024,128]{1,0:T(8,128)(2,1)S(1)}, bf16[1024,128]{1,0:T(8,128)(2,1)S(1)}, u32[]{:S(2)}, u32[]{:S(2)}) collective-permute-start(bf16[1024,128]{1,0:T(8,128)(2,1)S(1)} %copy-done.4), channel_id=1, source_target_pairs={{0,7},{1,0},{2,1},{3,2},{4,3},{5,4},{6,5},{7,6},{8,15},{9,8},{10,9... | collective-permute-start | bytes 786440 | tf_op jit(solution)/shard_map/ppermute | solution.py:313
  29.5 18.6 %collective-permute-start.6 = (bf16[1024,128]{1,0:T(8,128)(2,1)S(1)}, bf16[1024,128]{1,0:T(8,128)(2,1)S(1)}, u32[]{:S(2)}, u32[]{:S(2)}) collective-permute-start(bf16[1024,128]{1,0:T(8,128)(2,1)S(1)} %collective-permute-done.5), channel_id=1, source_target_pairs={{0,1},{1,2},{2,3},{3,4},{4,5},{5,6},{6,7},{7,0},{8,9},{9,10},{10,1... | collective-permute-start | bytes 786440 | tf_op jit(solution)/shard_map/ppermute | solution.py:313
  36.5 14.9 %collective-permute-start.4 = (bf16[1024,128]{1,0:T(8,128)(2,1)S(1)}, bf16[1024,128]{1,0:T(8,128)(2,1)S(1)}, u32[]{:S(2)}, u32[]{:S(2)}) collective-permute-start(bf16[1024,128]{1,0:T(8,128)(2,1)S(1)} %collective-permute-done.1), channel_id=1, source_target_pairs={{0,6},{1,7},{2,0},{3,1},{4,2},{5,3},{6,4},{7,5},{8,14},{9,15},{10,... | collective-permute-start | bytes 786440 | tf_op jit(solution)/shard_map/ppermute | solution.py:313
  39.9 18.2 %collective-permute-start.3 = (bf16[1024,128]{1,0:T(8,128)(2,1)S(1)}, bf16[1024,128]{1,0:T(8,128)(2,1)S(1)}, u32[]{:S(2)}, u32[]{:S(2)}) collective-permute-start(bf16[1024,128]{1,0:T(8,128)(2,1)S(1)} %collective-permute-done.1), channel_id=1, source_target_pairs={{0,7},{1,0},{2,1},{3,2},{4,3},{5,4},{6,5},{7,6},{8,15},{9,8},{10,9... | collective-permute-start | bytes 786440 | tf_op jit(solution)/shard_map/ppermute | solution.py:313
  44.8 25.5 %collective-permute-start.7 = (bf16[4,1024,128]{2,1,0:T(8,128)(2,1)}, bf16[4,1024,128]{2,1,0:T(8,128)(2,1)}, u32[]{:S(2)}, u32[]{:S(2)}) collective-permute-start(bf16[4,1024,128]{2,1,0:T(8,128)(2,1)} %pad_maximum_fusion.near), channel_id=1, source_target_pairs={{0,64},{64,0},{1,65},{65,1},{2,66},{66,2},{3,67},{67,3},{4,68},{68... | collective-permute-start | bytes 3145736 | tf_op jit(solution)/shard_map/ppermute | solution.py:321
  60.6 1.2 copy-start
  61.9 8.5 %copy-start.3 = (bf16[8,512,128]{2,1,0:T(8,128)(2,1)S(1)}, bf16[8,512,128]{2,1,0:T(8,128)(2,1)}, u32[]{:S(2)}) copy-start(bf16[8,512,128]{2,1,0:T(8,128)(2,1)} %get-tuple-element.16.more) | copy-start | bytes 3145732
  66.7 16.8 %collective-permute-start.9 = (bf16[4,2,128,512]{3,2,1,0:T(8,128)(2,1)S(1)}, bf16[4,2,128,512]{3,2,1,0:T(8,128)(2,1)S(1)}, u32[]{:S(2)}, u32[]{:S(2)}) collective-permute-start(bf16[4,2,128,512]{3,2,1,0:T(8,128)(2,1)S(1)} %combine.3), channel_id=1, source_target_pairs={{0,1},{1,0},{2,3},{3,2},{4,5},{5,4},{6,7},{7,6},{8,15},{9,10},{10,... | collective-permute-start | bytes 3145736 | tf_op jit(solution)/shard_map/ppermute | solution.py:331
  75.1 15.1 %copy-start.1 = (bf16[4,1024,128]{2,1,0:T(8,128)(2,1)S(1)}, bf16[4,1024,128]{2,1,0:T(8,128)(2,1)}, u32[]{:S(2)}) copy-start(bf16[4,1024,128]{2,1,0:T(8,128)(2,1)} %pad_maximum_fusion.1.first.near_late) | copy-start | bytes 3145732
  84.7 31.7 %all-to-all-start.2 = ((bf16[4,2,128,512]{3,2,1,0:T(8,128)(2,1)}), bf16[4,2,128,512]{3,2,1,0:T(8,128)(2,1)S(1)}, u32[]{:S(2)}, u32[]{:S(2)}) async-start(bf16[4,2,128,512]{3,2,1,0:T(8,128)(2,1)} %add.3), calls=%async_computation.2 | async-start | bytes 2097152 | tf_op jit(solution)/shard_map/all_to_all | solution.py:305
  90.2 26.3 %collective-permute-start.8 = (bf16[4,1024,128]{2,1,0:T(8,128)(2,1)S(1)}, bf16[4,1024,128]{2,1,0:T(8,128)(2,1)S(1)}, u32[]{:S(2)}, u32[]{:S(2)}) collective-permute-start(bf16[4,1024,128]{2,1,0:T(8,128)(2,1)S(1)} %copy-done.1), channel_id=1, source_target_pairs={{0,64},{64,0},{1,65},{65,1},{2,66},{66,2},{3,67},{67,3},{4,68},{68... | collective-permute-start | bytes 3145736 | tf_op jit(solution)/shard_map/ppermute | solution.py:323
  132.3 46.6 %copy-start.2 = (s32[64,64]{1,0:T(8,128)S(1)}, s32[64,64]{1,0:T(8,128)}, u32[]{:S(2)}) copy-start(s32[64,64]{1,0:T(8,128)} %pattern.3) | copy-start | bytes 49156
  132.3 8.0 %collective-permute-start.10 = (bf16[8,128,512]{2,1,0:T(8,128)(2,1)S(1)}, bf16[8,128,512]{2,1,0:T(8,128)(2,1)S(1)}, u32[]{:S(2)}, u32[]{:S(2)}) collective-permute-start(bf16[8,128,512]{2,1,0:T(8,128)(2,1)S(1)} %all_to_all.25.own), channel_id=1, source_target_pairs={{0,8},{8,0},{1,9},{9,1},{2,10},{10,2},{3,11},{11,3},{4,12},{12,4},... | collective-permute-start | bytes 3145736 | tf_op jit(solution)/shard_map/ppermute | solution.py:336

commit v7 on v6

--- a/solution.py
+++ b/solution.py
@@ -117,7 +117,7 @@
 
 
 def combine_kernel(
-    keeps, got, more, first, out, data, extra, meta, places, table, total, sems, meta_sem, table_sem, extra_sem
+    keeps, got, more, first, second, out, data, extra, meta, places, table, total, sems, meta_sem, table_sem, extra_sem
 ):
     head = pltpu.make_async_copy(got.at[:, pl.ds(BODY, META)], meta, meta_sem)
     head.start()
@@ -179,11 +179,11 @@
     lax.fori_loop(0, SIDE // 2, write, 0)
 
 
-def combine(keeps, got, more, first):
+def combine(keeps, got, more, first, second):
     return pl.pallas_call(
         functools.partial(combine_kernel, keeps),
         out_shape=jax.ShapeDtypeStruct((SIDE // 2, 2, TILE, SIDE * TILE // 2), jnp.bfloat16),
-        in_specs=[pl.BlockSpec(memory_space=pl.ANY)] * 3,
+        in_specs=[pl.BlockSpec(memory_space=pl.ANY)] * 4,
         out_specs=pl.BlockSpec(memory_space=pltpu.VMEM),
         scratch_shapes=[
             pltpu.VMEM((SIDE, BODY, TILE), jnp.bfloat16),
@@ -202,7 +202,7 @@
             flops=2 * MIB, bytes_accessed=4 * MIB, transcendentals=0
         ),
         name="combine",
-    )(got, more, first)
+    )(got, more, first, second)
 
 
 def spread_kernel(parts, far, out):
@@ -235,7 +235,8 @@
 
     def slot(block):
         distance = (block - column + SIDE) % SIDE
-        return jnp.where(distance == 7, 3, jnp.where(distance < 3, distance, distance + 1))
+        late = jnp.where(distance < 6, distance + 2, 10 - distance)
+        return jnp.where(distance < 3, distance, late)
 
     @pl.when(pl.program_id(0) == 0)
     def _():
@@ -248,7 +249,7 @@
                 ham[pl.ds(pl.multiple_of(theirs, TILE), TILE)] = other[l * 4 + j]
 
     parts = (near, near_late, far, far_late)
-    rows = jnp.concatenate([part[c] for part in parts for c in range(SIDE // 2)], axis=1)
+    rows = jnp.concatenate([part[c] for part in parts for c in range(part.shape[0])], axis=1)
     total = jnp.dot(rows, ham[...], preferred_element_type=jnp.float32)
     out[...] = total.astype(jnp.bfloat16)
 
@@ -257,13 +258,14 @@
     rows = near.shape[1]
     step = 256
     width = own.shape[2]
-    block = pl.BlockSpec((SIDE // 2, step, TILE), lambda i: (0, i, 0))
+    block = pl.BlockSpec((near.shape[0], step, TILE), lambda i: (0, i, 0))
+    late = pl.BlockSpec((near_late.shape[0], step, TILE), lambda i: (0, i, 0))
     whole = pl.BlockSpec(own.shape, lambda i: (0, 0, 0))
     return pl.pallas_call(
         product_kernel,
         out_shape=jax.ShapeDtypeStruct((rows, width), jnp.bfloat16),
         grid=(rows // step,),
-        in_specs=[block, block, block, block, whole, whole],
+        in_specs=[block, late, block, late, whole, whole],
         out_specs=pl.BlockSpec((step, width), lambda i: (i, 0)),
         scratch_shapes=[pltpu.VMEM((2 * SIDE * TILE, width), jnp.bfloat16)],
         compiler_params=pltpu.CompilerParams(vmem_limit_bytes=SMALL_MIB * MIB),
@@ -317,19 +319,19 @@
     one, last, two, sixth = (ahead(sparse, distance) for distance in (1, -1, 2, -2))
     three, fifth, four = ahead(two, 1), ahead(sixth, -1), ahead(two, 2)
     swap = [(0, 1), (1, 0)]
-    near = jnp.stack([sparse, one, two, last])
+    near = jnp.stack([sparse, one, two, last, sixth])
     far = lax.ppermute(near, "lq", swap)
-    near_late = jnp.stack([three, four, fifth, sixth])
+    near_late = jnp.stack([three, four, fifth])
     far_late = lax.ppermute(near_late, "lq", swap)
 
     anyone = jnp.max(got[:, BODY, FLAG].astype(jnp.float32)) > 0
     more = lax.cond(anyone, lambda v: exchange(v, ("rx", "rc")), lambda v: v, rest)
-    send = combine(False, got, more, near_late)
+    send = combine(False, got, more, three, fifth)
     count = SIDE
     even = [(c, c ^ 1) for c in range(count)]
     odd = [(count + c, count + (c + (1 if c % 2 else -1)) % count) for c in range(count)]
     taken = lax.ppermute(send, ("rc", "ch", "cl"), even + odd)
-    keep = combine(True, got, more, far)
+    keep = combine(True, got, more, far, near_late)
     parts = exchange(keep + taken, "ch")
 
     own = exchange(spread(parts, far_late), ("lq", "rx"))

time: 182 us -> 191 us (1.049)
  blocking collectives: 49.7 us -> 55.7 us
  local copies, waits for them, and re-layouts: 1.24 us -> 5.58 us
  starting transfers between devices: 60.1 us -> 56.3 us
  waiting for transfers between devices: 44.2 us -> 46.7 us
    ppermute x7, waiting for transfers between devices: 10.1 us -> 28.2 us  [ahead(): lax.ppermute(block, ('ch', 'cl'), [(c, (c - distance) % SIDE) for c in ra...]
    ppermute x1, waiting for transfers between devices: 8.3 us -> 0.01 us  [body(): taken = lax.ppermute(send, ('rc', 'ch', 'cl'), even + odd)]
    ppermute x1, waiting for transfers between devices: 23 us -> 15.8 us  [body(): far_late = lax.ppermute(near_late, 'lq', swap)]
    all_to_all x2, blocking collectives: 49.7 us -> 55.7 us  [exchange(): return lax.all_to_all(values, axes, split_axis=0, concat_axis=0, tiled=True)]
    ppermute x1, starting transfers between devices: 5.77 us -> 1.91 us  [body(): other = lax.ppermute(own, 'rc', swap)]
    unnamed x10 -> x14, local copies, waits for them, and re-layouts: 1.24 us -> 3.91 us
    ppermute x1, starting transfers between devices: 3.2 us -> 5.26 us  [body(): taken = lax.ppermute(send, ('rc', 'ch', 'cl'), even + odd)]
  transfers between devices with their start and end apart: 13 -> 13, of which waited for: 6 -> 6; matrix products, arithmetic and copies ran while one was open for 2% -> 4% of each run, Pallas kernels for 5% -> 5%
where the time goes in v7:
time: 191 us; the launch traced here: 188 us
  starting transfers between devices  56.3 us (29%)
  blocking collectives  55.7 us (29%)
  waiting for transfers between devices  46.7 us (24%)
  Pallas kernels  20.3 us (11%)
  local copies, waits for them, and re-layouts  5.58 us (3%)
  other arithmetic  3.02 us (2%)
    all_to_all x2, blocking collectives, exchange(): return lax.all_to_all(values, axes, split_axis=0, concat_axis=0, tiled=True)  55.7 us
    ppermute x7, waiting for transfers between devices, ahead(): lax.ppermute(block, ('ch', 'cl'), [(c, (c - distance) % SIDE) for c in ra...  28.2 us
    ppermute x7, starting transfers between devices, ahead(): lax.ppermute(block, ('ch', 'cl'), [(c, (c - distance) % SIDE) for c in ra...  28 us
    all_to_all x2, starting transfers between devices, exchange(): return lax.all_to_all(values, axes, split_axis=0, concat_axis=0, tiled=True)  16 us
    ppermute x1, waiting for transfers between devices, body(): far_late = lax.ppermute(near_late, 'lq', swap)  15.8 us
    pallas_call x2, Pallas kernels, combine(): pl.pallas_call(functools.partial(combine_kernel, keeps), out_shape=jax.Sh...  9.17 us
    ppermute x1, starting transfers between devices, body(): taken = lax.ppermute(send, ('rc', 'ch', 'cl'), even + odd)  5.26 us
    pallas_call x1, Pallas kernels, product_of(): pl.pallas_call(product_kernel, out_shape=jax.ShapeDtypeStruct((rows, widt...  4.64 us
  transfers between devices with their start and end apart: 13, of which 6 were waited for; matrix products, arithmetic and copies ran while one was open for 4% of the time, Pallas kernels for 5%

profile of v7, /device:TPU:1, one launch (start us, length us, event | category | flops | bytes accessed | tf_op | source)
XLA Modules:
  0.0 188.4 jit_solution(18182580680776243988)
XLA Ops:
  0.0 4.4 %pack.1 = (bf16[8,1552,128]{2,1,0:T(8,128)(2,1)}, bf16[8,512,128]{2,1,0:T(8,128)(2,1)}, bf16[1024,128]{1,0:T(8,128)(2,1)}) custom-call(s32[64]{0:T(128)} %bitcast.18, s32[64]{0:T(128)} %slots.1, s32[64,64]{1,0:T(8,128)} %pattern.3, bf16[64,128,128]{2,1,0:T(8,128)(2,1)} %contributions.1, bf16[1024,128]{1,0:T(8,128)(2,1)} %density.1), custom_call_target="tpu_custom_call" | custom-call | bytes 7340032 | tf_op jit(solution)/shard_map/pack/pallas_call | solution.py:86
  4.4 10.6 %all-to-all-start.1 = ((bf16[8,1552,128]{2,1,0:T(8,128)(2,1)}), bf16[8,1552,128]{2,1,0:T(8,128)(2,1)S(1)}, u32[]{:S(2)}, u32[]{:S(2)}) async-start(bf16[8,1552,128]{2,1,0:T(8,128)(2,1)} %get-tuple-element.14), calls=%async_computation.1 | async-start | bytes 6356992 | tf_op jit(solution)/shard_map/all_to_all | solution.py:307
  15.0 6.0 %collective-permute-start = (bf16[1024,128]{1,0:T(8,128)(2,1)S(1)}, bf16[1024,128]{1,0:T(8,128)(2,1)S(1)}, u32[]{:S(2)}, u32[]{:S(2)}) collective-permute-start(bf16[1024,128]{1,0:T(8,128)(2,1)S(1)} %copy-done.5), channel_id=1, source_target_pairs={{0,7},{1,0},{2,1},{3,2},{4,3},{5,4},{6,5},{7,6},{8,15},{9,8},{10,9... | collective-permute-start | bytes 786440 | tf_op jit(solution)/shard_map/ppermute | solution.py:315
  21.0 1.9 %collective-permute-start.3 = (bf16[1024,128]{1,0:T(8,128)(2,1)S(1)}, bf16[1024,128]{1,0:T(8,128)(2,1)}, u32[]{:S(2)}, u32[]{:S(2)}) collective-permute-start(bf16[1024,128]{1,0:T(8,128)(2,1)S(1)} %copy-done.5), channel_id=1, source_target_pairs={{0,2},{1,3},{2,4},{3,5},{4,6},{5,7},{6,0},{7,1},{8,10},{9,11},{10,... | collective-permute-start | bytes 786440 | tf_op jit(solution)/shard_map/ppermute | solution.py:315
  23.0 1.9 %collective-permute-start.2 = (bf16[1024,128]{1,0:T(8,128)(2,1)S(1)}, bf16[1024,128]{1,0:T(8,128)(2,1)S(1)}, u32[]{:S(2)}, u32[]{:S(2)}) collective-permute-start(bf16[1024,128]{1,0:T(8,128)(2,1)S(1)} %copy-done.5), channel_id=1, source_target_pairs={{0,1},{1,2},{2,3},{3,4},{4,5},{5,6},{6,7},{7,0},{8,9},{9,10},{10,1... | collective-permute-start | bytes 786440 | tf_op jit(solution)/shard_map/ppermute | solution.py:315
  24.9 5.5 %collective-permute-start.1 = (bf16[1024,128]{1,0:T(8,128)(2,1)S(1)}, bf16[1024,128]{1,0:T(8,128)(2,1)}, u32[]{:S(2)}, u32[]{:S(2)}) collective-permute-start(bf16[1024,128]{1,0:T(8,128)(2,1)S(1)} %copy-done.5), channel_id=1, source_target_pairs={{0,6},{1,7},{2,0},{3,1},{4,2},{5,3},{6,4},{7,5},{8,14},{9,15},{10,... | collective-permute-start | bytes 786440 | tf_op jit(solution)/shard_map/ppermute | solution.py:315
  30.4 0.7 bitcast_dynamic-update-slice_fusion.4
  31.1 0.7 bitcast_dynamic-update-slice_fusion.3
  31.9 8.8 %collective-permute-done.1 = bf16[1024,128]{1,0:T(8,128)(2,1)} collective-permute-done((bf16[1024,128]{1,0:T(8,128)(2,1)S(1)}, bf16[1024,128]{1,0:T(8,128)(2,1)}, u32[]{:S(2)}, u32[]{:S(2)}) %collective-permute-start.1) | collective-permute-done | bytes 262176 | tf_op jit(solution)/shard_map/ppermute | solution.py:315
  40.7 1.7 bitcast_dynamic-update-slice_fusion.2
  43.1 1.7 bitcast_dynamic-update-slice_fusion.near
  44.8 3.2 %collective-permute-start.7 = (bf16[5,1024,128]{2,1,0:T(8,128)(2,1)}, bf16[5,1024,128]{2,1,0:T(8,128)(2,1)}, u32[]{:S(2)}, u32[]{:S(2)}) collective-permute-start(bf16[5,1024,128]{2,1,0:T(8,128)(2,1)} %bitcast_dynamic-update-slice_fusion.near), channel_id=1, source_target_pairs={{0,64},{64,0},{1,65},{65,1},{2,66},{66,2},{3,67},{67,3},{4,68},{68... | collective-permute-start | bytes 3932168 | tf_op jit(solution)/shard_map/ppermute | solution.py:323
  47.9 2.3 %collective-permute-start.6 = (bf16[1024,128]{1,0:T(8,128)(2,1)}, bf16[1024,128]{1,0:T(8,128)(2,1)S(1)}, u32[]{:S(2)}, u32[]{:S(2)}) collective-permute-start(bf16[1024,128]{1,0:T(8,128)(2,1)} %collective-permute-done.3), channel_id=1, source_target_pairs={{0,1},{1,2},{2,3},{3,4},{4,5},{5,6},{6,7},{7,0},{8,9},{9,10},{10,1... | collective-permute-start | bytes 786440 | tf_op jit(solution)/shard_map/ppermute | solution.py:315
  50.3 5.2 %collective-permute-start.4 = (bf16[1024,128]{1,0:T(8,128)(2,1)}, bf16[1024,128]{1,0:T(8,128)(2,1)}, u32[]{:S(2)}, u32[]{:S(2)}) collective-permute-start(bf16[1024,128]{1,0:T(8,128)(2,1)} %collective-permute-done.1), channel_id=1, source_target_pairs={{0,7},{1,0},{2,1},{3,2},{4,3},{5,4},{6,5},{7,6},{8,15},{9,8},{10,9... | collective-permute-start | bytes 786440 | tf_op jit(solution)/shard_map/ppermute | solution.py:315
  56.8 1.7 collective-permute-done.6.second
  58.5 1.0 collective-permute-done.4.first
  59.5 4.6 %combine.3 = bf16[4,2,128,512]{3,2,1,0:T(8,128)(2,1)S(1)} custom-call(bf16[8,1552,128]{2,1,0:T(8,128)(2,1)S(1)} %all-to-all-done.1.got, bf16[8,512,128]{2,1,0:T(8,128)(2,1)} %get-tuple-element.16.more, bf16[1024,128]{1,0:T(8,128)(2,1)} %collective-permute-done.4.first, bf16[1024,128]{1,0:T(8,128)(2,1)S(1)} %collective-permute-done.6.second), custom_call_target="tpu_custom_call" | custom-call | flops 2097152 | bytes 4194304 | tf_op jit(solution)/shard_map/combine/pallas_call | solution.py:183
  64.1 5.3 %collective-permute-start.9 = (bf16[4,2,128,512]{3,2,1,0:T(8,128)(2,1)S(1)}, bf16[4,2,128,512]{3,2,1,0:T(8,128)(2,1)S(1)}, u32[]{:S(2)}, u32[]{:S(2)}) collective-permute-start(bf16[4,2,128,512]{3,2,1,0:T(8,128)(2,1)S(1)} %combine.3), channel_id=1, source_target_pairs={{0,1},{1,0},{2,3},{3,2},{4,5},{5,4},{6,7},{7,6},{8,15},{9,10},{10,... | collective-permute-start | bytes 3145736 | tf_op jit(solution)/shard_map/ppermute | solution.py:333
  69.4 5.2 %collective-permute-start.5 = (bf16[1024,128]{1,0:T(8,128)(2,1)}, bf16[1024,128]{1,0:T(8,128)(2,1)S(1)}, u32[]{:S(2)}, u32[]{:S(2)}) collective-permute-start(bf16[1024,128]{1,0:T(8,128)(2,1)} %collective-permute-done.1), channel_id=1, source_target_pairs={{0,6},{1,7},{2,0},{3,1},{4,2},{5,3},{6,4},{7,5},{8,14},{9,15},{10,... | collective-permute-start | bytes 786440 | tf_op jit(solution)/shard_map/ppermute | solution.py:315
  74.6 16.7 %collective-permute-done.5 = bf16[1024,128]{1,0:T(8,128)(2,1)S(1)} collective-permute-done((bf16[1024,128]{1,0:T(8,128)(2,1)}, bf16[1024,128]{1,0:T(8,128)(2,1)S(1)}, u32[]{:S(2)}, u32[]{:S(2)}) %collective-permute-start.5) | collective-permute-done | bytes 262176 | tf_op jit(solution)/shard_map/ppermute | solution.py:315
  91.3 1.0 pad_maximum_fusion.second.near_late
  92.3 4.5 %combine.2 = bf16[4,2,128,512]{3,2,1,0:T(8,128)(2,1)S(1)} custom-call(bf16[8,1552,128]{2,1,0:T(8,128)(2,1)S(1)} %all-to-all-done.1.got, bf16[8,512,128]{2,1,0:T(8,128)(2,1)S(1)} %copy-done.3, bf16[5,1024,128]{2,1,0:T(8,128)(2,1)} %collective-permute-done.7.first.far, bf16[3,1024,128]{2,1,0:T(8,128)(2,1)S(1)} %pad_maximum_fusion.second.near_late), custom_call_target="tpu_custom_call" | custom-call | flops 2097152 | bytes 4194304 | tf_op jit(solution)/shard_map/combine/pallas_call | solution.py:183
  96.9 1.3 add.3
  98.2 5.4 %all-to-all-start.2 = ((bf16[4,2,128,512]{3,2,1,0:T(8,128)(2,1)}), bf16[4,2,128,512]{3,2,1,0:T(8,128)(2,1)S(1)}, u32[]{:S(2)}, u32[]{:S(2)}) async-start(bf16[4,2,128,512]{3,2,1,0:T(8,128)(2,1)} %add.3), calls=%async_computation.2 | async-start | bytes 2097152 | tf_op jit(solution)/shard_map/all_to_all | solution.py:307
  103.7 1.9 %collective-permute-start.8 = (bf16[3,1024,128]{2,1,0:T(8,128)(2,1)S(1)}, bf16[3,1024,128]{2,1,0:T(8,128)(2,1)S(1)}, u32[]{:S(2)}, u32[]{:S(2)}) collective-permute-start(bf16[3,1024,128]{2,1,0:T(8,128)(2,1)S(1)} %copy-done.1), channel_id=1, source_target_pairs={{0,64},{64,0},{1,65},{65,1},{2,66},{66,2},{3,67},{67,3},{4,68},{68... | collective-permute-start | bytes 2359304 | tf_op jit(solution)/shard_map/ppermute | solution.py:325
  105.6 15.8 %collective-permute-done.8.far.far_late = bf16[3,1024,128]{2,1,0:T(8,128)(2,1)S(1)} collective-permute-done((bf16[3,1024,128]{2,1,0:T(8,128)(2,1)S(1)}, bf16[3,1024,128]{2,1,0:T(8,128)(2,1)S(1)}, u32[]{:S(2)}, u32[]{:S(2)}) %collective-permute-start.8) | collective-permute-done | bytes 786464 | tf_op jit(solution)/shard_map/ppermute | solution.py:325
  121.6 19.9 %all_to_all.25.own = bf16[8,128,512]{2,1,0:T(8,128)(2,1)S(1)} all-to-all(bf16[8,128,512]{2,1,0:T(8,128)(2,1)S(1)} %spread.1), channel_id=1, replica_groups=mesh['lg'=4,'lq'=2,'rx'=4,'rc'=2,'ch'=4,'cl'=2] {'lq','rx'}, dimensions={0} | all-to-all | bytes 2097152 | tf_op jit(solution)/shard_map/all_to_all | solution.py:307
  141.5 1.9 %collective-permute-start.10 = (bf16[8,128,512]{2,1,0:T(8,128)(2,1)S(1)}, bf16[8,128,512]{2,1,0:T(8,128)(2,1)S(1)}, u32[]{:S(2)}, u32[]{:S(2)}) collective-permute-start(bf16[8,128,512]{2,1,0:T(8,128)(2,1)S(1)} %all_to_all.25.own), channel_id=1, source_target_pairs={{0,8},{8,0},{1,9},{9,1},{2,10},{10,2},{3,11},{11,3},{4,12},{12,4},... | collective-permute-start | bytes 3145736 | tf_op jit(solution)/shard_map/ppermute | solution.py:338
  143.4 2.6 %collective-permute-done.10.other = bf16[8,128,512]{2,1,0:T(8,128)(2,1)S(1)} collective-permute-done((bf16[8,128,512]{2,1,0:T(8,128)(2,1)S(1)}, bf16[8,128,512]{2,1,0:T(8,128)(2,1)S(1)}, u32[]{:S(2)}, u32[]{:S(2)}) %collective-permute-start.10) | collective-permute-done | bytes 1048608 | tf_op jit(solution)/shard_map/ppermute | solution.py:338
  146.0 4.6 %product.1 = bf16[1024,512]{1,0:T(8,128)(2,1)S(1)} custom-call(bf16[5,1024,128]{2,1,0:T(8,128)(2,1)} %bitcast_dynamic-update-slice_fusion.near, bf16[3,1024,128]{2,1,0:T(8,128)(2,1)S(1)} %copy-done.1, bf16[5,1024,128]{2,1,0:T(8,128)(2,1)} %collective-permute-done.7.first.far, bf16[3,1024,128]{2,1,0:T(8,128)(2,1)S(1)} %collective-permute-done.8.far.far_late, ...), custom_call_target="tpu_custom_call" | custom-call | flops 2147483648 | bytes 7340032 | tf_op jit(solution)/shard_map/product/pallas_call | solution.py:264
  150.7 35.7 %all_to_all.26.terms = bf16[8,128,512]{2,1,0:T(8,128)(2,1)S(1)} all-to-all(bf16[8,128,512]{2,1,0:T(8,128)(2,1)S(1)} %bitcast.15), channel_id=1, replica_groups=mesh['lg'=4,'lq'=2,'rx'=4,'rc'=2,'ch'=4,'cl'=2] {'lg','lq'}, dimensions={0} | all-to-all | bytes 2097152 | tf_op jit(solution)/shard_map/all_to_all | solution.py:307
  186.4 1.9 %finish.1 = bf16[128,1024]{1,0:T(8,128)(2,1)} custom-call(s32[64,64]{1,0:T(8,128)S(1)} %copy-done.2, bf16[8,128,512]{2,1,0:T(8,128)(2,1)S(1)} %all_to_all.26.terms), custom_call_target="tpu_custom_call" | custom-call | flops 1048576 | bytes 2097152 | tf_op jit(solution)/shard_map/finish/pallas_call | solution.py:292
  (21 shorter events, 1.6 us)
Async XLA Ops:
  4.4 10.6 %copy-start.5 = (bf16[1024,128]{1,0:T(8,128)(2,1)S(1)}, bf16[1024,128]{1,0:T(8,128)(2,1)}, u32[]{:S(2)}) copy-start(bf16[1024,128]{1,0:T(8,128)(2,1)} %get-tuple-element.13) | copy-start | bytes 786436
  4.4 51.0 %all-to-all-start.1 = ((bf16[8,1552,128]{2,1,0:T(8,128)(2,1)}), bf16[8,1552,128]{2,1,0:T(8,128)(2,1)S(1)}, u32[]{:S(2)}, u32[]{:S(2)}) async-start(bf16[8,1552,128]{2,1,0:T(8,128)(2,1)} %get-tuple-element.14), calls=%async_computation.1 | async-start | bytes 6356992 | tf_op jit(solution)/shard_map/all_to_all | solution.py:307
  15.0 16.1 %collective-permute-start = (bf16[1024,128]{1,0:T(8,128)(2,1)S(1)}, bf16[1024,128]{1,0:T(8,128)(2,1)S(1)}, u32[]{:S(2)}, u32[]{:S(2)}) collective-permute-start(bf16[1024,128]{1,0:T(8,128)(2,1)S(1)} %copy-done.5), channel_id=1, source_target_pairs={{0,7},{1,0},{2,1},{3,2},{4,3},{5,4},{6,5},{7,6},{8,15},{9,8},{10,9... | collective-permute-start | bytes 786440 | tf_op jit(solution)/shard_map/ppermute | solution.py:315
  21.0 22.0 %collective-permute-start.3 = (bf16[1024,128]{1,0:T(8,128)(2,1)S(1)}, bf16[1024,128]{1,0:T(8,128)(2,1)}, u32[]{:S(2)}, u32[]{:S(2)}) collective-permute-start(bf16[1024,128]{1,0:T(8,128)(2,1)S(1)} %copy-done.5), channel_id=1, source_target_pairs={{0,2},{1,3},{2,4},{3,5},{4,6},{5,7},{6,0},{7,1},{8,10},{9,11},{10,... | collective-permute-start | bytes 786440 | tf_op jit(solution)/shard_map/ppermute | solution.py:315
  23.0 19.4 %collective-permute-start.2 = (bf16[1024,128]{1,0:T(8,128)(2,1)S(1)}, bf16[1024,128]{1,0:T(8,128)(2,1)S(1)}, u32[]{:S(2)}, u32[]{:S(2)}) collective-permute-start(bf16[1024,128]{1,0:T(8,128)(2,1)S(1)} %copy-done.5), channel_id=1, source_target_pairs={{0,1},{1,2},{2,3},{3,4},{4,5},{5,6},{6,7},{7,0},{8,9},{9,10},{10,1... | collective-permute-start | bytes 786440 | tf_op jit(solution)/shard_map/ppermute | solution.py:315
  24.9 15.8 %collective-permute-start.1 = (bf16[1024,128]{1,0:T(8,128)(2,1)S(1)}, bf16[1024,128]{1,0:T(8,128)(2,1)}, u32[]{:S(2)}, u32[]{:S(2)}) collective-permute-start(bf16[1024,128]{1,0:T(8,128)(2,1)S(1)} %copy-done.5), channel_id=1, source_target_pairs={{0,6},{1,7},{2,0},{3,1},{4,2},{5,3},{6,4},{7,5},{8,14},{9,15},{10,... | collective-permute-start | bytes 786440 | tf_op jit(solution)/shard_map/ppermute | solution.py:315
  44.8 47.6 %collective-permute-start.7 = (bf16[5,1024,128]{2,1,0:T(8,128)(2,1)}, bf16[5,1024,128]{2,1,0:T(8,128)(2,1)}, u32[]{:S(2)}, u32[]{:S(2)}) collective-permute-start(bf16[5,1024,128]{2,1,0:T(8,128)(2,1)} %bitcast_dynamic-update-slice_fusion.near), channel_id=1, source_target_pairs={{0,64},{64,0},{1,65},{65,1},{2,66},{66,2},{3,67},{67,3},{4,68},{68... | collective-permute-start | bytes 3932168 | tf_op jit(solution)/shard_map/ppermute | solution.py:323
  47.9 10.6 %collective-permute-start.6 = (bf16[1024,128]{1,0:T(8,128)(2,1)}, bf16[1024,128]{1,0:T(8,128)(2,1)S(1)}, u32[]{:S(2)}, u32[]{:S(2)}) collective-permute-start(bf16[1024,128]{1,0:T(8,128)(2,1)} %collective-permute-done.3), channel_id=1, source_target_pairs={{0,1},{1,2},{2,3},{3,4},{4,5},{5,6},{6,7},{7,0},{8,9},{9,10},{10,1... | collective-permute-start | bytes 786440 | tf_op jit(solution)/shard_map/ppermute | solution.py:315
  50.3 9.2 %collective-permute-start.4 = (bf16[1024,128]{1,0:T(8,128)(2,1)}, bf16[1024,128]{1,0:T(8,128)(2,1)}, u32[]{:S(2)}, u32[]{:S(2)}) collective-permute-start(bf16[1024,128]{1,0:T(8,128)(2,1)} %collective-permute-done.1), channel_id=1, source_target_pairs={{0,7},{1,0},{2,1},{3,2},{4,3},{5,4},{6,5},{7,6},{8,15},{9,8},{10,9... | collective-permute-start | bytes 786440 | tf_op jit(solution)/shard_map/ppermute | solution.py:315
  64.1 28.2 %copy-start.3 = (bf16[8,512,128]{2,1,0:T(8,128)(2,1)S(1)}, bf16[8,512,128]{2,1,0:T(8,128)(2,1)}, u32[]{:S(2)}) copy-start(bf16[8,512,128]{2,1,0:T(8,128)(2,1)} %get-tuple-element.16.more) | copy-start | bytes 3145732
  64.1 32.8 %collective-permute-start.9 = (bf16[4,2,128,512]{3,2,1,0:T(8,128)(2,1)S(1)}, bf16[4,2,128,512]{3,2,1,0:T(8,128)(2,1)S(1)}, u32[]{:S(2)}, u32[]{:S(2)}) collective-permute-start(bf16[4,2,128,512]{3,2,1,0:T(8,128)(2,1)S(1)} %combine.3), channel_id=1, source_target_pairs={{0,1},{1,0},{2,3},{3,2},{4,5},{5,4},{6,7},{7,6},{8,15},{9,10},{10,... | collective-permute-start | bytes 3145736 | tf_op jit(solution)/shard_map/ppermute | solution.py:333
  69.4 21.9 %collective-permute-start.5 = (bf16[1024,128]{1,0:T(8,128)(2,1)}, bf16[1024,128]{1,0:T(8,128)(2,1)S(1)}, u32[]{:S(2)}, u32[]{:S(2)}) collective-permute-start(bf16[1024,128]{1,0:T(8,128)(2,1)} %collective-permute-done.1), channel_id=1, source_target_pairs={{0,6},{1,7},{2,0},{3,1},{4,2},{5,3},{6,4},{7,5},{8,14},{9,15},{10,... | collective-permute-start | bytes 786440 | tf_op jit(solution)/shard_map/ppermute | solution.py:315
  92.3 4.6 %copy-start = (bf16[3,1024,128]{2,1,0:T(8,128)(2,1)}, bf16[3,1024,128]{2,1,0:T(8,128)(2,1)S(1)}, u32[]{:S(2)}) copy-start(bf16[3,1024,128]{2,1,0:T(8,128)(2,1)S(1)} %pad_maximum_fusion.second.near_late) | copy-start | bytes 2359300
  98.2 5.4 %copy-start.1 = (bf16[3,1024,128]{2,1,0:T(8,128)(2,1)S(1)}, bf16[3,1024,128]{2,1,0:T(8,128)(2,1)}, u32[]{:S(2)}) copy-start(bf16[3,1024,128]{2,1,0:T(8,128)(2,1)} %copy-done) | copy-start | bytes 2359300
  98.2 23.2 %all-to-all-start.2 = ((bf16[4,2,128,512]{3,2,1,0:T(8,128)(2,1)}), bf16[4,2,128,512]{3,2,1,0:T(8,128)(2,1)S(1)}, u32[]{:S(2)}, u32[]{:S(2)}) async-start(bf16[4,2,128,512]{3,2,1,0:T(8,128)(2,1)} %add.3), calls=%async_computation.2 | async-start | bytes 2097152 | tf_op jit(solution)/shard_map/all_to_all | solution.py:307
  103.7 17.7 %collective-permute-start.8 = (bf16[3,1024,128]{2,1,0:T(8,128)(2,1)S(1)}, bf16[3,1024,128]{2,1,0:T(8,128)(2,1)S(1)}, u32[]{:S(2)}, u32[]{:S(2)}) collective-permute-start(bf16[3,1024,128]{2,1,0:T(8,128)(2,1)S(1)} %copy-done.1), channel_id=1, source_target_pairs={{0,64},{64,0},{1,65},{65,1},{2,66},{66,2},{3,67},{67,3},{4,68},{68... | collective-permute-start | bytes 2359304 | tf_op jit(solution)/shard_map/ppermute | solution.py:325
  141.5 4.5 %collective-permute-start.10 = (bf16[8,128,512]{2,1,0:T(8,128)(2,1)S(1)}, bf16[8,128,512]{2,1,0:T(8,128)(2,1)S(1)}, u32[]{:S(2)}, u32[]{:S(2)}) collective-permute-start(bf16[8,128,512]{2,1,0:T(8,128)(2,1)S(1)} %all_to_all.25.own), channel_id=1, source_target_pairs={{0,8},{8,0},{1,9},{9,1},{2,10},{10,2},{3,11},{11,3},{4,12},{12,4},... | collective-permute-start | bytes 3145736 | tf_op jit(solution)/shard_map/ppermute | solution.py:338
  150.7 35.7 %copy-start.2 = (s32[64,64]{1,0:T(8,128)S(1)}, s32[64,64]{1,0:T(8,128)}, u32[]{:S(2)}) copy-start(s32[64,64]{1,0:T(8,128)} %pattern.3) | copy-start | bytes 49156

commit v8 on v7

--- a/solution.py
+++ b/solution.py
@@ -117,7 +117,7 @@
 
 
 def combine_kernel(
-    keeps, got, more, first, second, out, data, extra, meta, places, table, total, sems, meta_sem, table_sem, extra_sem
+    keeps, got, more, first, second, third, out, data, extra, meta, places, table, total, sems, meta_sem, table_sem, extra_sem
 ):
     head = pltpu.make_async_copy(got.at[:, pl.ds(BODY, META)], meta, meta_sem)
     head.start()
@@ -179,11 +179,11 @@
     lax.fori_loop(0, SIDE // 2, write, 0)
 
 
-def combine(keeps, got, more, first, second):
+def combine(keeps, got, more, *waits):
     return pl.pallas_call(
         functools.partial(combine_kernel, keeps),
         out_shape=jax.ShapeDtypeStruct((SIDE // 2, 2, TILE, SIDE * TILE // 2), jnp.bfloat16),
-        in_specs=[pl.BlockSpec(memory_space=pl.ANY)] * 4,
+        in_specs=[pl.BlockSpec(memory_space=pl.ANY)] * 5,
         out_specs=pl.BlockSpec(memory_space=pltpu.VMEM),
         scratch_shapes=[
             pltpu.VMEM((SIDE, BODY, TILE), jnp.bfloat16),
@@ -202,7 +202,23 @@
             flops=2 * MIB, bytes_accessed=4 * MIB, transcendentals=0
         ),
         name="combine",
-    )(got, more, first, second)
+    )(got, more, *waits)
+
+
+def add_kernel(keep, taken, wait, out):
+    out[...] = keep[...] + taken[...]
+
+
+def add(keep, taken, wait):
+    return pl.pallas_call(
+        add_kernel,
+        out_shape=jax.ShapeDtypeStruct(keep.shape, keep.dtype),
+        in_specs=[pl.BlockSpec(memory_space=pltpu.VMEM)] * 2 + [pl.BlockSpec(memory_space=pl.ANY)],
+        out_specs=pl.BlockSpec(memory_space=pltpu.VMEM),
+        compiler_params=pltpu.CompilerParams(vmem_limit_bytes=SMALL_MIB * MIB),
+        cost_estimate=pl.CostEstimate(flops=MIB, bytes_accessed=3 * MIB, transcendentals=0),
+        name="add",
+    )(keep, taken, wait)
 
 
 def spread_kernel(parts, far, out):
@@ -228,14 +244,15 @@
     )(parts, far)
 
 
-def product_kernel(near, near_late, far, far_late, own, other, out, ham):
+def product_kernel(*refs):
+    *parts, own, other, out, ham = refs
     half = SIDE * TILE
     core, layer = lax.axis_index("rc"), lax.axis_index("lq")
     column = lax.axis_index(("ch", "cl"))
 
     def slot(block):
         distance = (block - column + SIDE) % SIDE
-        late = jnp.where(distance < 6, distance + 2, 10 - distance)
+        late = jnp.where(distance < 5, distance + 3, 10 - distance)
         return jnp.where(distance < 3, distance, late)
 
     @pl.when(pl.program_id(0) == 0)
@@ -248,24 +265,22 @@
                 ham[pl.ds(pl.multiple_of(mine, TILE), TILE)] = own[l * 4 + j]
                 ham[pl.ds(pl.multiple_of(theirs, TILE), TILE)] = other[l * 4 + j]
 
-    parts = (near, near_late, far, far_late)
     rows = jnp.concatenate([part[c] for part in parts for c in range(part.shape[0])], axis=1)
     total = jnp.dot(rows, ham[...], preferred_element_type=jnp.float32)
     out[...] = total.astype(jnp.bfloat16)
 
 
-def product_of(near, near_late, far, far_late, own, other):
-    rows = near.shape[1]
+def product_of(parts, own, other):
+    rows = parts[0].shape[1]
     step = 256
     width = own.shape[2]
-    block = pl.BlockSpec((near.shape[0], step, TILE), lambda i: (0, i, 0))
-    late = pl.BlockSpec((near_late.shape[0], step, TILE), lambda i: (0, i, 0))
+    blocks = [pl.BlockSpec((p.shape[0], step, TILE), lambda i: (0, i, 0)) for p in parts]
     whole = pl.BlockSpec(own.shape, lambda i: (0, 0, 0))
     return pl.pallas_call(
         product_kernel,
         out_shape=jax.ShapeDtypeStruct((rows, width), jnp.bfloat16),
         grid=(rows // step,),
-        in_specs=[block, late, block, late, whole, whole],
+        in_specs=[*blocks, whole, whole],
         out_specs=pl.BlockSpec((step, width), lambda i: (i, 0)),
         scratch_shapes=[pltpu.VMEM((2 * SIDE * TILE, width), jnp.bfloat16)],
         compiler_params=pltpu.CompilerParams(vmem_limit_bytes=SMALL_MIB * MIB),
@@ -273,7 +288,7 @@
             flops=4 * rows * rows * width, bytes_accessed=7 * MIB, transcendentals=0
         ),
         name="product",
-    )(near, near_late, far, far_late, own, other)
+    )(*parts, own, other)
 
 
 def finish_kernel(pattern, terms, out):
@@ -319,24 +334,26 @@
     one, last, two, sixth = (ahead(sparse, distance) for distance in (1, -1, 2, -2))
     three, fifth, four = ahead(two, 1), ahead(sixth, -1), ahead(two, 2)
     swap = [(0, 1), (1, 0)]
-    near = jnp.stack([sparse, one, two, last, sixth])
+    near = jnp.stack([sparse, one, two, last])
     far = lax.ppermute(near, "lq", swap)
-    near_late = jnp.stack([three, four, fifth])
+    near_mid = jnp.stack([sixth, fifth])
+    far_mid = lax.ppermute(near_mid, "lq", swap)
+    near_late = jnp.stack([three, four])
     far_late = lax.ppermute(near_late, "lq", swap)
 
     anyone = jnp.max(got[:, BODY, FLAG].astype(jnp.float32)) > 0
     more = lax.cond(anyone, lambda v: exchange(v, ("rx", "rc")), lambda v: v, rest)
-    send = combine(False, got, more, three, fifth)
+    send = combine(False, got, more, three, four, fifth)
     count = SIDE
     even = [(c, c ^ 1) for c in range(count)]
     odd = [(count + c, count + (c + (1 if c % 2 else -1)) % count) for c in range(count)]
     taken = lax.ppermute(send, ("rc", "ch", "cl"), even + odd)
-    keep = combine(True, got, more, far, near_late)
-    parts = exchange(keep + taken, "ch")
+    keep = combine(True, got, more, far, near_mid, near_late)
+    parts = exchange(add(keep, taken, far_mid), "ch")
 
     own = exchange(spread(parts, far_late), ("lq", "rx"))
     other = lax.ppermute(own, "rc", swap)
-    term = product_of(near, near_late, far, far_late, own, other)
+    term = product_of((near, near_mid, near_late, far, far_mid, far_late), own, other)
     terms = exchange(term.reshape(SIDE, TILE, -1), ("lg", "lq"))
     return finish(pattern, terms)
 

time: 191 us -> 181 us (0.948)
  waiting for transfers between devices: 46.7 us -> 31.7 us
  starting transfers between devices: 56.3 us -> 61.3 us
  local copies, waits for them, and re-layouts: 5.58 us -> 0.81 us
  blocking collectives: 55.7 us -> 58 us
    ppermute x7, waiting for transfers between devices: 28.2 us -> 4.5 us  [ahead(): lax.ppermute(block, ('ch', 'cl'), [(c, (c - distance) % SIDE) for c in ra...]
    all_to_all x2, waiting for transfers between devices: 0.01 us -> 7.78 us  [exchange(): return lax.all_to_all(values, axes, split_axis=0, concat_axis=0, tiled=True)]
    ppermute x0 -> x1, waiting for transfers between devices: none -> 6.73 us  [body(): far_mid = lax.ppermute(near_mid, 'lq', swap)]
    ppermute x1, waiting for transfers between devices: 15.8 us -> 10.3 us  [body(): far_late = lax.ppermute(near_late, 'lq', swap)]
    ppermute x1, starting transfers between devices: 1.91 us -> 5.68 us  [body(): other = lax.ppermute(own, 'rc', swap)]
    another operation x1 -> x3, other arithmetic: 1.04 us -> 4.21 us  [the longest x1 2.13 us: body(): near = jnp.stack([sparse, one, two, last])]
    unnamed x14 -> x16, local copies, waits for them, and re-layouts: 3.91 us -> 0.81 us
    ppermute x0 -> x1, starting transfers between devices: none -> 3.09 us  [body(): far_mid = lax.ppermute(near_mid, 'lq', swap)]
  transfers between devices with their start and end apart: 13 -> 14, of which waited for: 6 -> 7; matrix products, arithmetic and copies ran while one was open for 4% -> 3% of each run, Pallas kernels for 5% -> 5%
where the time goes in v8:
time: 181 us; the launch traced here: 180 us
  starting transfers between devices  61.3 us (34%)
  blocking collectives  58 us (32%)
  waiting for transfers between devices  31.7 us (18%)
  Pallas kernels  22 us (12%)
  other arithmetic  4.89 us (3%)
    all_to_all x2, blocking collectives, exchange(): return lax.all_to_all(values, axes, split_axis=0, concat_axis=0, tiled=True)  58 us
    ppermute x7, starting transfers between devices, ahead(): lax.ppermute(block, ('ch', 'cl'), [(c, (c - distance) % SIDE) for c in ra...  29 us
    all_to_all x2, starting transfers between devices, exchange(): return lax.all_to_all(values, axes, split_axis=0, concat_axis=0, tiled=True)  14.3 us
    ppermute x1, waiting for transfers between devices, body(): far_late = lax.ppermute(near_late, 'lq', swap)  10.3 us
    pallas_call x2, Pallas kernels, combine(): pl.pallas_call(functools.partial(combine_kernel, keeps), out_shape=jax.Sh...  9.82 us
    all_to_all x2, waiting for transfers between devices, exchange(): return lax.all_to_all(values, axes, split_axis=0, concat_axis=0, tiled=True)  7.78 us
    ppermute x1, waiting for transfers between devices, body(): far_mid = lax.ppermute(near_mid, 'lq', swap)  6.73 us
    ppermute x1, starting transfers between devices, body(): other = lax.ppermute(own, 'rc', swap)  5.68 us
  transfers between devices with their start and end apart: 14, of which 7 were waited for; matrix products, arithmetic and copies ran while one was open for 3% of the time, Pallas kernels for 5%

profile of v8, /device:TPU:1, one launch (start us, length us, event | category | flops | bytes accessed | tf_op | source)
XLA Modules:
  0.0 179.6 jit_solution(15363994814616591894)
XLA Ops:
  0.0 4.4 %pack.1 = (bf16[8,1552,128]{2,1,0:T(8,128)(2,1)}, bf16[8,512,128]{2,1,0:T(8,128)(2,1)}, bf16[1024,128]{1,0:T(8,128)(2,1)}) custom-call(s32[64]{0:T(128)} %bitcast.14, s32[64]{0:T(128)} %slots.1, s32[64,64]{1,0:T(8,128)} %pattern.3, bf16[64,128,128]{2,1,0:T(8,128)(2,1)} %contributions.1, bf16[1024,128]{1,0:T(8,128)(2,1)} %density.1), custom_call_target="tpu_custom_call" | custom-call | bytes 7340032 | tf_op jit(solution)/shard_map/pack/pallas_call | solution.py:86
  4.4 10.4 %all-to-all-start.1 = ((bf16[8,1552,128]{2,1,0:T(8,128)(2,1)}), bf16[8,1552,128]{2,1,0:T(8,128)(2,1)S(1)}, u32[]{:S(2)}, u32[]{:S(2)}) async-start(bf16[8,1552,128]{2,1,0:T(8,128)(2,1)} %get-tuple-element.14), calls=%async_computation.1 | async-start | bytes 6356992 | tf_op jit(solution)/shard_map/all_to_all | solution.py:322
  14.9 1.9 %collective-permute-start.3 = (bf16[1024,128]{1,0:T(8,128)(2,1)}, bf16[1024,128]{1,0:T(8,128)(2,1)}, u32[]{:S(2)}, u32[]{:S(2)}) collective-permute-start(bf16[1024,128]{1,0:T(8,128)(2,1)} %get-tuple-element.13), channel_id=1, source_target_pairs={{0,2},{1,3},{2,4},{3,5},{4,6},{5,7},{6,0},{7,1},{8,10},{9,11},{10,... | collective-permute-start | bytes 786440 | tf_op jit(solution)/shard_map/ppermute | solution.py:330
  16.8 6.0 %collective-permute-start.1 = (bf16[1024,128]{1,0:T(8,128)(2,1)}, bf16[1024,128]{1,0:T(8,128)(2,1)}, u32[]{:S(2)}, u32[]{:S(2)}) collective-permute-start(bf16[1024,128]{1,0:T(8,128)(2,1)} %get-tuple-element.13), channel_id=1, source_target_pairs={{0,6},{1,7},{2,0},{3,1},{4,2},{5,3},{6,4},{7,5},{8,14},{9,15},{10,... | collective-permute-start | bytes 786440 | tf_op jit(solution)/shard_map/ppermute | solution.py:330
  22.8 3.1 %collective-permute-start.2 = (bf16[1024,128]{1,0:T(8,128)(2,1)}, bf16[1024,128]{1,0:T(8,128)(2,1)S(1)}, u32[]{:S(2)}, u32[]{:S(2)}) collective-permute-start(bf16[1024,128]{1,0:T(8,128)(2,1)} %get-tuple-element.13), channel_id=1, source_target_pairs={{0,1},{1,2},{2,3},{3,4},{4,5},{5,6},{6,7},{7,0},{8,9},{9,10},{10,1... | collective-permute-start | bytes 786440 | tf_op jit(solution)/shard_map/ppermute | solution.py:330
  25.9 3.4 %collective-permute-start = (bf16[1024,128]{1,0:T(8,128)(2,1)}, bf16[1024,128]{1,0:T(8,128)(2,1)S(1)}, u32[]{:S(2)}, u32[]{:S(2)}) collective-permute-start(bf16[1024,128]{1,0:T(8,128)(2,1)} %get-tuple-element.13), channel_id=1, source_target_pairs={{0,7},{1,0},{2,1},{3,2},{4,3},{5,4},{6,5},{7,6},{8,15},{9,8},{10,9... | collective-permute-start | bytes 786440 | tf_op jit(solution)/shard_map/ppermute | solution.py:330
  29.3 7.4 %collective-permute-start.4 = (bf16[1024,128]{1,0:T(8,128)(2,1)}, bf16[1024,128]{1,0:T(8,128)(2,1)S(1)}, u32[]{:S(2)}, u32[]{:S(2)}) collective-permute-start(bf16[1024,128]{1,0:T(8,128)(2,1)} %collective-permute-done.3), channel_id=1, source_target_pairs={{0,1},{1,2},{2,3},{3,4},{4,5},{5,6},{6,7},{7,0},{8,9},{9,10},{10,1... | collective-permute-start | bytes 786440 | tf_op jit(solution)/shard_map/ppermute | solution.py:330
  36.8 3.4 %collective-permute-start.6 = (bf16[1024,128]{1,0:T(8,128)(2,1)}, bf16[1024,128]{1,0:T(8,128)(2,1)}, u32[]{:S(2)}, u32[]{:S(2)}) collective-permute-start(bf16[1024,128]{1,0:T(8,128)(2,1)} %collective-permute-done.1), channel_id=1, source_target_pairs={{0,6},{1,7},{2,0},{3,1},{4,2},{5,3},{6,4},{7,5},{8,14},{9,15},{10,... | collective-permute-start | bytes 786440 | tf_op jit(solution)/shard_map/ppermute | solution.py:330
  40.2 3.8 %collective-permute-start.5 = (bf16[1024,128]{1,0:T(8,128)(2,1)}, bf16[1024,128]{1,0:T(8,128)(2,1)}, u32[]{:S(2)}, u32[]{:S(2)}) collective-permute-start(bf16[1024,128]{1,0:T(8,128)(2,1)} %collective-permute-done.1), channel_id=1, source_target_pairs={{0,7},{1,0},{2,1},{3,2},{4,3},{5,4},{6,5},{7,6},{8,15},{9,8},{10,9... | collective-permute-start | bytes 786440 | tf_op jit(solution)/shard_map/ppermute | solution.py:330
  44.0 2.1 %pad_maximum_fusion.refs_0_ = bf16[4,1024,128]{2,1,0:T(8,128)(2,1)} fusion(bf16[1,1024,128]{2,1,0:T(8,128)(2,1)S(1)} %bitcast.12, bf16[1,1024,128]{2,1,0:T(8,128)(2,1)} %bitcast.3, bf16[1,1024,128]{2,1,0:T(8,128)(2,1)S(1)} %bitcast.13, bf16[1,1024,128]{2,1,0:T(8,128)(2,1)} %bitcast.1), kind=kLoop, calls=%fused_computation | loop fusion | flops 1572864 | bytes 2097152 | tf_op jit(solution)/shard_map/stack | solution.py:337
  46.1 3.2 %collective-permute-start.7 = (bf16[4,1024,128]{2,1,0:T(8,128)(2,1)}, bf16[4,1024,128]{2,1,0:T(8,128)(2,1)}, u32[]{:S(2)}, u32[]{:S(2)}) collective-permute-start(bf16[4,1024,128]{2,1,0:T(8,128)(2,1)} %pad_maximum_fusion.refs_0_), channel_id=1, source_target_pairs={{0,64},{64,0},{1,65},{65,1},{2,66},{66,2},{3,67},{67,3},{4,68},{68... | collective-permute-start | bytes 3145736 | tf_op jit(solution)/shard_map/ppermute | solution.py:338
  49.3 3.5 %all-to-all-done.1.got = bf16[8,1552,128]{2,1,0:T(8,128)(2,1)S(1)} async-done(((bf16[8,1552,128]{2,1,0:T(8,128)(2,1)}), bf16[8,1552,128]{2,1,0:T(8,128)(2,1)S(1)}, u32[]{:S(2)}, u32[]{:S(2)}) %all-to-all-start.1) | async-done | bytes 3178528 | tf_op jit(solution)/shard_map/all_to_all | solution.py:322
  54.2 4.5 %collective-permute-done.5.first = bf16[1024,128]{1,0:T(8,128)(2,1)} collective-permute-done((bf16[1024,128]{1,0:T(8,128)(2,1)}, bf16[1024,128]{1,0:T(8,128)(2,1)}, u32[]{:S(2)}, u32[]{:S(2)}) %collective-permute-start.5) | collective-permute-done | bytes 262176 | tf_op jit(solution)/shard_map/ppermute | solution.py:330
  58.7 5.0 %combine.3 = bf16[4,2,128,512]{3,2,1,0:T(8,128)(2,1)S(1)} custom-call(bf16[8,1552,128]{2,1,0:T(8,128)(2,1)S(1)} %all-to-all-done.1.got, bf16[8,512,128]{2,1,0:T(8,128)(2,1)} %get-tuple-element.16.more, bf16[1024,128]{1,0:T(8,128)(2,1)} %collective-permute-done.5.first, bf16[1024,128]{1,0:T(8,128)(2,1)} %collective-permute-done.6.second, ...), custom_call_target="tpu_custom_call" | custom-call | flops 2097152 | bytes 4194304 | tf_op jit(solution)/shard_map/combine/pallas_call | solution.py:183
  63.7 2.7 %collective-permute-start.10 = (bf16[4,2,128,512]{3,2,1,0:T(8,128)(2,1)S(1)}, bf16[4,2,128,512]{3,2,1,0:T(8,128)(2,1)S(1)}, u32[]{:S(2)}, u32[]{:S(2)}) collective-permute-start(bf16[4,2,128,512]{3,2,1,0:T(8,128)(2,1)S(1)} %combine.3), channel_id=1, source_target_pairs={{0,1},{1,0},{2,3},{3,2},{4,5},{5,4},{6,7},{7,6},{8,15},{9,10},{10,... | collective-permute-start | bytes 3145736 | tf_op jit(solution)/shard_map/ppermute | solution.py:350
  66.4 1.0 pad_maximum_fusion.1.second.refs_1_
  67.4 3.1 %collective-permute-start.8 = (bf16[2,1024,128]{2,1,0:T(8,128)(2,1)S(1)}, bf16[2,1024,128]{2,1,0:T(8,128)(2,1)S(1)}, u32[]{:S(2)}, u32[]{:S(2)}) collective-permute-start(bf16[2,1024,128]{2,1,0:T(8,128)(2,1)S(1)} %pad_maximum_fusion.1.second.refs_1_), channel_id=1, source_target_pairs={{0,64},{64,0},{1,65},{65,1},{2,66},{66,2},{3,67},{67,3},{4,68},{68... | collective-permute-start | bytes 1572872 | tf_op jit(solution)/shard_map/ppermute | solution.py:340
  70.5 1.1 pad_maximum_fusion.2.third.refs_2_
  71.7 4.8 %combine.2.keep = bf16[4,2,128,512]{3,2,1,0:T(8,128)(2,1)S(1)} custom-call(bf16[8,1552,128]{2,1,0:T(8,128)(2,1)S(1)} %all-to-all-done.1.got, bf16[8,512,128]{2,1,0:T(8,128)(2,1)S(1)} %copy-done.7, bf16[4,1024,128]{2,1,0:T(8,128)(2,1)} %collective-permute-done.7.first.refs_3_, bf16[2,1024,128]{2,1,0:T(8,128)(2,1)S(1)} %pad_maximum_fusion.1.second.refs_1_, ...), custom_call_target="tpu_custom_call" | custom-call | flops 2097152 | bytes 4194304 | tf_op jit(solution)/shard_map/combine/pallas_call | solution.py:183
  76.6 6.7 %collective-permute-done.8.wait.refs_4_ = bf16[2,1024,128]{2,1,0:T(8,128)(2,1)S(1)} collective-permute-done((bf16[2,1024,128]{2,1,0:T(8,128)(2,1)S(1)}, bf16[2,1024,128]{2,1,0:T(8,128)(2,1)S(1)}, u32[]{:S(2)}, u32[]{:S(2)}) %collective-permute-start.8) | collective-permute-done | bytes 524320 | tf_op jit(solution)/shard_map/ppermute | solution.py:340
  83.3 1.1 add.1
  84.4 0.8 copy-done.4
  85.2 3.9 %all-to-all-start.2 = ((bf16[4,2,128,512]{3,2,1,0:T(8,128)(2,1)}), bf16[4,2,128,512]{3,2,1,0:T(8,128)(2,1)S(1)}, u32[]{:S(2)}, u32[]{:S(2)}) async-start(bf16[4,2,128,512]{3,2,1,0:T(8,128)(2,1)} %add.1), calls=%async_computation.2 | async-start | bytes 2097152 | tf_op jit(solution)/shard_map/all_to_all | solution.py:322
  89.1 3.3 %collective-permute-start.9 = (bf16[2,1024,128]{2,1,0:T(8,128)(2,1)S(1)}, bf16[2,1024,128]{2,1,0:T(8,128)(2,1)S(1)}, u32[]{:S(2)}, u32[]{:S(2)}) collective-permute-start(bf16[2,1024,128]{2,1,0:T(8,128)(2,1)S(1)} %copy-done.3), channel_id=1, source_target_pairs={{0,64},{64,0},{1,65},{65,1},{2,66},{66,2},{3,67},{67,3},{4,68},{68... | collective-permute-start | bytes 1572872 | tf_op jit(solution)/shard_map/ppermute | solution.py:342
  92.4 10.3 %collective-permute-done.9.far.refs_5_ = bf16[2,1024,128]{2,1,0:T(8,128)(2,1)S(1)} collective-permute-done((bf16[2,1024,128]{2,1,0:T(8,128)(2,1)S(1)}, bf16[2,1024,128]{2,1,0:T(8,128)(2,1)S(1)}, u32[]{:S(2)}, u32[]{:S(2)}) %collective-permute-start.9) | collective-permute-done | bytes 524320 | tf_op jit(solution)/shard_map/ppermute | solution.py:342
  102.7 4.3 %all-to-all-done.2.parts = bf16[4,2,128,512]{3,2,1,0:T(8,128)(2,1)S(1)} async-done(((bf16[4,2,128,512]{3,2,1,0:T(8,128)(2,1)}), bf16[4,2,128,512]{3,2,1,0:T(8,128)(2,1)S(1)}, u32[]{:S(2)}, u32[]{:S(2)}) %all-to-all-start.2) | async-done | bytes 1048608 | tf_op jit(solution)/shard_map/all_to_all | solution.py:322
  107.1 23.1 %all_to_all.25.refs_6_ = bf16[8,128,512]{2,1,0:T(8,128)(2,1)S(1)} all-to-all(bf16[8,128,512]{2,1,0:T(8,128)(2,1)S(1)} %spread.1), channel_id=1, replica_groups=mesh['lg'=4,'lq'=2,'rx'=4,'rc'=2,'ch'=4,'cl'=2] {'lq','rx'}, dimensions={0} | all-to-all | bytes 2097152 | tf_op jit(solution)/shard_map/all_to_all | solution.py:322
  130.2 5.7 %collective-permute-start.11 = (bf16[8,128,512]{2,1,0:T(8,128)(2,1)S(1)}, bf16[8,128,512]{2,1,0:T(8,128)(2,1)S(1)}, u32[]{:S(2)}, u32[]{:S(2)}) collective-permute-start(bf16[8,128,512]{2,1,0:T(8,128)(2,1)S(1)} %all_to_all.25.refs_6_), channel_id=1, source_target_pairs={{0,8},{8,0},{1,9},{9,1},{2,10},{10,2},{3,11},{11,3},{4,12},{12,4},... | collective-permute-start | bytes 3145736 | tf_op jit(solution)/shard_map/ppermute | solution.py:355
  135.9 2.3 %collective-permute-done.11.refs_7_ = bf16[8,128,512]{2,1,0:T(8,128)(2,1)S(1)} collective-permute-done((bf16[8,128,512]{2,1,0:T(8,128)(2,1)S(1)}, bf16[8,128,512]{2,1,0:T(8,128)(2,1)S(1)}, u32[]{:S(2)}, u32[]{:S(2)}) %collective-permute-start.11) | collective-permute-done | bytes 1048608 | tf_op jit(solution)/shard_map/ppermute | solution.py:355
  138.2 4.6 %product.1 = bf16[1024,512]{1,0:T(8,128)(2,1)S(1)} custom-call(bf16[4,1024,128]{2,1,0:T(8,128)(2,1)} %pad_maximum_fusion.refs_0_, bf16[2,1024,128]{2,1,0:T(8,128)(2,1)S(1)} %copy-done.1, bf16[2,1024,128]{2,1,0:T(8,128)(2,1)S(1)} %copy-done.3, bf16[4,1024,128]{2,1,0:T(8,128)(2,1)} %collective-permute-done.7.first.refs_3_, ...), custom_call_target="tpu_custom_call" | custom-call | flops 2147483648 | bytes 7340032 | tf_op jit(solution)/shard_map/product/pallas_call | solution.py:279
  142.7 34.9 %all_to_all.26.terms = bf16[8,128,512]{2,1,0:T(8,128)(2,1)S(1)} all-to-all(bf16[8,128,512]{2,1,0:T(8,128)(2,1)S(1)} %bitcast.10), channel_id=1, replica_groups=mesh['lg'=4,'lq'=2,'rx'=4,'rc'=2,'ch'=4,'cl'=2] {'lg','lq'}, dimensions={0} | all-to-all | bytes 2097152 | tf_op jit(solution)/shard_map/all_to_all | solution.py:322
  177.7 1.9 %finish.1 = bf16[128,1024]{1,0:T(8,128)(2,1)} custom-call(s32[64,64]{1,0:T(8,128)S(1)} %copy-done.6, bf16[8,128,512]{2,1,0:T(8,128)(2,1)S(1)} %all_to_all.26.terms), custom_call_target="tpu_custom_call" | custom-call | flops 1048576 | bytes 2097152 | tf_op jit(solution)/shard_map/finish/pallas_call | solution.py:307
  (26 shorter events, 1.0 us)
Async XLA Ops:
  4.4 48.4 %all-to-all-start.1 = ((bf16[8,1552,128]{2,1,0:T(8,128)(2,1)}), bf16[8,1552,128]{2,1,0:T(8,128)(2,1)S(1)}, u32[]{:S(2)}, u32[]{:S(2)}) async-start(bf16[8,1552,128]{2,1,0:T(8,128)(2,1)} %get-tuple-element.14), calls=%async_computation.1 | async-start | bytes 6356992 | tf_op jit(solution)/shard_map/all_to_all | solution.py:322
  14.9 14.5 %collective-permute-start.3 = (bf16[1024,128]{1,0:T(8,128)(2,1)}, bf16[1024,128]{1,0:T(8,128)(2,1)}, u32[]{:S(2)}, u32[]{:S(2)}) collective-permute-start(bf16[1024,128]{1,0:T(8,128)(2,1)} %get-tuple-element.13), channel_id=1, source_target_pairs={{0,2},{1,3},{2,4},{3,5},{4,6},{5,7},{6,0},{7,1},{8,10},{9,11},{10,... | collective-permute-start | bytes 786440 | tf_op jit(solution)/shard_map/ppermute | solution.py:330
  16.8 20.0 %collective-permute-start.1 = (bf16[1024,128]{1,0:T(8,128)(2,1)}, bf16[1024,128]{1,0:T(8,128)(2,1)}, u32[]{:S(2)}, u32[]{:S(2)}) collective-permute-start(bf16[1024,128]{1,0:T(8,128)(2,1)} %get-tuple-element.13), channel_id=1, source_target_pairs={{0,6},{1,7},{2,0},{3,1},{4,2},{5,3},{6,4},{7,5},{8,14},{9,15},{10,... | collective-permute-start | bytes 786440 | tf_op jit(solution)/shard_map/ppermute | solution.py:330
  22.8 21.2 %collective-permute-start.2 = (bf16[1024,128]{1,0:T(8,128)(2,1)}, bf16[1024,128]{1,0:T(8,128)(2,1)S(1)}, u32[]{:S(2)}, u32[]{:S(2)}) collective-permute-start(bf16[1024,128]{1,0:T(8,128)(2,1)} %get-tuple-element.13), channel_id=1, source_target_pairs={{0,1},{1,2},{2,3},{3,4},{4,5},{5,6},{6,7},{7,0},{8,9},{9,10},{10,1... | collective-permute-start | bytes 786440 | tf_op jit(solution)/shard_map/ppermute | solution.py:330
  25.9 18.0 %collective-permute-start = (bf16[1024,128]{1,0:T(8,128)(2,1)}, bf16[1024,128]{1,0:T(8,128)(2,1)S(1)}, u32[]{:S(2)}, u32[]{:S(2)}) collective-permute-start(bf16[1024,128]{1,0:T(8,128)(2,1)} %get-tuple-element.13), channel_id=1, source_target_pairs={{0,7},{1,0},{2,1},{3,2},{4,3},{5,4},{6,5},{7,6},{8,15},{9,8},{10,9... | collective-permute-start | bytes 786440 | tf_op jit(solution)/shard_map/ppermute | solution.py:330
  29.3 24.8 %collective-permute-start.4 = (bf16[1024,128]{1,0:T(8,128)(2,1)}, bf16[1024,128]{1,0:T(8,128)(2,1)S(1)}, u32[]{:S(2)}, u32[]{:S(2)}) collective-permute-start(bf16[1024,128]{1,0:T(8,128)(2,1)} %collective-permute-done.3), channel_id=1, source_target_pairs={{0,1},{1,2},{2,3},{3,4},{4,5},{5,6},{6,7},{7,0},{8,9},{9,10},{10,1... | collective-permute-start | bytes 786440 | tf_op jit(solution)/shard_map/ppermute | solution.py:330
  36.8 17.4 %collective-permute-start.6 = (bf16[1024,128]{1,0:T(8,128)(2,1)}, bf16[1024,128]{1,0:T(8,128)(2,1)}, u32[]{:S(2)}, u32[]{:S(2)}) collective-permute-start(bf16[1024,128]{1,0:T(8,128)(2,1)} %collective-permute-done.1), channel_id=1, source_target_pairs={{0,6},{1,7},{2,0},{3,1},{4,2},{5,3},{6,4},{7,5},{8,14},{9,15},{10,... | collective-permute-start | bytes 786440 | tf_op jit(solution)/shard_map/ppermute | solution.py:330
  40.2 18.5 %collective-permute-start.5 = (bf16[1024,128]{1,0:T(8,128)(2,1)}, bf16[1024,128]{1,0:T(8,128)(2,1)}, u32[]{:S(2)}, u32[]{:S(2)}) collective-permute-start(bf16[1024,128]{1,0:T(8,128)(2,1)} %collective-permute-done.1), channel_id=1, source_target_pairs={{0,7},{1,0},{2,1},{3,2},{4,3},{5,4},{6,5},{7,6},{8,15},{9,8},{10,9... | collective-permute-start | bytes 786440 | tf_op jit(solution)/shard_map/ppermute | solution.py:330
  46.1 25.6 %collective-permute-start.7 = (bf16[4,1024,128]{2,1,0:T(8,128)(2,1)}, bf16[4,1024,128]{2,1,0:T(8,128)(2,1)}, u32[]{:S(2)}, u32[]{:S(2)}) collective-permute-start(bf16[4,1024,128]{2,1,0:T(8,128)(2,1)} %pad_maximum_fusion.refs_0_), channel_id=1, source_target_pairs={{0,64},{64,0},{1,65},{65,1},{2,66},{66,2},{3,67},{67,3},{4,68},{68... | collective-permute-start | bytes 3145736 | tf_op jit(solution)/shard_map/ppermute | solution.py:338
  54.1 17.6 %copy-start.7 = (bf16[8,512,128]{2,1,0:T(8,128)(2,1)S(1)}, bf16[8,512,128]{2,1,0:T(8,128)(2,1)}, u32[]{:S(2)}) copy-start(bf16[8,512,128]{2,1,0:T(8,128)(2,1)} %get-tuple-element.16.more) | copy-start | bytes 3145732
  63.7 19.7 %collective-permute-start.10 = (bf16[4,2,128,512]{3,2,1,0:T(8,128)(2,1)S(1)}, bf16[4,2,128,512]{3,2,1,0:T(8,128)(2,1)S(1)}, u32[]{:S(2)}, u32[]{:S(2)}) collective-permute-start(bf16[4,2,128,512]{3,2,1,0:T(8,128)(2,1)S(1)} %combine.3), channel_id=1, source_target_pairs={{0,1},{1,0},{2,3},{3,2},{4,5},{5,4},{6,7},{7,6},{8,15},{9,10},{10,... | collective-permute-start | bytes 3145736 | tf_op jit(solution)/shard_map/ppermute | solution.py:350
  67.4 9.2 %copy-start = (bf16[2,1024,128]{2,1,0:T(8,128)(2,1)}, bf16[2,1024,128]{2,1,0:T(8,128)(2,1)S(1)}, u32[]{:S(2)}) copy-start(bf16[2,1024,128]{2,1,0:T(8,128)(2,1)S(1)} %pad_maximum_fusion.1.second.refs_1_) | copy-start | bytes 1572868
  67.4 15.9 %collective-permute-start.8 = (bf16[2,1024,128]{2,1,0:T(8,128)(2,1)S(1)}, bf16[2,1024,128]{2,1,0:T(8,128)(2,1)S(1)}, u32[]{:S(2)}, u32[]{:S(2)}) collective-permute-start(bf16[2,1024,128]{2,1,0:T(8,128)(2,1)S(1)} %pad_maximum_fusion.1.second.refs_1_), channel_id=1, source_target_pairs={{0,64},{64,0},{1,65},{65,1},{2,66},{66,2},{3,67},{67,3},{4,68},{68... | collective-permute-start | bytes 1572872 | tf_op jit(solution)/shard_map/ppermute | solution.py:340
  71.6 5.0 %copy-start.2 = (bf16[2,1024,128]{2,1,0:T(8,128)(2,1)}, bf16[2,1024,128]{2,1,0:T(8,128)(2,1)S(1)}, u32[]{:S(2)}) copy-start(bf16[2,1024,128]{2,1,0:T(8,128)(2,1)S(1)} %pad_maximum_fusion.2.third.refs_2_) | copy-start | bytes 1572868
  83.3 5.8 %copy-start.3 = (bf16[2,1024,128]{2,1,0:T(8,128)(2,1)S(1)}, bf16[2,1024,128]{2,1,0:T(8,128)(2,1)}, u32[]{:S(2)}) copy-start(bf16[2,1024,128]{2,1,0:T(8,128)(2,1)} %copy-done.2) | copy-start | bytes 1572868
  84.4 0.8 copy-start.4
  85.2 52.9 %copy-start.1 = (bf16[2,1024,128]{2,1,0:T(8,128)(2,1)S(1)}, bf16[2,1024,128]{2,1,0:T(8,128)(2,1)}, u32[]{:S(2)}) copy-start(bf16[2,1024,128]{2,1,0:T(8,128)(2,1)} %copy-done) | copy-start | bytes 1572868
  85.2 21.8 %all-to-all-start.2 = ((bf16[4,2,128,512]{3,2,1,0:T(8,128)(2,1)}), bf16[4,2,128,512]{3,2,1,0:T(8,128)(2,1)S(1)}, u32[]{:S(2)}, u32[]{:S(2)}) async-start(bf16[4,2,128,512]{3,2,1,0:T(8,128)(2,1)} %add.1), calls=%async_computation.2 | async-start | bytes 2097152 | tf_op jit(solution)/shard_map/all_to_all | solution.py:322
  89.1 49.0 %copy-start.5 = (bf16[2,1024,128]{2,1,0:T(8,128)(2,1)S(1)}, bf16[2,1024,128]{2,1,0:T(8,128)(2,1)}, u32[]{:S(2)}) copy-start(bf16[2,1024,128]{2,1,0:T(8,128)(2,1)} %copy-done.4) | copy-start | bytes 1572868
  89.1 13.6 %collective-permute-start.9 = (bf16[2,1024,128]{2,1,0:T(8,128)(2,1)S(1)}, bf16[2,1024,128]{2,1,0:T(8,128)(2,1)S(1)}, u32[]{:S(2)}, u32[]{:S(2)}) collective-permute-start(bf16[2,1024,128]{2,1,0:T(8,128)(2,1)S(1)} %copy-done.3), channel_id=1, source_target_pairs={{0,64},{64,0},{1,65},{65,1},{2,66},{66,2},{3,67},{67,3},{4,68},{68... | collective-permute-start | bytes 1572872 | tf_op jit(solution)/shard_map/ppermute | solution.py:342
  130.2 47.5 %copy-start.6 = (s32[64,64]{1,0:T(8,128)S(1)}, s32[64,64]{1,0:T(8,128)}, u32[]{:S(2)}) copy-start(s32[64,64]{1,0:T(8,128)} %pattern.3) | copy-start | bytes 49156
  130.2 8.0 %collective-permute-start.11 = (bf16[8,128,512]{2,1,0:T(8,128)(2,1)S(1)}, bf16[8,128,512]{2,1,0:T(8,128)(2,1)S(1)}, u32[]{:S(2)}, u32[]{:S(2)}) collective-permute-start(bf16[8,128,512]{2,1,0:T(8,128)(2,1)S(1)} %all_to_all.25.refs_6_), channel_id=1, source_target_pairs={{0,8},{8,0},{1,9},{9,1},{2,10},{10,2},{3,11},{11,3},{4,12},{12,4},... | collective-permute-start | bytes 3145736 | tf_op jit(solution)/shard_map/ppermute | solution.py:355

commit v9 on v8

--- a/solution.py
+++ b/solution.py
@@ -332,7 +332,11 @@
         )
 
     one, last, two, sixth = (ahead(sparse, distance) for distance in (1, -1, 2, -2))
-    three, fifth, four = ahead(two, 1), ahead(sixth, -1), ahead(two, 2)
+    three, fifth = ahead(two, 1), ahead(sixth, -1)
+    down = [(c, (c - 2) % SIDE) for c in range(SIDE)]
+    up = [(SIDE + c, SIDE + (c + 2) % SIDE) for c in range(SIDE)]
+    opposite = jnp.where(lax.axis_index("rc") == 0, two, sixth)
+    four = lax.ppermute(opposite, ("rc", "ch", "cl"), down + up)
     swap = [(0, 1), (1, 0)]
     near = jnp.stack([sparse, one, two, last])
     far = lax.ppermute(near, "lq", swap)

time: 181 us -> 184 us (1.017)
  blocking collectives: 58 us -> 51.1 us
  waiting for transfers between devices: 31.7 us -> 36.6 us
  starting transfers between devices: 61.3 us -> 64.8 us
  other arithmetic: 4.89 us -> 6.76 us
    all_to_all x2, waiting for transfers between devices: 7.78 us -> 15.1 us  [exchange(): return lax.all_to_all(values, axes, split_axis=0, concat_axis=0, tiled=True)]
    all_to_all x2, blocking collectives: 58 us -> 51.1 us  [exchange(): return lax.all_to_all(values, axes, split_axis=0, concat_axis=0, tiled=True)]
    ppermute x7 -> x6, waiting for transfers between devices: 4.5 us -> 1.33 us  [ahead(): lax.ppermute(block, ('ch', 'cl'), [(c, (c - distance) % SIDE) for c in ra...]
    all_to_all x2, starting transfers between devices: 14.3 us -> 17.5 us  [exchange(): return lax.all_to_all(values, axes, split_axis=0, concat_axis=0, tiled=True)]
    ppermute x7 -> x6, starting transfers between devices: 29 us -> 26.2 us  [ahead(): lax.ppermute(block, ('ch', 'cl'), [(c, (c - distance) % SIDE) for c in ra...]
    ppermute x0 -> x1, starting transfers between devices: none -> 1.91 us  [body(): four = lax.ppermute(opposite, ('rc', 'ch', 'cl'), down + up)]
  transfers between devices with their start and end apart: 14 -> 14, of which waited for: 7 -> 7; matrix products, arithmetic and copies ran while one was open for 3% -> 4% of each run, Pallas kernels for 5% -> 5%
where the time goes in v9:
time: 184 us; the launch traced here: 183 us
  starting transfers between devices  64.8 us (35%)
  blocking collectives  51.1 us (28%)
  waiting for transfers between devices  36.6 us (20%)
  Pallas kernels  22.1 us (12%)
  other arithmetic  6.76 us (4%)
    all_to_all x2, blocking collectives, exchange(): return lax.all_to_all(values, axes, split_axis=0, concat_axis=0, tiled=True)  51.1 us
    ppermute x6, starting transfers between devices, ahead(): lax.ppermute(block, ('ch', 'cl'), [(c, (c - distance) % SIDE) for c in ra...  26.2 us
    all_to_all x2, starting transfers between devices, exchange(): return lax.all_to_all(values, axes, split_axis=0, concat_axis=0, tiled=True)  17.5 us
    all_to_all x2, waiting for transfers between devices, exchange(): return lax.all_to_all(values, axes, split_axis=0, concat_axis=0, tiled=True)  15.1 us
    ppermute x1, waiting for transfers between devices, body(): far_late = lax.ppermute(near_late, 'lq', swap)  10.4 us
    pallas_call x2, Pallas kernels, combine(): pl.pallas_call(functools.partial(combine_kernel, keeps), out_shape=jax.Sh...  10 us
    ppermute x1, waiting for transfers between devices, body(): far_mid = lax.ppermute(near_mid, 'lq', swap)  6.23 us
    ppermute x1, starting transfers between devices, body(): other = lax.ppermute(own, 'rc', swap)  5.16 us
  transfers between devices with their start and end apart: 14, of which 7 were waited for; matrix products, arithmetic and copies ran while one was open for 4% of the time, Pallas kernels for 5%

profile of v9, /device:TPU:1, one launch (start us, length us, event | category | flops | bytes accessed | tf_op | source)
XLA Modules:
  0.0 183.1 jit_solution(66937669851001744)
XLA Ops:
  0.0 4.4 %pack.1 = (bf16[8,1552,128]{2,1,0:T(8,128)(2,1)}, bf16[8,512,128]{2,1,0:T(8,128)(2,1)}, bf16[1024,128]{1,0:T(8,128)(2,1)}) custom-call(s32[64]{0:T(128)} %bitcast.12, s32[64]{0:T(128)} %slots.1, s32[64,64]{1,0:T(8,128)} %pattern.3, bf16[64,128,128]{2,1,0:T(8,128)(2,1)} %contributions.1, bf16[1024,128]{1,0:T(8,128)(2,1)} %density.1), custom_call_target="tpu_custom_call" | custom-call | bytes 7340032 | tf_op jit(solution)/shard_map/pack/pallas_call | solution.py:86
  4.4 10.4 %all-to-all-start.1 = ((bf16[8,1552,128]{2,1,0:T(8,128)(2,1)}), bf16[8,1552,128]{2,1,0:T(8,128)(2,1)S(1)}, u32[]{:S(2)}, u32[]{:S(2)}) async-start(bf16[8,1552,128]{2,1,0:T(8,128)(2,1)} %get-tuple-element.14), calls=%async_computation.1 | async-start | bytes 6356992 | tf_op jit(solution)/shard_map/all_to_all | solution.py:322
  14.9 1.9 %collective-permute-start.3 = (bf16[1024,128]{1,0:T(8,128)(2,1)}, bf16[1024,128]{1,0:T(8,128)(2,1)}, u32[]{:S(2)}, u32[]{:S(2)}) collective-permute-start(bf16[1024,128]{1,0:T(8,128)(2,1)} %get-tuple-element.13), channel_id=1, source_target_pairs={{0,2},{1,3},{2,4},{3,5},{4,6},{5,7},{6,0},{7,1},{8,10},{9,11},{10,... | collective-permute-start | bytes 786440 | tf_op jit(solution)/shard_map/ppermute | solution.py:330
  16.8 6.0 %collective-permute-start.1 = (bf16[1024,128]{1,0:T(8,128)(2,1)}, bf16[1024,128]{1,0:T(8,128)(2,1)}, u32[]{:S(2)}, u32[]{:S(2)}) collective-permute-start(bf16[1024,128]{1,0:T(8,128)(2,1)} %get-tuple-element.13), channel_id=1, source_target_pairs={{0,6},{1,7},{2,0},{3,1},{4,2},{5,3},{6,4},{7,5},{8,14},{9,15},{10,... | collective-permute-start | bytes 786440 | tf_op jit(solution)/shard_map/ppermute | solution.py:330
  22.8 3.1 %collective-permute-start.2 = (bf16[1024,128]{1,0:T(8,128)(2,1)}, bf16[1024,128]{1,0:T(8,128)(2,1)}, u32[]{:S(2)}, u32[]{:S(2)}) collective-permute-start(bf16[1024,128]{1,0:T(8,128)(2,1)} %get-tuple-element.13), channel_id=1, source_target_pairs={{0,1},{1,2},{2,3},{3,4},{4,5},{5,6},{6,7},{7,0},{8,9},{9,10},{10,1... | collective-permute-start | bytes 786440 | tf_op jit(solution)/shard_map/ppermute | solution.py:330
  25.9 3.4 %collective-permute-start = (bf16[1024,128]{1,0:T(8,128)(2,1)}, bf16[1024,128]{1,0:T(8,128)(2,1)}, u32[]{:S(2)}, u32[]{:S(2)}) collective-permute-start(bf16[1024,128]{1,0:T(8,128)(2,1)} %get-tuple-element.13), channel_id=1, source_target_pairs={{0,7},{1,0},{2,1},{3,2},{4,3},{5,4},{6,5},{7,6},{8,15},{9,8},{10,9... | collective-permute-start | bytes 786440 | tf_op jit(solution)/shard_map/ppermute | solution.py:330
  29.3 7.4 %collective-permute-start.4 = (bf16[1024,128]{1,0:T(8,128)(2,1)}, bf16[1024,128]{1,0:T(8,128)(2,1)S(1)}, u32[]{:S(2)}, u32[]{:S(2)}) collective-permute-start(bf16[1024,128]{1,0:T(8,128)(2,1)} %collective-permute-done.3), channel_id=1, source_target_pairs={{0,1},{1,2},{2,3},{3,4},{4,5},{5,6},{6,7},{7,0},{8,9},{9,10},{10,1... | collective-permute-start | bytes 786440 | tf_op jit(solution)/shard_map/ppermute | solution.py:330
  36.8 1.7 broadcast_select_fusion
  38.5 1.9 %collective-permute-start.6 = (bf16[1024,128]{1,0:T(8,128)(2,1)}, bf16[1024,128]{1,0:T(8,128)(2,1)}, u32[]{:S(2)}, u32[]{:S(2)}) collective-permute-start(bf16[1024,128]{1,0:T(8,128)(2,1)} %broadcast_select_fusion), channel_id=1, source_target_pairs={{0,6},{1,7},{2,0},{3,1},{4,2},{5,3},{6,4},{7,5},{8,10},{9,11},{10,... | collective-permute-start | bytes 786440 | tf_op jit(solution)/shard_map/ppermute | solution.py:339
  40.4 4.3 %collective-permute-start.5 = (bf16[1024,128]{1,0:T(8,128)(2,1)}, bf16[1024,128]{1,0:T(8,128)(2,1)}, u32[]{:S(2)}, u32[]{:S(2)}) collective-permute-start(bf16[1024,128]{1,0:T(8,128)(2,1)} %collective-permute-done.1), channel_id=1, source_target_pairs={{0,7},{1,0},{2,1},{3,2},{4,3},{5,4},{6,5},{7,6},{8,15},{9,8},{10,9... | collective-permute-start | bytes 786440 | tf_op jit(solution)/shard_map/ppermute | solution.py:330
  44.7 2.3 %pad_maximum_fusion.refs_0_ = bf16[4,1024,128]{2,1,0:T(8,128)(2,1)} fusion(bf16[1,1024,128]{2,1,0:T(8,128)(2,1)} %bitcast.4, bf16[1,1024,128]{2,1,0:T(8,128)(2,1)} %bitcast.3, bf16[1,1024,128]{2,1,0:T(8,128)(2,1)} %bitcast.2, bf16[1,1024,128]{2,1,0:T(8,128)(2,1)} %bitcast.1), kind=kLoop, calls=%fused_computation | loop fusion | flops 1572864 | bytes 2097152 | tf_op jit(solution)/shard_map/stack | solution.py:341
  47.0 3.2 %collective-permute-start.7 = (bf16[4,1024,128]{2,1,0:T(8,128)(2,1)}, bf16[4,1024,128]{2,1,0:T(8,128)(2,1)}, u32[]{:S(2)}, u32[]{:S(2)}) collective-permute-start(bf16[4,1024,128]{2,1,0:T(8,128)(2,1)} %pad_maximum_fusion.refs_0_), channel_id=1, source_target_pairs={{0,64},{64,0},{1,65},{65,1},{2,66},{66,2},{3,67},{67,3},{4,68},{68... | collective-permute-start | bytes 3145736 | tf_op jit(solution)/shard_map/ppermute | solution.py:342
  50.2 2.6 %all-to-all-done.1.got = bf16[8,1552,128]{2,1,0:T(8,128)(2,1)S(1)} async-done(((bf16[8,1552,128]{2,1,0:T(8,128)(2,1)}), bf16[8,1552,128]{2,1,0:T(8,128)(2,1)S(1)}, u32[]{:S(2)}, u32[]{:S(2)}) %all-to-all-start.1) | async-done | bytes 3178528 | tf_op jit(solution)/shard_map/all_to_all | solution.py:322
  54.2 1.3 collective-permute-done.5.first
  55.5 5.1 %combine.3 = bf16[4,2,128,512]{3,2,1,0:T(8,128)(2,1)S(1)} custom-call(bf16[8,1552,128]{2,1,0:T(8,128)(2,1)S(1)} %all-to-all-done.1.got, bf16[8,512,128]{2,1,0:T(8,128)(2,1)} %get-tuple-element.16.more, bf16[1024,128]{1,0:T(8,128)(2,1)} %collective-permute-done.5.first, bf16[1024,128]{1,0:T(8,128)(2,1)} %collective-permute-done.6.second, ...), custom_call_target="tpu_custom_call" | custom-call | flops 2097152 | bytes 4194304 | tf_op jit(solution)/shard_map/combine/pallas_call | solution.py:183
  60.6 4.5 %collective-permute-start.10 = (bf16[4,2,128,512]{3,2,1,0:T(8,128)(2,1)S(1)}, bf16[4,2,128,512]{3,2,1,0:T(8,128)(2,1)S(1)}, u32[]{:S(2)}, u32[]{:S(2)}) collective-permute-start(bf16[4,2,128,512]{3,2,1,0:T(8,128)(2,1)S(1)} %combine.3), channel_id=1, source_target_pairs={{0,1},{1,0},{2,3},{3,2},{4,5},{5,4},{6,7},{7,6},{8,15},{9,10},{10,... | collective-permute-start | bytes 3145736 | tf_op jit(solution)/shard_map/ppermute | solution.py:354
  66.1 3.2 %collective-permute-start.8 = (bf16[2,1024,128]{2,1,0:T(8,128)(2,1)S(1)}, bf16[2,1024,128]{2,1,0:T(8,128)(2,1)S(1)}, u32[]{:S(2)}, u32[]{:S(2)}) collective-permute-start(bf16[2,1024,128]{2,1,0:T(8,128)(2,1)S(1)} %pad_maximum_fusion.1.second.refs_1_), channel_id=1, source_target_pairs={{0,64},{64,0},{1,65},{65,1},{2,66},{66,2},{3,67},{67,3},{4,68},{68... | collective-permute-start | bytes 1572872 | tf_op jit(solution)/shard_map/ppermute | solution.py:344
  69.3 1.1 pad_maximum_fusion.2.third.refs_2_
  70.4 1.3 collective-permute-done.7.first.refs_3_
  71.7 4.9 %combine.2.keep = bf16[4,2,128,512]{3,2,1,0:T(8,128)(2,1)S(1)} custom-call(bf16[8,1552,128]{2,1,0:T(8,128)(2,1)S(1)} %all-to-all-done.1.got, bf16[8,512,128]{2,1,0:T(8,128)(2,1)S(1)} %copy-done.7, bf16[4,1024,128]{2,1,0:T(8,128)(2,1)} %collective-permute-done.7.first.refs_3_, bf16[2,1024,128]{2,1,0:T(8,128)(2,1)S(1)} %pad_maximum_fusion.1.second.refs_1_, ...), custom_call_target="tpu_custom_call" | custom-call | flops 2097152 | bytes 4194304 | tf_op jit(solution)/shard_map/combine/pallas_call | solution.py:183
  76.6 6.2 %collective-permute-done.8.wait.refs_4_ = bf16[2,1024,128]{2,1,0:T(8,128)(2,1)S(1)} collective-permute-done((bf16[2,1024,128]{2,1,0:T(8,128)(2,1)S(1)}, bf16[2,1024,128]{2,1,0:T(8,128)(2,1)S(1)}, u32[]{:S(2)}, u32[]{:S(2)}) %collective-permute-start.8) | collective-permute-done | bytes 524320 | tf_op jit(solution)/shard_map/ppermute | solution.py:344
  82.9 1.1 add.1
  84.8 7.1 %all-to-all-start.2 = ((bf16[4,2,128,512]{3,2,1,0:T(8,128)(2,1)}), bf16[4,2,128,512]{3,2,1,0:T(8,128)(2,1)S(1)}, u32[]{:S(2)}, u32[]{:S(2)}) async-start(bf16[4,2,128,512]{3,2,1,0:T(8,128)(2,1)} %add.1), calls=%async_computation.2 | async-start | bytes 2097152 | tf_op jit(solution)/shard_map/all_to_all | solution.py:322
  91.8 3.2 %collective-permute-start.9 = (bf16[2,1024,128]{2,1,0:T(8,128)(2,1)S(1)}, bf16[2,1024,128]{2,1,0:T(8,128)(2,1)S(1)}, u32[]{:S(2)}, u32[]{:S(2)}) collective-permute-start(bf16[2,1024,128]{2,1,0:T(8,128)(2,1)S(1)} %copy-done.3), channel_id=1, source_target_pairs={{0,64},{64,0},{1,65},{65,1},{2,66},{66,2},{3,67},{67,3},{4,68},{68... | collective-permute-start | bytes 1572872 | tf_op jit(solution)/shard_map/ppermute | solution.py:346
  95.0 10.4 %collective-permute-done.9.far.refs_5_ = bf16[2,1024,128]{2,1,0:T(8,128)(2,1)S(1)} collective-permute-done((bf16[2,1024,128]{2,1,0:T(8,128)(2,1)S(1)}, bf16[2,1024,128]{2,1,0:T(8,128)(2,1)S(1)}, u32[]{:S(2)}, u32[]{:S(2)}) %collective-permute-start.9) | collective-permute-done | bytes 524320 | tf_op jit(solution)/shard_map/ppermute | solution.py:346
  105.4 12.5 %all-to-all-done.2.parts = bf16[4,2,128,512]{3,2,1,0:T(8,128)(2,1)S(1)} async-done(((bf16[4,2,128,512]{3,2,1,0:T(8,128)(2,1)}), bf16[4,2,128,512]{3,2,1,0:T(8,128)(2,1)S(1)}, u32[]{:S(2)}, u32[]{:S(2)}) %all-to-all-start.2) | async-done | bytes 1048608 | tf_op jit(solution)/shard_map/all_to_all | solution.py:322
  118.0 17.0 %all_to_all.25.refs_6_ = bf16[8,128,512]{2,1,0:T(8,128)(2,1)S(1)} all-to-all(bf16[8,128,512]{2,1,0:T(8,128)(2,1)S(1)} %spread.1), channel_id=1, replica_groups=mesh['lg'=4,'lq'=2,'rx'=4,'rc'=2,'ch'=4,'cl'=2] {'lq','rx'}, dimensions={0} | all-to-all | bytes 2097152 | tf_op jit(solution)/shard_map/all_to_all | solution.py:322
  135.0 5.2 %collective-permute-start.11 = (bf16[8,128,512]{2,1,0:T(8,128)(2,1)S(1)}, bf16[8,128,512]{2,1,0:T(8,128)(2,1)S(1)}, u32[]{:S(2)}, u32[]{:S(2)}) collective-permute-start(bf16[8,128,512]{2,1,0:T(8,128)(2,1)S(1)} %all_to_all.25.refs_6_), channel_id=1, source_target_pairs={{0,8},{8,0},{1,9},{9,1},{2,10},{10,2},{3,11},{11,3},{4,12},{12,4},... | collective-permute-start | bytes 3145736 | tf_op jit(solution)/shard_map/ppermute | solution.py:359
  140.2 2.3 %collective-permute-done.11.refs_7_ = bf16[8,128,512]{2,1,0:T(8,128)(2,1)S(1)} collective-permute-done((bf16[8,128,512]{2,1,0:T(8,128)(2,1)S(1)}, bf16[8,128,512]{2,1,0:T(8,128)(2,1)S(1)}, u32[]{:S(2)}, u32[]{:S(2)}) %collective-permute-start.11) | collective-permute-done | bytes 1048608 | tf_op jit(solution)/shard_map/ppermute | solution.py:359
  142.4 4.6 %product.1 = bf16[1024,512]{1,0:T(8,128)(2,1)S(1)} custom-call(bf16[4,1024,128]{2,1,0:T(8,128)(2,1)} %pad_maximum_fusion.refs_0_, bf16[2,1024,128]{2,1,0:T(8,128)(2,1)S(1)} %copy-done.1, bf16[2,1024,128]{2,1,0:T(8,128)(2,1)S(1)} %copy-done.3, bf16[4,1024,128]{2,1,0:T(8,128)(2,1)} %collective-permute-done.7.first.refs_3_, ...), custom_call_target="tpu_custom_call" | custom-call | flops 2147483648 | bytes 7340032 | tf_op jit(solution)/shard_map/product/pallas_call | solution.py:279
  147.0 34.1 %all_to_all.26.terms = bf16[8,128,512]{2,1,0:T(8,128)(2,1)S(1)} all-to-all(bf16[8,128,512]{2,1,0:T(8,128)(2,1)S(1)} %bitcast.10), channel_id=1, replica_groups=mesh['lg'=4,'lq'=2,'rx'=4,'rc'=2,'ch'=4,'cl'=2] {'lg','lq'}, dimensions={0} | all-to-all | bytes 2097152 | tf_op jit(solution)/shard_map/all_to_all | solution.py:322
  181.1 1.9 %finish.1 = bf16[128,1024]{1,0:T(8,128)(2,1)} custom-call(s32[64,64]{1,0:T(8,128)S(1)} %copy-done.6, bf16[8,128,512]{2,1,0:T(8,128)(2,1)S(1)} %all_to_all.26.terms), custom_call_target="tpu_custom_call" | custom-call | flops 1048576 | bytes 2097152 | tf_op jit(solution)/shard_map/finish/pallas_call | solution.py:307
  (27 shorter events, 2.6 us)
Async XLA Ops:
  4.4 48.4 %all-to-all-start.1 = ((bf16[8,1552,128]{2,1,0:T(8,128)(2,1)}), bf16[8,1552,128]{2,1,0:T(8,128)(2,1)S(1)}, u32[]{:S(2)}, u32[]{:S(2)}) async-start(bf16[8,1552,128]{2,1,0:T(8,128)(2,1)} %get-tuple-element.14), calls=%async_computation.1 | async-start | bytes 6356992 | tf_op jit(solution)/shard_map/all_to_all | solution.py:322
  14.9 14.5 %collective-permute-start.3 = (bf16[1024,128]{1,0:T(8,128)(2,1)}, bf16[1024,128]{1,0:T(8,128)(2,1)}, u32[]{:S(2)}, u32[]{:S(2)}) collective-permute-start(bf16[1024,128]{1,0:T(8,128)(2,1)} %get-tuple-element.13), channel_id=1, source_target_pairs={{0,2},{1,3},{2,4},{3,5},{4,6},{5,7},{6,0},{7,1},{8,10},{9,11},{10,... | collective-permute-start | bytes 786440 | tf_op jit(solution)/shard_map/ppermute | solution.py:330
  16.8 20.0 %collective-permute-start.1 = (bf16[1024,128]{1,0:T(8,128)(2,1)}, bf16[1024,128]{1,0:T(8,128)(2,1)}, u32[]{:S(2)}, u32[]{:S(2)}) collective-permute-start(bf16[1024,128]{1,0:T(8,128)(2,1)} %get-tuple-element.13), channel_id=1, source_target_pairs={{0,6},{1,7},{2,0},{3,1},{4,2},{5,3},{6,4},{7,5},{8,14},{9,15},{10,... | collective-permute-start | bytes 786440 | tf_op jit(solution)/shard_map/ppermute | solution.py:330
  22.8 21.9 %collective-permute-start.2 = (bf16[1024,128]{1,0:T(8,128)(2,1)}, bf16[1024,128]{1,0:T(8,128)(2,1)}, u32[]{:S(2)}, u32[]{:S(2)}) collective-permute-start(bf16[1024,128]{1,0:T(8,128)(2,1)} %get-tuple-element.13), channel_id=1, source_target_pairs={{0,1},{1,2},{2,3},{3,4},{4,5},{5,6},{6,7},{7,0},{8,9},{9,10},{10,1... | collective-permute-start | bytes 786440 | tf_op jit(solution)/shard_map/ppermute | solution.py:330
  25.9 18.8 %collective-permute-start = (bf16[1024,128]{1,0:T(8,128)(2,1)}, bf16[1024,128]{1,0:T(8,128)(2,1)}, u32[]{:S(2)}, u32[]{:S(2)}) collective-permute-start(bf16[1024,128]{1,0:T(8,128)(2,1)} %get-tuple-element.13), channel_id=1, source_target_pairs={{0,7},{1,0},{2,1},{3,2},{4,3},{5,4},{6,5},{7,6},{8,15},{9,8},{10,9... | collective-permute-start | bytes 786440 | tf_op jit(solution)/shard_map/ppermute | solution.py:330
  29.3 24.8 %collective-permute-start.4 = (bf16[1024,128]{1,0:T(8,128)(2,1)}, bf16[1024,128]{1,0:T(8,128)(2,1)S(1)}, u32[]{:S(2)}, u32[]{:S(2)}) collective-permute-start(bf16[1024,128]{1,0:T(8,128)(2,1)} %collective-permute-done.3), channel_id=1, source_target_pairs={{0,1},{1,2},{2,3},{3,4},{4,5},{5,6},{6,7},{7,0},{8,9},{9,10},{10,1... | collective-permute-start | bytes 786440 | tf_op jit(solution)/shard_map/ppermute | solution.py:330
  38.5 15.7 %collective-permute-start.6 = (bf16[1024,128]{1,0:T(8,128)(2,1)}, bf16[1024,128]{1,0:T(8,128)(2,1)}, u32[]{:S(2)}, u32[]{:S(2)}) collective-permute-start(bf16[1024,128]{1,0:T(8,128)(2,1)} %broadcast_select_fusion), channel_id=1, source_target_pairs={{0,6},{1,7},{2,0},{3,1},{4,2},{5,3},{6,4},{7,5},{8,10},{9,11},{10,... | collective-permute-start | bytes 786440 | tf_op jit(solution)/shard_map/ppermute | solution.py:339
  40.4 15.1 %collective-permute-start.5 = (bf16[1024,128]{1,0:T(8,128)(2,1)}, bf16[1024,128]{1,0:T(8,128)(2,1)}, u32[]{:S(2)}, u32[]{:S(2)}) collective-permute-start(bf16[1024,128]{1,0:T(8,128)(2,1)} %collective-permute-done.1), channel_id=1, source_target_pairs={{0,7},{1,0},{2,1},{3,2},{4,3},{5,4},{6,5},{7,6},{8,15},{9,8},{10,9... | collective-permute-start | bytes 786440 | tf_op jit(solution)/shard_map/ppermute | solution.py:330
  47.0 24.7 %collective-permute-start.7 = (bf16[4,1024,128]{2,1,0:T(8,128)(2,1)}, bf16[4,1024,128]{2,1,0:T(8,128)(2,1)}, u32[]{:S(2)}, u32[]{:S(2)}) collective-permute-start(bf16[4,1024,128]{2,1,0:T(8,128)(2,1)} %pad_maximum_fusion.refs_0_), channel_id=1, source_target_pairs={{0,64},{64,0},{1,65},{65,1},{2,66},{66,2},{3,67},{67,3},{4,68},{68... | collective-permute-start | bytes 3145736 | tf_op jit(solution)/shard_map/ppermute | solution.py:342
  54.1 17.6 %copy-start.7 = (bf16[8,512,128]{2,1,0:T(8,128)(2,1)S(1)}, bf16[8,512,128]{2,1,0:T(8,128)(2,1)}, u32[]{:S(2)}) copy-start(bf16[8,512,128]{2,1,0:T(8,128)(2,1)} %get-tuple-element.16.more) | copy-start | bytes 3145732
  60.6 22.2 %collective-permute-start.10 = (bf16[4,2,128,512]{3,2,1,0:T(8,128)(2,1)S(1)}, bf16[4,2,128,512]{3,2,1,0:T(8,128)(2,1)S(1)}, u32[]{:S(2)}, u32[]{:S(2)}) collective-permute-start(bf16[4,2,128,512]{3,2,1,0:T(8,128)(2,1)S(1)} %combine.3), channel_id=1, source_target_pairs={{0,1},{1,0},{2,3},{3,2},{4,5},{5,4},{6,7},{7,6},{8,15},{9,10},{10,... | collective-permute-start | bytes 3145736 | tf_op jit(solution)/shard_map/ppermute | solution.py:354
  66.1 10.5 %copy-start = (bf16[2,1024,128]{2,1,0:T(8,128)(2,1)}, bf16[2,1024,128]{2,1,0:T(8,128)(2,1)S(1)}, u32[]{:S(2)}) copy-start(bf16[2,1024,128]{2,1,0:T(8,128)(2,1)S(1)} %pad_maximum_fusion.1.second.refs_1_) | copy-start | bytes 1572868
  66.1 16.7 %collective-permute-start.8 = (bf16[2,1024,128]{2,1,0:T(8,128)(2,1)S(1)}, bf16[2,1024,128]{2,1,0:T(8,128)(2,1)S(1)}, u32[]{:S(2)}, u32[]{:S(2)}) collective-permute-start(bf16[2,1024,128]{2,1,0:T(8,128)(2,1)S(1)} %pad_maximum_fusion.1.second.refs_1_), channel_id=1, source_target_pairs={{0,64},{64,0},{1,65},{65,1},{2,66},{66,2},{3,67},{67,3},{4,68},{68... | collective-permute-start | bytes 1572872 | tf_op jit(solution)/shard_map/ppermute | solution.py:344
  70.4 6.2 %copy-start.2 = (bf16[2,1024,128]{2,1,0:T(8,128)(2,1)}, bf16[2,1024,128]{2,1,0:T(8,128)(2,1)S(1)}, u32[]{:S(2)}) copy-start(bf16[2,1024,128]{2,1,0:T(8,128)(2,1)S(1)} %pad_maximum_fusion.2.third.refs_2_) | copy-start | bytes 1572868
  82.9 9.0 %copy-start.3 = (bf16[2,1024,128]{2,1,0:T(8,128)(2,1)S(1)}, bf16[2,1024,128]{2,1,0:T(8,128)(2,1)}, u32[]{:S(2)}) copy-start(bf16[2,1024,128]{2,1,0:T(8,128)(2,1)} %copy-done.2) | copy-start | bytes 1572868
  84.0 0.8 copy-start.4
  84.7 57.7 %copy-start.1 = (bf16[2,1024,128]{2,1,0:T(8,128)(2,1)S(1)}, bf16[2,1024,128]{2,1,0:T(8,128)(2,1)}, u32[]{:S(2)}) copy-start(bf16[2,1024,128]{2,1,0:T(8,128)(2,1)} %copy-done) | copy-start | bytes 1572868
  84.8 33.2 %all-to-all-start.2 = ((bf16[4,2,128,512]{3,2,1,0:T(8,128)(2,1)}), bf16[4,2,128,512]{3,2,1,0:T(8,128)(2,1)S(1)}, u32[]{:S(2)}, u32[]{:S(2)}) async-start(bf16[4,2,128,512]{3,2,1,0:T(8,128)(2,1)} %add.1), calls=%async_computation.2 | async-start | bytes 2097152 | tf_op jit(solution)/shard_map/all_to_all | solution.py:322
  91.8 50.6 %copy-start.5 = (bf16[2,1024,128]{2,1,0:T(8,128)(2,1)S(1)}, bf16[2,1024,128]{2,1,0:T(8,128)(2,1)}, u32[]{:S(2)}) copy-start(bf16[2,1024,128]{2,1,0:T(8,128)(2,1)} %copy-done.4) | copy-start | bytes 1572868
  91.8 13.6 %collective-permute-start.9 = (bf16[2,1024,128]{2,1,0:T(8,128)(2,1)S(1)}, bf16[2,1024,128]{2,1,0:T(8,128)(2,1)S(1)}, u32[]{:S(2)}, u32[]{:S(2)}) collective-permute-start(bf16[2,1024,128]{2,1,0:T(8,128)(2,1)S(1)} %copy-done.3), channel_id=1, source_target_pairs={{0,64},{64,0},{1,65},{65,1},{2,66},{66,2},{3,67},{67,3},{4,68},{68... | collective-permute-start | bytes 1572872 | tf_op jit(solution)/shard_map/ppermute | solution.py:346
  135.0 46.1 %copy-start.6 = (s32[64,64]{1,0:T(8,128)S(1)}, s32[64,64]{1,0:T(8,128)}, u32[]{:S(2)}) copy-start(s32[64,64]{1,0:T(8,128)} %pattern.3) | copy-start | bytes 49156
  135.0 7.4 %collective-permute-start.11 = (bf16[8,128,512]{2,1,0:T(8,128)(2,1)S(1)}, bf16[8,128,512]{2,1,0:T(8,128)(2,1)S(1)}, u32[]{:S(2)}, u32[]{:S(2)}) collective-permute-start(bf16[8,128,512]{2,1,0:T(8,128)(2,1)S(1)} %all_to_all.25.refs_6_), channel_id=1, source_target_pairs={{0,8},{8,0},{1,9},{9,1},{2,10},{10,2},{3,11},{11,3},{4,12},{12,4},... | collective-permute-start | bytes 3145736 | tf_op jit(solution)/shard_map/ppermute | solution.py:359

commit v10 on v9

--- a/solution.py
+++ b/solution.py
@@ -340,9 +340,7 @@
     swap = [(0, 1), (1, 0)]
     near = jnp.stack([sparse, one, two, last])
     far = lax.ppermute(near, "lq", swap)
-    near_mid = jnp.stack([sixth, fifth])
-    far_mid = lax.ppermute(near_mid, "lq", swap)
-    near_late = jnp.stack([three, four])
+    near_late = jnp.stack([sixth, fifth, three, four])
     far_late = lax.ppermute(near_late, "lq", swap)
 
     anyone = jnp.max(got[:, BODY, FLAG].astype(jnp.float32)) > 0
@@ -352,12 +350,12 @@
     even = [(c, c ^ 1) for c in range(count)]
     odd = [(count + c, count + (c + (1 if c % 2 else -1)) % count) for c in range(count)]
     taken = lax.ppermute(send, ("rc", "ch", "cl"), even + odd)
-    keep = combine(True, got, more, far, near_mid, near_late)
-    parts = exchange(add(keep, taken, far_mid), "ch")
+    keep = combine(True, got, more, near, near_late, near_late)
+    parts = exchange(add(keep, taken, far), "ch")
 
     own = exchange(spread(parts, far_late), ("lq", "rx"))
     other = lax.ppermute(own, "rc", swap)
-    term = product_of((near, near_mid, near_late, far, far_mid, far_late), own, other)
+    term = product_of((near, near_late, far, far_late), own, other)
     terms = exchange(term.reshape(SIDE, TILE, -1), ("lg", "lq"))
     return finish(pattern, terms)
 

time: 184 us -> 175 us (0.951)
  starting transfers between devices: 64.8 us -> 59 us
  waiting for transfers between devices: 36.6 us -> 33.9 us
  blocking collectives: 51.1 us -> 53.6 us
    all_to_all x2, waiting for transfers between devices: 15.1 us -> 2.53 us  [exchange(): return lax.all_to_all(values, axes, split_axis=0, concat_axis=0, tiled=True)]
    ppermute x1, waiting for transfers between devices: 10.4 us -> 21 us  [body(): far_late = lax.ppermute(near_late, 'lq', swap)]
    ppermute x1 -> x0, waiting for transfers between devices: 6.23 us -> none  [body(): far_mid = lax.ppermute(near_mid, 'lq', swap)]
    ppermute x1, waiting for transfers between devices: 0.01 us -> 4.86 us  [body(): taken = lax.ppermute(send, ('rc', 'ch', 'cl'), even + odd)]
    ppermute x1 -> x0, starting transfers between devices: 3.21 us -> none  [body(): far_mid = lax.ppermute(near_mid, 'lq', swap)]
    all_to_all x2, starting transfers between devices: 17.5 us -> 14.3 us  [exchange(): return lax.all_to_all(values, axes, split_axis=0, concat_axis=0, tiled=True)]
    all_to_all x2, blocking collectives: 51.1 us -> 53.6 us  [exchange(): return lax.all_to_all(values, axes, split_axis=0, concat_axis=0, tiled=True)]
  transfers between devices with their start and end apart: 14 -> 13, of which waited for: 7 -> 6; matrix products, arithmetic and copies ran while one was open for 4% -> 3% of each run, Pallas kernels for 5% -> 5%
where the time goes in v10:
time: 175 us; the launch traced here: 174 us
  starting transfers between devices  59 us (34%)
  blocking collectives  53.6 us (31%)
  waiting for transfers between devices  33.9 us (19%)
  Pallas kernels  20.8 us (12%)
  other arithmetic  5.95 us (3%)
    all_to_all x2, blocking collectives, exchange(): return lax.all_to_all(values, axes, split_axis=0, concat_axis=0, tiled=True)  53.6 us
    ppermute x6, starting transfers between devices, ahead(): lax.ppermute(block, ('ch', 'cl'), [(c, (c - distance) % SIDE) for c in ra...  26.2 us
    ppermute x1, waiting for transfers between devices, body(): far_late = lax.ppermute(near_late, 'lq', swap)  21 us
    all_to_all x2, starting transfers between devices, exchange(): return lax.all_to_all(values, axes, split_axis=0, concat_axis=0, tiled=True)  14.3 us
    pallas_call x2, Pallas kernels, combine(): pl.pallas_call(functools.partial(combine_kernel, keeps), out_shape=jax.Sh...  8.62 us
    ppermute x1, starting transfers between devices, body(): other = lax.ppermute(own, 'rc', swap)  5.67 us
    ppermute x1, waiting for transfers between devices, body(): taken = lax.ppermute(send, ('rc', 'ch', 'cl'), even + odd)  4.86 us
    pallas_call x1, Pallas kernels, product_of(): pl.pallas_call(product_kernel, out_shape=jax.ShapeDtypeStruct((rows, widt...  4.55 us
  transfers between devices with their start and end apart: 13, of which 6 were waited for; matrix products, arithmetic and copies ran while one was open for 3% of the time, Pallas kernels for 5%

profile of v10, /device:TPU:1, one launch (start us, length us, event | category | flops | bytes accessed | tf_op | source)
XLA Modules:
  0.0 174.2 jit_solution(2069509995616953792)
XLA Ops:
  0.0 4.4 %pack.1 = (bf16[8,1552,128]{2,1,0:T(8,128)(2,1)}, bf16[8,512,128]{2,1,0:T(8,128)(2,1)}, bf16[1024,128]{1,0:T(8,128)(2,1)}) custom-call(s32[64]{0:T(128)} %bitcast.12, s32[64]{0:T(128)} %slots.1, s32[64,64]{1,0:T(8,128)} %pattern.3, bf16[64,128,128]{2,1,0:T(8,128)(2,1)} %contributions.1, bf16[1024,128]{1,0:T(8,128)(2,1)} %density.1), custom_call_target="tpu_custom_call" | custom-call | bytes 7340032 | tf_op jit(solution)/shard_map/pack/pallas_call | solution.py:86
  4.4 10.4 %all-to-all-start.1 = ((bf16[8,1552,128]{2,1,0:T(8,128)(2,1)}), bf16[8,1552,128]{2,1,0:T(8,128)(2,1)S(1)}, u32[]{:S(2)}, u32[]{:S(2)}) async-start(bf16[8,1552,128]{2,1,0:T(8,128)(2,1)} %get-tuple-element.14), calls=%async_computation.1 | async-start | bytes 6356992 | tf_op jit(solution)/shard_map/all_to_all | solution.py:322
  14.9 1.9 %collective-permute-start.3 = (bf16[1024,128]{1,0:T(8,128)(2,1)}, bf16[1024,128]{1,0:T(8,128)(2,1)}, u32[]{:S(2)}, u32[]{:S(2)}) collective-permute-start(bf16[1024,128]{1,0:T(8,128)(2,1)} %get-tuple-element.13), channel_id=1, source_target_pairs={{0,2},{1,3},{2,4},{3,5},{4,6},{5,7},{6,0},{7,1},{8,10},{9,11},{10,... | collective-permute-start | bytes 786440 | tf_op jit(solution)/shard_map/ppermute | solution.py:330
  16.8 6.0 %collective-permute-start.1 = (bf16[1024,128]{1,0:T(8,128)(2,1)}, bf16[1024,128]{1,0:T(8,128)(2,1)}, u32[]{:S(2)}, u32[]{:S(2)}) collective-permute-start(bf16[1024,128]{1,0:T(8,128)(2,1)} %get-tuple-element.13), channel_id=1, source_target_pairs={{0,6},{1,7},{2,0},{3,1},{4,2},{5,3},{6,4},{7,5},{8,14},{9,15},{10,... | collective-permute-start | bytes 786440 | tf_op jit(solution)/shard_map/ppermute | solution.py:330
  22.8 3.1 %collective-permute-start.2 = (bf16[1024,128]{1,0:T(8,128)(2,1)}, bf16[1024,128]{1,0:T(8,128)(2,1)}, u32[]{:S(2)}, u32[]{:S(2)}) collective-permute-start(bf16[1024,128]{1,0:T(8,128)(2,1)} %get-tuple-element.13), channel_id=1, source_target_pairs={{0,1},{1,2},{2,3},{3,4},{4,5},{5,6},{6,7},{7,0},{8,9},{9,10},{10,1... | collective-permute-start | bytes 786440 | tf_op jit(solution)/shard_map/ppermute | solution.py:330
  25.9 3.4 %collective-permute-start = (bf16[1024,128]{1,0:T(8,128)(2,1)}, bf16[1024,128]{1,0:T(8,128)(2,1)}, u32[]{:S(2)}, u32[]{:S(2)}) collective-permute-start(bf16[1024,128]{1,0:T(8,128)(2,1)} %get-tuple-element.13), channel_id=1, source_target_pairs={{0,7},{1,0},{2,1},{3,2},{4,3},{5,4},{6,5},{7,6},{8,15},{9,8},{10,9... | collective-permute-start | bytes 786440 | tf_op jit(solution)/shard_map/ppermute | solution.py:330
  29.3 7.4 %collective-permute-start.4 = (bf16[1024,128]{1,0:T(8,128)(2,1)}, bf16[1024,128]{1,0:T(8,128)(2,1)S(1)}, u32[]{:S(2)}, u32[]{:S(2)}) collective-permute-start(bf16[1024,128]{1,0:T(8,128)(2,1)} %collective-permute-done.3), channel_id=1, source_target_pairs={{0,1},{1,2},{2,3},{3,4},{4,5},{5,6},{6,7},{7,0},{8,9},{9,10},{10,1... | collective-permute-start | bytes 786440 | tf_op jit(solution)/shard_map/ppermute | solution.py:330
  36.8 1.7 broadcast_select_fusion
  38.5 1.9 %collective-permute-start.6 = (bf16[1024,128]{1,0:T(8,128)(2,1)}, bf16[1024,128]{1,0:T(8,128)(2,1)}, u32[]{:S(2)}, u32[]{:S(2)}) collective-permute-start(bf16[1024,128]{1,0:T(8,128)(2,1)} %broadcast_select_fusion), channel_id=1, source_target_pairs={{0,6},{1,7},{2,0},{3,1},{4,2},{5,3},{6,4},{7,5},{8,10},{9,11},{10,... | collective-permute-start | bytes 786440 | tf_op jit(solution)/shard_map/ppermute | solution.py:339
  40.4 4.3 %collective-permute-start.5 = (bf16[1024,128]{1,0:T(8,128)(2,1)}, bf16[1024,128]{1,0:T(8,128)(2,1)}, u32[]{:S(2)}, u32[]{:S(2)}) collective-permute-start(bf16[1024,128]{1,0:T(8,128)(2,1)} %collective-permute-done.1), channel_id=1, source_target_pairs={{0,7},{1,0},{2,1},{3,2},{4,3},{5,4},{6,5},{7,6},{8,15},{9,8},{10,9... | collective-permute-start | bytes 786440 | tf_op jit(solution)/shard_map/ppermute | solution.py:330
  44.8 2.3 %pad_maximum_fusion.first.refs_0_ = bf16[4,1024,128]{2,1,0:T(8,128)(2,1)} fusion(bf16[1,1024,128]{2,1,0:T(8,128)(2,1)} %bitcast.4, bf16[1,1024,128]{2,1,0:T(8,128)(2,1)} %bitcast.3, bf16[1,1024,128]{2,1,0:T(8,128)(2,1)} %bitcast.2, bf16[1,1024,128]{2,1,0:T(8,128)(2,1)} %bitcast.1), kind=kLoop, calls=%fused_computation | loop fusion | flops 1572864 | bytes 2097152 | tf_op jit(solution)/shard_map/stack | solution.py:341
  47.1 3.2 %collective-permute-start.7 = (bf16[4,1024,128]{2,1,0:T(8,128)(2,1)}, bf16[4,1024,128]{2,1,0:T(8,128)(2,1)}, u32[]{:S(2)}, u32[]{:S(2)}) collective-permute-start(bf16[4,1024,128]{2,1,0:T(8,128)(2,1)} %pad_maximum_fusion.first.refs_0_), channel_id=1, source_target_pairs={{0,64},{64,0},{1,65},{65,1},{2,66},{66,2},{3,67},{67,3},{4,68},{68... | collective-permute-start | bytes 3145736 | tf_op jit(solution)/shard_map/ppermute | solution.py:342
  50.3 2.5 %all-to-all-done.1.got = bf16[8,1552,128]{2,1,0:T(8,128)(2,1)S(1)} async-done(((bf16[8,1552,128]{2,1,0:T(8,128)(2,1)}), bf16[8,1552,128]{2,1,0:T(8,128)(2,1)S(1)}, u32[]{:S(2)}, u32[]{:S(2)}) %all-to-all-start.1) | async-done | bytes 3178528 | tf_op jit(solution)/shard_map/all_to_all | solution.py:322
  52.8 0.7 slice_reduce_fusion
  54.2 1.4 collective-permute-done.5.first
  55.6 4.3 %combine.3 = bf16[4,2,128,512]{3,2,1,0:T(8,128)(2,1)S(1)} custom-call(bf16[8,1552,128]{2,1,0:T(8,128)(2,1)S(1)} %all-to-all-done.1.got, bf16[8,512,128]{2,1,0:T(8,128)(2,1)} %get-tuple-element.16.more, bf16[1024,128]{1,0:T(8,128)(2,1)} %collective-permute-done.5.first, bf16[1024,128]{1,0:T(8,128)(2,1)} %collective-permute-done.6.second, ...), custom_call_target="tpu_custom_call" | custom-call | flops 2097152 | bytes 4194304 | tf_op jit(solution)/shard_map/combine/pallas_call | solution.py:183
  59.9 4.4 %collective-permute-start.9 = (bf16[4,2,128,512]{3,2,1,0:T(8,128)(2,1)S(1)}, bf16[4,2,128,512]{3,2,1,0:T(8,128)(2,1)S(1)}, u32[]{:S(2)}, u32[]{:S(2)}) collective-permute-start(bf16[4,2,128,512]{3,2,1,0:T(8,128)(2,1)S(1)} %combine.3), channel_id=1, source_target_pairs={{0,1},{1,0},{2,3},{3,2},{4,5},{5,4},{6,7},{7,6},{8,15},{9,10},{10,... | collective-permute-start | bytes 3145736 | tf_op jit(solution)/shard_map/ppermute | solution.py:352
  64.3 1.2 pad_maximum_fusion.1.second.third.refs_1_
  65.5 4.3 %combine.2.keep = bf16[4,2,128,512]{3,2,1,0:T(8,128)(2,1)S(1)} custom-call(bf16[8,1552,128]{2,1,0:T(8,128)(2,1)S(1)} %all-to-all-done.1.got, bf16[8,512,128]{2,1,0:T(8,128)(2,1)S(1)} %copy-done.3, bf16[4,1024,128]{2,1,0:T(8,128)(2,1)} %pad_maximum_fusion.first.refs_0_, bf16[4,1024,128]{2,1,0:T(8,128)(2,1)S(1)} %pad_maximum_fusion.1.second.third.refs_1_, ...), custom_call_target="tpu_custom_call" | custom-call | flops 2097152 | bytes 4194304 | tf_op jit(solution)/shard_map/combine/pallas_call | solution.py:183
  69.9 1.9 %collective-permute-done.7.wait.refs_2_ = bf16[4,1024,128]{2,1,0:T(8,128)(2,1)} collective-permute-done((bf16[4,1024,128]{2,1,0:T(8,128)(2,1)}, bf16[4,1024,128]{2,1,0:T(8,128)(2,1)}, u32[]{:S(2)}, u32[]{:S(2)}) %collective-permute-start.7) | collective-permute-done | bytes 1048608 | tf_op jit(solution)/shard_map/ppermute | solution.py:342
  71.8 4.9 %collective-permute-done.9.taken = bf16[4,2,128,512]{3,2,1,0:T(8,128)(2,1)S(1)} collective-permute-done((bf16[4,2,128,512]{3,2,1,0:T(8,128)(2,1)S(1)}, bf16[4,2,128,512]{3,2,1,0:T(8,128)(2,1)S(1)}, u32[]{:S(2)}, u32[]{:S(2)}) %collective-permute-start.9) | collective-permute-done | bytes 1048608 | tf_op jit(solution)/shard_map/ppermute | solution.py:352
  76.6 1.1 add.1
  77.7 3.9 %all-to-all-start.2 = ((bf16[4,2,128,512]{3,2,1,0:T(8,128)(2,1)}), bf16[4,2,128,512]{3,2,1,0:T(8,128)(2,1)S(1)}, u32[]{:S(2)}, u32[]{:S(2)}) async-start(bf16[4,2,128,512]{3,2,1,0:T(8,128)(2,1)} %add.1), calls=%async_computation.2 | async-start | bytes 2097152 | tf_op jit(solution)/shard_map/all_to_all | solution.py:322
  81.6 3.3 %collective-permute-start.8 = (bf16[4,1024,128]{2,1,0:T(8,128)(2,1)S(1)}, bf16[4,1024,128]{2,1,0:T(8,128)(2,1)S(1)}, u32[]{:S(2)}, u32[]{:S(2)}) collective-permute-start(bf16[4,1024,128]{2,1,0:T(8,128)(2,1)S(1)} %copy-done.1), channel_id=1, source_target_pairs={{0,64},{64,0},{1,65},{65,1},{2,66},{66,2},{3,67},{67,3},{4,68},{68... | collective-permute-start | bytes 3145736 | tf_op jit(solution)/shard_map/ppermute | solution.py:344
  85.0 21.0 %collective-permute-done.8.far.refs_3_ = bf16[4,1024,128]{2,1,0:T(8,128)(2,1)S(1)} collective-permute-done((bf16[4,1024,128]{2,1,0:T(8,128)(2,1)S(1)}, bf16[4,1024,128]{2,1,0:T(8,128)(2,1)S(1)}, u32[]{:S(2)}, u32[]{:S(2)}) %collective-permute-start.8) | collective-permute-done | bytes 1048608 | tf_op jit(solution)/shard_map/ppermute | solution.py:344
  106.0 0.1 spread.1
  106.1 19.9 %all_to_all.25.refs_4_ = bf16[8,128,512]{2,1,0:T(8,128)(2,1)S(1)} all-to-all(bf16[8,128,512]{2,1,0:T(8,128)(2,1)S(1)} %spread.1), channel_id=1, replica_groups=mesh['lg'=4,'lq'=2,'rx'=4,'rc'=2,'ch'=4,'cl'=2] {'lq','rx'}, dimensions={0} | all-to-all | bytes 2097152 | tf_op jit(solution)/shard_map/all_to_all | solution.py:322
  126.0 5.7 %collective-permute-start.10 = (bf16[8,128,512]{2,1,0:T(8,128)(2,1)S(1)}, bf16[8,128,512]{2,1,0:T(8,128)(2,1)S(1)}, u32[]{:S(2)}, u32[]{:S(2)}) collective-permute-start(bf16[8,128,512]{2,1,0:T(8,128)(2,1)S(1)} %all_to_all.25.refs_4_), channel_id=1, source_target_pairs={{0,8},{8,0},{1,9},{9,1},{2,10},{10,2},{3,11},{11,3},{4,12},{12,4},... | collective-permute-start | bytes 3145736 | tf_op jit(solution)/shard_map/ppermute | solution.py:357
  131.7 2.3 %collective-permute-done.10.refs_5_ = bf16[8,128,512]{2,1,0:T(8,128)(2,1)S(1)} collective-permute-done((bf16[8,128,512]{2,1,0:T(8,128)(2,1)S(1)}, bf16[8,128,512]{2,1,0:T(8,128)(2,1)S(1)}, u32[]{:S(2)}, u32[]{:S(2)}) %collective-permute-start.10) | collective-permute-done | bytes 1048608 | tf_op jit(solution)/shard_map/ppermute | solution.py:357
  133.9 4.6 %product.1 = bf16[1024,512]{1,0:T(8,128)(2,1)S(1)} custom-call(bf16[4,1024,128]{2,1,0:T(8,128)(2,1)} %pad_maximum_fusion.first.refs_0_, bf16[4,1024,128]{2,1,0:T(8,128)(2,1)S(1)} %copy-done.1, bf16[4,1024,128]{2,1,0:T(8,128)(2,1)} %collective-permute-done.7.wait.refs_2_, bf16[4,1024,128]{2,1,0:T(8,128)(2,1)S(1)} %collective-permute-done.8.far.refs_3_, ...), custom_call_target="tpu_custom_call" | custom-call | flops 2147483648 | bytes 7340032 | tf_op jit(solution)/shard_map/product/pallas_call | solution.py:279
  138.5 33.7 %all_to_all.26.terms = bf16[8,128,512]{2,1,0:T(8,128)(2,1)S(1)} all-to-all(bf16[8,128,512]{2,1,0:T(8,128)(2,1)S(1)} %bitcast.10), channel_id=1, replica_groups=mesh['lg'=4,'lq'=2,'rx'=4,'rc'=2,'ch'=4,'cl'=2] {'lg','lq'}, dimensions={0} | all-to-all | bytes 2097152 | tf_op jit(solution)/shard_map/all_to_all | solution.py:322
  172.2 1.9 %finish.1 = bf16[128,1024]{1,0:T(8,128)(2,1)} custom-call(s32[64,64]{1,0:T(8,128)S(1)} %copy-done.2, bf16[8,128,512]{2,1,0:T(8,128)(2,1)S(1)} %all_to_all.26.terms), custom_call_target="tpu_custom_call" | custom-call | flops 1048576 | bytes 2097152 | tf_op jit(solution)/shard_map/finish/pallas_call | solution.py:307
  (16 shorter events, 0.0 us)
Async XLA Ops:
  4.4 48.4 %all-to-all-start.1 = ((bf16[8,1552,128]{2,1,0:T(8,128)(2,1)}), bf16[8,1552,128]{2,1,0:T(8,128)(2,1)S(1)}, u32[]{:S(2)}, u32[]{:S(2)}) async-start(bf16[8,1552,128]{2,1,0:T(8,128)(2,1)} %get-tuple-element.14), calls=%async_computation.1 | async-start | bytes 6356992 | tf_op jit(solution)/shard_map/all_to_all | solution.py:322
  14.9 14.5 %collective-permute-start.3 = (bf16[1024,128]{1,0:T(8,128)(2,1)}, bf16[1024,128]{1,0:T(8,128)(2,1)}, u32[]{:S(2)}, u32[]{:S(2)}) collective-permute-start(bf16[1024,128]{1,0:T(8,128)(2,1)} %get-tuple-element.13), channel_id=1, source_target_pairs={{0,2},{1,3},{2,4},{3,5},{4,6},{5,7},{6,0},{7,1},{8,10},{9,11},{10,... | collective-permute-start | bytes 786440 | tf_op jit(solution)/shard_map/ppermute | solution.py:330
  16.8 20.0 %collective-permute-start.1 = (bf16[1024,128]{1,0:T(8,128)(2,1)}, bf16[1024,128]{1,0:T(8,128)(2,1)}, u32[]{:S(2)}, u32[]{:S(2)}) collective-permute-start(bf16[1024,128]{1,0:T(8,128)(2,1)} %get-tuple-element.13), channel_id=1, source_target_pairs={{0,6},{1,7},{2,0},{3,1},{4,2},{5,3},{6,4},{7,5},{8,14},{9,15},{10,... | collective-permute-start | bytes 786440 | tf_op jit(solution)/shard_map/ppermute | solution.py:330
  22.8 21.9 %collective-permute-start.2 = (bf16[1024,128]{1,0:T(8,128)(2,1)}, bf16[1024,128]{1,0:T(8,128)(2,1)}, u32[]{:S(2)}, u32[]{:S(2)}) collective-permute-start(bf16[1024,128]{1,0:T(8,128)(2,1)} %get-tuple-element.13), channel_id=1, source_target_pairs={{0,1},{1,2},{2,3},{3,4},{4,5},{5,6},{6,7},{7,0},{8,9},{9,10},{10,1... | collective-permute-start | bytes 786440 | tf_op jit(solution)/shard_map/ppermute | solution.py:330
  25.9 18.8 %collective-permute-start = (bf16[1024,128]{1,0:T(8,128)(2,1)}, bf16[1024,128]{1,0:T(8,128)(2,1)}, u32[]{:S(2)}, u32[]{:S(2)}) collective-permute-start(bf16[1024,128]{1,0:T(8,128)(2,1)} %get-tuple-element.13), channel_id=1, source_target_pairs={{0,7},{1,0},{2,1},{3,2},{4,3},{5,4},{6,5},{7,6},{8,15},{9,8},{10,9... | collective-permute-start | bytes 786440 | tf_op jit(solution)/shard_map/ppermute | solution.py:330
  29.3 24.8 %collective-permute-start.4 = (bf16[1024,128]{1,0:T(8,128)(2,1)}, bf16[1024,128]{1,0:T(8,128)(2,1)S(1)}, u32[]{:S(2)}, u32[]{:S(2)}) collective-permute-start(bf16[1024,128]{1,0:T(8,128)(2,1)} %collective-permute-done.3), channel_id=1, source_target_pairs={{0,1},{1,2},{2,3},{3,4},{4,5},{5,6},{6,7},{7,0},{8,9},{9,10},{10,1... | collective-permute-start | bytes 786440 | tf_op jit(solution)/shard_map/ppermute | solution.py:330
  38.5 15.7 %collective-permute-start.6 = (bf16[1024,128]{1,0:T(8,128)(2,1)}, bf16[1024,128]{1,0:T(8,128)(2,1)}, u32[]{:S(2)}, u32[]{:S(2)}) collective-permute-start(bf16[1024,128]{1,0:T(8,128)(2,1)} %broadcast_select_fusion), channel_id=1, source_target_pairs={{0,6},{1,7},{2,0},{3,1},{4,2},{5,3},{6,4},{7,5},{8,10},{9,11},{10,... | collective-permute-start | bytes 786440 | tf_op jit(solution)/shard_map/ppermute | solution.py:339
  40.4 15.1 %collective-permute-start.5 = (bf16[1024,128]{1,0:T(8,128)(2,1)}, bf16[1024,128]{1,0:T(8,128)(2,1)}, u32[]{:S(2)}, u32[]{:S(2)}) collective-permute-start(bf16[1024,128]{1,0:T(8,128)(2,1)} %collective-permute-done.1), channel_id=1, source_target_pairs={{0,7},{1,0},{2,1},{3,2},{4,3},{5,4},{6,5},{7,6},{8,15},{9,8},{10,9... | collective-permute-start | bytes 786440 | tf_op jit(solution)/shard_map/ppermute | solution.py:330
  47.1 24.7 %collective-permute-start.7 = (bf16[4,1024,128]{2,1,0:T(8,128)(2,1)}, bf16[4,1024,128]{2,1,0:T(8,128)(2,1)}, u32[]{:S(2)}, u32[]{:S(2)}) collective-permute-start(bf16[4,1024,128]{2,1,0:T(8,128)(2,1)} %pad_maximum_fusion.first.refs_0_), channel_id=1, source_target_pairs={{0,64},{64,0},{1,65},{65,1},{2,66},{66,2},{3,67},{67,3},{4,68},{68... | collective-permute-start | bytes 3145736 | tf_op jit(solution)/shard_map/ppermute | solution.py:342
  54.1 11.4 %copy-start.3 = (bf16[8,512,128]{2,1,0:T(8,128)(2,1)S(1)}, bf16[8,512,128]{2,1,0:T(8,128)(2,1)}, u32[]{:S(2)}) copy-start(bf16[8,512,128]{2,1,0:T(8,128)(2,1)} %get-tuple-element.16.more) | copy-start | bytes 3145732
  59.9 16.8 %collective-permute-start.9 = (bf16[4,2,128,512]{3,2,1,0:T(8,128)(2,1)S(1)}, bf16[4,2,128,512]{3,2,1,0:T(8,128)(2,1)S(1)}, u32[]{:S(2)}, u32[]{:S(2)}) collective-permute-start(bf16[4,2,128,512]{3,2,1,0:T(8,128)(2,1)S(1)} %combine.3), channel_id=1, source_target_pairs={{0,1},{1,0},{2,3},{3,2},{4,5},{5,4},{6,7},{7,6},{8,15},{9,10},{10,... | collective-permute-start | bytes 3145736 | tf_op jit(solution)/shard_map/ppermute | solution.py:352
  65.5 4.3 %copy-start = (bf16[4,1024,128]{2,1,0:T(8,128)(2,1)}, bf16[4,1024,128]{2,1,0:T(8,128)(2,1)S(1)}, u32[]{:S(2)}) copy-start(bf16[4,1024,128]{2,1,0:T(8,128)(2,1)S(1)} %pad_maximum_fusion.1.second.third.refs_1_) | copy-start | bytes 3145732
  71.8 9.9 %copy-start.1 = (bf16[4,1024,128]{2,1,0:T(8,128)(2,1)S(1)}, bf16[4,1024,128]{2,1,0:T(8,128)(2,1)}, u32[]{:S(2)}) copy-start(bf16[4,1024,128]{2,1,0:T(8,128)(2,1)} %copy-done) | copy-start | bytes 3145732
  77.7 28.2 %all-to-all-start.2 = ((bf16[4,2,128,512]{3,2,1,0:T(8,128)(2,1)}), bf16[4,2,128,512]{3,2,1,0:T(8,128)(2,1)S(1)}, u32[]{:S(2)}, u32[]{:S(2)}) async-start(bf16[4,2,128,512]{3,2,1,0:T(8,128)(2,1)} %add.1), calls=%async_computation.2 | async-start | bytes 2097152 | tf_op jit(solution)/shard_map/all_to_all | solution.py:322
  81.6 24.3 %collective-permute-start.8 = (bf16[4,1024,128]{2,1,0:T(8,128)(2,1)S(1)}, bf16[4,1024,128]{2,1,0:T(8,128)(2,1)S(1)}, u32[]{:S(2)}, u32[]{:S(2)}) collective-permute-start(bf16[4,1024,128]{2,1,0:T(8,128)(2,1)S(1)} %copy-done.1), channel_id=1, source_target_pairs={{0,64},{64,0},{1,65},{65,1},{2,66},{66,2},{3,67},{67,3},{4,68},{68... | collective-permute-start | bytes 3145736 | tf_op jit(solution)/shard_map/ppermute | solution.py:344
  126.0 46.3 %copy-start.2 = (s32[64,64]{1,0:T(8,128)S(1)}, s32[64,64]{1,0:T(8,128)}, u32[]{:S(2)}) copy-start(s32[64,64]{1,0:T(8,128)} %pattern.3) | copy-start | bytes 49156
  126.0 7.9 %collective-permute-start.10 = (bf16[8,128,512]{2,1,0:T(8,128)(2,1)S(1)}, bf16[8,128,512]{2,1,0:T(8,128)(2,1)S(1)}, u32[]{:S(2)}, u32[]{:S(2)}) collective-permute-start(bf16[8,128,512]{2,1,0:T(8,128)(2,1)S(1)} %all_to_all.25.refs_4_), channel_id=1, source_target_pairs={{0,8},{8,0},{1,9},{9,1},{2,10},{10,2},{3,11},{11,3},{4,12},{12,4},... | collective-permute-start | bytes 3145736 | tf_op jit(solution)/shard_map/ppermute | solution.py:357

commit v11 on v10

--- a/solution.py
+++ b/solution.py
@@ -205,20 +205,20 @@
     )(got, more, *waits)
 
 
-def add_kernel(keep, taken, wait, out):
+def add_kernel(keep, taken, first, second, out):
     out[...] = keep[...] + taken[...]
 
 
-def add(keep, taken, wait):
+def add(keep, taken, *waits):
     return pl.pallas_call(
         add_kernel,
         out_shape=jax.ShapeDtypeStruct(keep.shape, keep.dtype),
-        in_specs=[pl.BlockSpec(memory_space=pltpu.VMEM)] * 2 + [pl.BlockSpec(memory_space=pl.ANY)],
+        in_specs=[pl.BlockSpec(memory_space=pltpu.VMEM)] * 2 + [pl.BlockSpec(memory_space=pl.ANY)] * 2,
         out_specs=pl.BlockSpec(memory_space=pltpu.VMEM),
         compiler_params=pltpu.CompilerParams(vmem_limit_bytes=SMALL_MIB * MIB),
         cost_estimate=pl.CostEstimate(flops=MIB, bytes_accessed=3 * MIB, transcendentals=0),
         name="add",
-    )(keep, taken, wait)
+    )(keep, taken, *waits)
 
 
 def spread_kernel(parts, far, out):
@@ -340,7 +340,9 @@
     swap = [(0, 1), (1, 0)]
     near = jnp.stack([sparse, one, two, last])
     far = lax.ppermute(near, "lq", swap)
-    near_late = jnp.stack([sixth, fifth, three, four])
+    near_mid = sixth[None]
+    far_mid = lax.ppermute(near_mid, "lq", swap)
+    near_late = jnp.stack([fifth, three, four])
     far_late = lax.ppermute(near_late, "lq", swap)
 
     anyone = jnp.max(got[:, BODY, FLAG].astype(jnp.float32)) > 0
@@ -351,11 +353,11 @@
     odd = [(count + c, count + (c + (1 if c % 2 else -1)) % count) for c in range(count)]
     taken = lax.ppermute(send, ("rc", "ch", "cl"), even + odd)
     keep = combine(True, got, more, near, near_late, near_late)
-    parts = exchange(add(keep, taken, far), "ch")
+    parts = exchange(add(keep, taken, far, far_mid), "ch")
 
     own = exchange(spread(parts, far_late), ("lq", "rx"))
     other = lax.ppermute(own, "rc", swap)
-    term = product_of((near, near_late, far, far_late), own, other)
+    term = product_of((near, near_mid, near_late, far, far_mid, far_late), own, other)
     terms = exchange(term.reshape(SIDE, TILE, -1), ("lg", "lq"))
     return finish(pattern, terms)
 

time: 175 us -> 178 us (1.017)
  starting transfers between devices: 59 us -> 65.4 us
  blocking collectives: 53.6 us -> 50.1 us
    all_to_all x2, waiting for transfers between devices: 2.53 us -> 9.74 us  [exchange(): return lax.all_to_all(values, axes, split_axis=0, concat_axis=0, tiled=True)]
    ppermute x1, waiting for transfers between devices: 21 us -> 15.9 us  [body(): far_late = lax.ppermute(near_late, 'lq', swap)]
    ppermute x1, waiting for transfers between devices: 4.86 us -> 0.01 us  [body(): taken = lax.ppermute(send, ('rc', 'ch', 'cl'), even + odd)]
    ppermute x0 -> x1, waiting for transfers between devices: none -> 3.8 us  [body(): far_mid = lax.ppermute(near_mid, 'lq', swap)]
    all_to_all x2, blocking collectives: 53.6 us -> 50.1 us  [exchange(): return lax.all_to_all(values, axes, split_axis=0, concat_axis=0, tiled=True)]
    ppermute x0 -> x1, starting transfers between devices: none -> 3.12 us  [body(): far_mid = lax.ppermute(near_mid, 'lq', swap)]
    all_to_all x2, starting transfers between devices: 14.3 us -> 17.2 us  [exchange(): return lax.all_to_all(values, axes, split_axis=0, concat_axis=0, tiled=True)]
    ppermute x1, waiting for transfers between devices: 1.87 us -> 0.01 us  [body(): far = lax.ppermute(near, 'lq', swap)]
  transfers between devices with their start and end apart: 13 -> 14, of which waited for: 6 -> 6; matrix products, arithmetic and copies ran while one was open for 3% -> 3% of each run, Pallas kernels for 5% -> 5%
where the time goes in v11:
time: 178 us; the launch traced here: 177 us
  starting transfers between devices  65.4 us (37%)
  blocking collectives  50.1 us (28%)
  waiting for transfers between devices  33.1 us (19%)
  Pallas kernels  21 us (12%)
  other arithmetic  5.78 us (3%)
    all_to_all x2, blocking collectives, exchange(): return lax.all_to_all(values, axes, split_axis=0, concat_axis=0, tiled=True)  50.1 us
    ppermute x6, starting transfers between devices, ahead(): lax.ppermute(block, ('ch', 'cl'), [(c, (c - distance) % SIDE) for c in ra...  26.2 us
    all_to_all x2, starting transfers between devices, exchange(): return lax.all_to_all(values, axes, split_axis=0, concat_axis=0, tiled=True)  17.2 us
    ppermute x1, waiting for transfers between devices, body(): far_late = lax.ppermute(near_late, 'lq', swap)  15.9 us
    all_to_all x2, waiting for transfers between devices, exchange(): return lax.all_to_all(values, axes, split_axis=0, concat_axis=0, tiled=True)  9.74 us
    pallas_call x2, Pallas kernels, combine(): pl.pallas_call(functools.partial(combine_kernel, keeps), out_shape=jax.Sh...  8.86 us
    ppermute x1, starting transfers between devices, body(): other = lax.ppermute(own, 'rc', swap)  5.75 us
    ppermute x1, starting transfers between devices, body(): taken = lax.ppermute(send, ('rc', 'ch', 'cl'), even + odd)  4.76 us
  transfers between devices with their start and end apart: 14, of which 6 were waited for; matrix products, arithmetic and copies ran while one was open for 3% of the time, Pallas kernels for 5%

profile of v11, /device:TPU:1, one launch (start us, length us, event | category | flops | bytes accessed | tf_op | source)
XLA Modules:
  0.0 177.1 jit_solution(10964303067325580834)
XLA Ops:
  0.0 4.4 %pack.1 = (bf16[8,1552,128]{2,1,0:T(8,128)(2,1)}, bf16[8,512,128]{2,1,0:T(8,128)(2,1)}, bf16[1024,128]{1,0:T(8,128)(2,1)}) custom-call(s32[64]{0:T(128)} %bitcast.12, s32[64]{0:T(128)} %slots.1, s32[64,64]{1,0:T(8,128)} %pattern.3, bf16[64,128,128]{2,1,0:T(8,128)(2,1)} %contributions.1, bf16[1024,128]{1,0:T(8,128)(2,1)} %density.1), custom_call_target="tpu_custom_call" | custom-call | bytes 7340032 | tf_op jit(solution)/shard_map/pack/pallas_call | solution.py:86
  4.4 10.5 %all-to-all-start.1 = ((bf16[8,1552,128]{2,1,0:T(8,128)(2,1)}), bf16[8,1552,128]{2,1,0:T(8,128)(2,1)S(1)}, u32[]{:S(2)}, u32[]{:S(2)}) async-start(bf16[8,1552,128]{2,1,0:T(8,128)(2,1)} %get-tuple-element.14), calls=%async_computation.1 | async-start | bytes 6356992 | tf_op jit(solution)/shard_map/all_to_all | solution.py:322
  14.9 1.9 %collective-permute-start.3 = (bf16[1024,128]{1,0:T(8,128)(2,1)}, bf16[1024,128]{1,0:T(8,128)(2,1)}, u32[]{:S(2)}, u32[]{:S(2)}) collective-permute-start(bf16[1024,128]{1,0:T(8,128)(2,1)} %get-tuple-element.13), channel_id=1, source_target_pairs={{0,2},{1,3},{2,4},{3,5},{4,6},{5,7},{6,0},{7,1},{8,10},{9,11},{10,... | collective-permute-start | bytes 786440 | tf_op jit(solution)/shard_map/ppermute | solution.py:330
  16.8 6.0 %collective-permute-start.1 = (bf16[1024,128]{1,0:T(8,128)(2,1)}, bf16[1024,128]{1,0:T(8,128)(2,1)}, u32[]{:S(2)}, u32[]{:S(2)}) collective-permute-start(bf16[1024,128]{1,0:T(8,128)(2,1)} %get-tuple-element.13), channel_id=1, source_target_pairs={{0,6},{1,7},{2,0},{3,1},{4,2},{5,3},{6,4},{7,5},{8,14},{9,15},{10,... | collective-permute-start | bytes 786440 | tf_op jit(solution)/shard_map/ppermute | solution.py:330
  22.8 3.1 %collective-permute-start.2 = (bf16[1024,128]{1,0:T(8,128)(2,1)}, bf16[1024,128]{1,0:T(8,128)(2,1)}, u32[]{:S(2)}, u32[]{:S(2)}) collective-permute-start(bf16[1024,128]{1,0:T(8,128)(2,1)} %get-tuple-element.13), channel_id=1, source_target_pairs={{0,1},{1,2},{2,3},{3,4},{4,5},{5,6},{6,7},{7,0},{8,9},{9,10},{10,1... | collective-permute-start | bytes 786440 | tf_op jit(solution)/shard_map/ppermute | solution.py:330
  25.9 3.4 %collective-permute-start = (bf16[1024,128]{1,0:T(8,128)(2,1)}, bf16[1024,128]{1,0:T(8,128)(2,1)}, u32[]{:S(2)}, u32[]{:S(2)}) collective-permute-start(bf16[1024,128]{1,0:T(8,128)(2,1)} %get-tuple-element.13), channel_id=1, source_target_pairs={{0,7},{1,0},{2,1},{3,2},{4,3},{5,4},{6,5},{7,6},{8,15},{9,8},{10,9... | collective-permute-start | bytes 786440 | tf_op jit(solution)/shard_map/ppermute | solution.py:330
  29.4 7.4 %collective-permute-start.4 = (bf16[1024,128]{1,0:T(8,128)(2,1)}, bf16[1024,128]{1,0:T(8,128)(2,1)S(1)}, u32[]{:S(2)}, u32[]{:S(2)}) collective-permute-start(bf16[1024,128]{1,0:T(8,128)(2,1)} %collective-permute-done.3), channel_id=1, source_target_pairs={{0,1},{1,2},{2,3},{3,4},{4,5},{5,6},{6,7},{7,0},{8,9},{9,10},{10,1... | collective-permute-start | bytes 786440 | tf_op jit(solution)/shard_map/ppermute | solution.py:330
  36.8 1.7 broadcast_select_fusion
  38.5 1.9 %collective-permute-start.6 = (bf16[1024,128]{1,0:T(8,128)(2,1)}, bf16[1024,128]{1,0:T(8,128)(2,1)}, u32[]{:S(2)}, u32[]{:S(2)}) collective-permute-start(bf16[1024,128]{1,0:T(8,128)(2,1)} %broadcast_select_fusion), channel_id=1, source_target_pairs={{0,6},{1,7},{2,0},{3,1},{4,2},{5,3},{6,4},{7,5},{8,10},{9,11},{10,... | collective-permute-start | bytes 786440 | tf_op jit(solution)/shard_map/ppermute | solution.py:339
  40.4 4.3 %collective-permute-start.5 = (bf16[1024,128]{1,0:T(8,128)(2,1)}, bf16[1024,128]{1,0:T(8,128)(2,1)}, u32[]{:S(2)}, u32[]{:S(2)}) collective-permute-start(bf16[1024,128]{1,0:T(8,128)(2,1)} %collective-permute-done.1), channel_id=1, source_target_pairs={{0,7},{1,0},{2,1},{3,2},{4,3},{5,4},{6,5},{7,6},{8,15},{9,8},{10,9... | collective-permute-start | bytes 786440 | tf_op jit(solution)/shard_map/ppermute | solution.py:330
  44.8 2.3 %pad_maximum_fusion.first.refs_0_ = bf16[4,1024,128]{2,1,0:T(8,128)(2,1)} fusion(bf16[1,1024,128]{2,1,0:T(8,128)(2,1)} %bitcast.4, bf16[1,1024,128]{2,1,0:T(8,128)(2,1)} %bitcast.3, bf16[1,1024,128]{2,1,0:T(8,128)(2,1)} %bitcast.2, bf16[1,1024,128]{2,1,0:T(8,128)(2,1)} %bitcast.1), kind=kLoop, calls=%fused_computation | loop fusion | flops 1572864 | bytes 2097152 | tf_op jit(solution)/shard_map/stack | solution.py:341
  47.0 3.2 %collective-permute-start.7 = (bf16[4,1024,128]{2,1,0:T(8,128)(2,1)}, bf16[4,1024,128]{2,1,0:T(8,128)(2,1)}, u32[]{:S(2)}, u32[]{:S(2)}) collective-permute-start(bf16[4,1024,128]{2,1,0:T(8,128)(2,1)} %pad_maximum_fusion.first.refs_0_), channel_id=1, source_target_pairs={{0,64},{64,0},{1,65},{65,1},{2,66},{66,2},{3,67},{67,3},{4,68},{68... | collective-permute-start | bytes 3145736 | tf_op jit(solution)/shard_map/ppermute | solution.py:342
  50.2 2.6 %all-to-all-done.1.got = bf16[8,1552,128]{2,1,0:T(8,128)(2,1)S(1)} async-done(((bf16[8,1552,128]{2,1,0:T(8,128)(2,1)}), bf16[8,1552,128]{2,1,0:T(8,128)(2,1)S(1)}, u32[]{:S(2)}, u32[]{:S(2)}) %all-to-all-start.1) | async-done | bytes 3178528 | tf_op jit(solution)/shard_map/all_to_all | solution.py:322
  54.2 1.4 collective-permute-done.5.first
  55.6 4.4 %combine.3 = bf16[4,2,128,512]{3,2,1,0:T(8,128)(2,1)S(1)} custom-call(bf16[8,1552,128]{2,1,0:T(8,128)(2,1)S(1)} %all-to-all-done.1.got, bf16[8,512,128]{2,1,0:T(8,128)(2,1)} %get-tuple-element.16.more, bf16[1024,128]{1,0:T(8,128)(2,1)} %collective-permute-done.5.first, bf16[1024,128]{1,0:T(8,128)(2,1)} %collective-permute-done.6.second, ...), custom_call_target="tpu_custom_call" | custom-call | flops 2097152 | bytes 4194304 | tf_op jit(solution)/shard_map/combine/pallas_call | solution.py:183
  60.0 4.8 %collective-permute-start.10 = (bf16[4,2,128,512]{3,2,1,0:T(8,128)(2,1)S(1)}, bf16[4,2,128,512]{3,2,1,0:T(8,128)(2,1)S(1)}, u32[]{:S(2)}, u32[]{:S(2)}) collective-permute-start(bf16[4,2,128,512]{3,2,1,0:T(8,128)(2,1)S(1)} %combine.3), channel_id=1, source_target_pairs={{0,1},{1,0},{2,3},{3,2},{4,5},{5,4},{6,7},{7,6},{8,15},{9,10},{10,... | collective-permute-start | bytes 3145736 | tf_op jit(solution)/shard_map/ppermute | solution.py:354
  64.8 3.1 %collective-permute-start.8 = (bf16[1,1024,128]{2,1,0:T(8,128)(2,1)}, bf16[1,1024,128]{2,1,0:T(8,128)(2,1)S(1)}, u32[]{:S(2)}, u32[]{:S(2)}) collective-permute-start(bf16[1,1024,128]{2,1,0:T(8,128)(2,1)} %bitcast.5.refs_1_), channel_id=1, source_target_pairs={{0,64},{64,0},{1,65},{65,1},{2,66},{66,2},{3,67},{67,3},{4,68},{68... | collective-permute-start | bytes 786440 | tf_op jit(solution)/shard_map/ppermute | solution.py:344
  67.9 1.1 pad_maximum_fusion.1.second.third.refs_2_
  69.0 4.5 %combine.2.keep = bf16[4,2,128,512]{3,2,1,0:T(8,128)(2,1)S(1)} custom-call(bf16[8,1552,128]{2,1,0:T(8,128)(2,1)S(1)} %all-to-all-done.1.got, bf16[8,512,128]{2,1,0:T(8,128)(2,1)S(1)} %copy-done.5, bf16[4,1024,128]{2,1,0:T(8,128)(2,1)} %pad_maximum_fusion.first.refs_0_, bf16[3,1024,128]{2,1,0:T(8,128)(2,1)S(1)} %pad_maximum_fusion.1.second.third.refs_2_, ...), custom_call_target="tpu_custom_call" | custom-call | flops 2097152 | bytes 4194304 | tf_op jit(solution)/shard_map/combine/pallas_call | solution.py:183
  73.5 3.8 %collective-permute-done.8.second.refs_4_ = bf16[1,1024,128]{2,1,0:T(8,128)(2,1)S(1)} collective-permute-done((bf16[1,1024,128]{2,1,0:T(8,128)(2,1)}, bf16[1,1024,128]{2,1,0:T(8,128)(2,1)S(1)}, u32[]{:S(2)}, u32[]{:S(2)}) %collective-permute-start.8) | collective-permute-done | bytes 262176 | tf_op jit(solution)/shard_map/ppermute | solution.py:344
  77.3 1.1 add.1
  78.4 0.7 copy-done.2
  79.1 6.8 %all-to-all-start.2 = ((bf16[4,2,128,512]{3,2,1,0:T(8,128)(2,1)}), bf16[4,2,128,512]{3,2,1,0:T(8,128)(2,1)S(1)}, u32[]{:S(2)}, u32[]{:S(2)}) async-start(bf16[4,2,128,512]{3,2,1,0:T(8,128)(2,1)} %add.1), calls=%async_computation.2 | async-start | bytes 2097152 | tf_op jit(solution)/shard_map/all_to_all | solution.py:322
  85.9 3.3 %collective-permute-start.9 = (bf16[3,1024,128]{2,1,0:T(8,128)(2,1)S(1)}, bf16[3,1024,128]{2,1,0:T(8,128)(2,1)S(1)}, u32[]{:S(2)}, u32[]{:S(2)}) collective-permute-start(bf16[3,1024,128]{2,1,0:T(8,128)(2,1)S(1)} %copy-done.1), channel_id=1, source_target_pairs={{0,64},{64,0},{1,65},{65,1},{2,66},{66,2},{3,67},{67,3},{4,68},{68... | collective-permute-start | bytes 2359304 | tf_op jit(solution)/shard_map/ppermute | solution.py:346
  89.2 15.9 %collective-permute-done.9.far.refs_5_ = bf16[3,1024,128]{2,1,0:T(8,128)(2,1)S(1)} collective-permute-done((bf16[3,1024,128]{2,1,0:T(8,128)(2,1)S(1)}, bf16[3,1024,128]{2,1,0:T(8,128)(2,1)S(1)}, u32[]{:S(2)}, u32[]{:S(2)}) %collective-permute-start.9) | collective-permute-done | bytes 786464 | tf_op jit(solution)/shard_map/ppermute | solution.py:346
  105.1 7.2 %all-to-all-done.2.parts = bf16[4,2,128,512]{3,2,1,0:T(8,128)(2,1)S(1)} async-done(((bf16[4,2,128,512]{3,2,1,0:T(8,128)(2,1)}), bf16[4,2,128,512]{3,2,1,0:T(8,128)(2,1)S(1)}, u32[]{:S(2)}, u32[]{:S(2)}) %all-to-all-start.2) | async-done | bytes 1048608 | tf_op jit(solution)/shard_map/all_to_all | solution.py:322
  112.3 15.6 %all_to_all.25.refs_6_ = bf16[8,128,512]{2,1,0:T(8,128)(2,1)S(1)} all-to-all(bf16[8,128,512]{2,1,0:T(8,128)(2,1)S(1)} %spread.1), channel_id=1, replica_groups=mesh['lg'=4,'lq'=2,'rx'=4,'rc'=2,'ch'=4,'cl'=2] {'lq','rx'}, dimensions={0} | all-to-all | bytes 2097152 | tf_op jit(solution)/shard_map/all_to_all | solution.py:322
  128.0 5.8 %collective-permute-start.11 = (bf16[8,128,512]{2,1,0:T(8,128)(2,1)S(1)}, bf16[8,128,512]{2,1,0:T(8,128)(2,1)S(1)}, u32[]{:S(2)}, u32[]{:S(2)}) collective-permute-start(bf16[8,128,512]{2,1,0:T(8,128)(2,1)S(1)} %all_to_all.25.refs_6_), channel_id=1, source_target_pairs={{0,8},{8,0},{1,9},{9,1},{2,10},{10,2},{3,11},{11,3},{4,12},{12,4},... | collective-permute-start | bytes 3145736 | tf_op jit(solution)/shard_map/ppermute | solution.py:359
  133.7 2.3 %collective-permute-done.11.refs_7_ = bf16[8,128,512]{2,1,0:T(8,128)(2,1)S(1)} collective-permute-done((bf16[8,128,512]{2,1,0:T(8,128)(2,1)S(1)}, bf16[8,128,512]{2,1,0:T(8,128)(2,1)S(1)}, u32[]{:S(2)}, u32[]{:S(2)}) %collective-permute-start.11) | collective-permute-done | bytes 1048608 | tf_op jit(solution)/shard_map/ppermute | solution.py:359
  136.0 4.6 %product.1 = bf16[1024,512]{1,0:T(8,128)(2,1)S(1)} custom-call(bf16[4,1024,128]{2,1,0:T(8,128)(2,1)} %pad_maximum_fusion.first.refs_0_, bf16[1,1024,128]{2,1,0:T(8,128)(2,1)} %bitcast.5.refs_1_, bf16[3,1024,128]{2,1,0:T(8,128)(2,1)S(1)} %copy-done.1, bf16[4,1024,128]{2,1,0:T(8,128)(2,1)} %collective-permute-done.7.first.refs_3_, ...), custom_call_target="tpu_custom_call" | custom-call | flops 2147483648 | bytes 7340032 | tf_op jit(solution)/shard_map/product/pallas_call | solution.py:279
  140.6 34.5 %all_to_all.26.terms = bf16[8,128,512]{2,1,0:T(8,128)(2,1)S(1)} all-to-all(bf16[8,128,512]{2,1,0:T(8,128)(2,1)S(1)} %bitcast.10), channel_id=1, replica_groups=mesh['lg'=4,'lq'=2,'rx'=4,'rc'=2,'ch'=4,'cl'=2] {'lg','lq'}, dimensions={0} | all-to-all | bytes 2097152 | tf_op jit(solution)/shard_map/all_to_all | solution.py:322
  175.1 1.9 %finish.1 = bf16[128,1024]{1,0:T(8,128)(2,1)} custom-call(s32[64,64]{1,0:T(8,128)S(1)} %copy-done.4, bf16[8,128,512]{2,1,0:T(8,128)(2,1)S(1)} %all_to_all.26.terms), custom_call_target="tpu_custom_call" | custom-call | flops 1048576 | bytes 2097152 | tf_op jit(solution)/shard_map/finish/pallas_call | solution.py:307
  (22 shorter events, 0.9 us)
Async XLA Ops:
  4.4 48.4 %all-to-all-start.1 = ((bf16[8,1552,128]{2,1,0:T(8,128)(2,1)}), bf16[8,1552,128]{2,1,0:T(8,128)(2,1)S(1)}, u32[]{:S(2)}, u32[]{:S(2)}) async-start(bf16[8,1552,128]{2,1,0:T(8,128)(2,1)} %get-tuple-element.14), calls=%async_computation.1 | async-start | bytes 6356992 | tf_op jit(solution)/shard_map/all_to_all | solution.py:322
  14.9 14.5 %collective-permute-start.3 = (bf16[1024,128]{1,0:T(8,128)(2,1)}, bf16[1024,128]{1,0:T(8,128)(2,1)}, u32[]{:S(2)}, u32[]{:S(2)}) collective-permute-start(bf16[1024,128]{1,0:T(8,128)(2,1)} %get-tuple-element.13), channel_id=1, source_target_pairs={{0,2},{1,3},{2,4},{3,5},{4,6},{5,7},{6,0},{7,1},{8,10},{9,11},{10,... | collective-permute-start | bytes 786440 | tf_op jit(solution)/shard_map/ppermute | solution.py:330
  16.8 20.0 %collective-permute-start.1 = (bf16[1024,128]{1,0:T(8,128)(2,1)}, bf16[1024,128]{1,0:T(8,128)(2,1)}, u32[]{:S(2)}, u32[]{:S(2)}) collective-permute-start(bf16[1024,128]{1,0:T(8,128)(2,1)} %get-tuple-element.13), channel_id=1, source_target_pairs={{0,6},{1,7},{2,0},{3,1},{4,2},{5,3},{6,4},{7,5},{8,14},{9,15},{10,... | collective-permute-start | bytes 786440 | tf_op jit(solution)/shard_map/ppermute | solution.py:330
  22.8 21.9 %collective-permute-start.2 = (bf16[1024,128]{1,0:T(8,128)(2,1)}, bf16[1024,128]{1,0:T(8,128)(2,1)}, u32[]{:S(2)}, u32[]{:S(2)}) collective-permute-start(bf16[1024,128]{1,0:T(8,128)(2,1)} %get-tuple-element.13), channel_id=1, source_target_pairs={{0,1},{1,2},{2,3},{3,4},{4,5},{5,6},{6,7},{7,0},{8,9},{9,10},{10,1... | collective-permute-start | bytes 786440 | tf_op jit(solution)/shard_map/ppermute | solution.py:330
  25.9 18.8 %collective-permute-start = (bf16[1024,128]{1,0:T(8,128)(2,1)}, bf16[1024,128]{1,0:T(8,128)(2,1)}, u32[]{:S(2)}, u32[]{:S(2)}) collective-permute-start(bf16[1024,128]{1,0:T(8,128)(2,1)} %get-tuple-element.13), channel_id=1, source_target_pairs={{0,7},{1,0},{2,1},{3,2},{4,3},{5,4},{6,5},{7,6},{8,15},{9,8},{10,9... | collective-permute-start | bytes 786440 | tf_op jit(solution)/shard_map/ppermute | solution.py:330
  29.4 24.8 %collective-permute-start.4 = (bf16[1024,128]{1,0:T(8,128)(2,1)}, bf16[1024,128]{1,0:T(8,128)(2,1)S(1)}, u32[]{:S(2)}, u32[]{:S(2)}) collective-permute-start(bf16[1024,128]{1,0:T(8,128)(2,1)} %collective-permute-done.3), channel_id=1, source_target_pairs={{0,1},{1,2},{2,3},{3,4},{4,5},{5,6},{6,7},{7,0},{8,9},{9,10},{10,1... | collective-permute-start | bytes 786440 | tf_op jit(solution)/shard_map/ppermute | solution.py:330
  38.5 15.7 %collective-permute-start.6 = (bf16[1024,128]{1,0:T(8,128)(2,1)}, bf16[1024,128]{1,0:T(8,128)(2,1)}, u32[]{:S(2)}, u32[]{:S(2)}) collective-permute-start(bf16[1024,128]{1,0:T(8,128)(2,1)} %broadcast_select_fusion), channel_id=1, source_target_pairs={{0,6},{1,7},{2,0},{3,1},{4,2},{5,3},{6,4},{7,5},{8,10},{9,11},{10,... | collective-permute-start | bytes 786440 | tf_op jit(solution)/shard_map/ppermute | solution.py:339
  40.4 15.2 %collective-permute-start.5 = (bf16[1024,128]{1,0:T(8,128)(2,1)}, bf16[1024,128]{1,0:T(8,128)(2,1)}, u32[]{:S(2)}, u32[]{:S(2)}) collective-permute-start(bf16[1024,128]{1,0:T(8,128)(2,1)} %collective-permute-done.1), channel_id=1, source_target_pairs={{0,7},{1,0},{2,1},{3,2},{4,3},{5,4},{6,5},{7,6},{8,15},{9,8},{10,9... | collective-permute-start | bytes 786440 | tf_op jit(solution)/shard_map/ppermute | solution.py:330
  47.0 30.3 %collective-permute-start.7 = (bf16[4,1024,128]{2,1,0:T(8,128)(2,1)}, bf16[4,1024,128]{2,1,0:T(8,128)(2,1)}, u32[]{:S(2)}, u32[]{:S(2)}) collective-permute-start(bf16[4,1024,128]{2,1,0:T(8,128)(2,1)} %pad_maximum_fusion.first.refs_0_), channel_id=1, source_target_pairs={{0,64},{64,0},{1,65},{65,1},{2,66},{66,2},{3,67},{67,3},{4,68},{68... | collective-permute-start | bytes 3145736 | tf_op jit(solution)/shard_map/ppermute | solution.py:342
  54.2 14.8 %copy-start.5 = (bf16[8,512,128]{2,1,0:T(8,128)(2,1)S(1)}, bf16[8,512,128]{2,1,0:T(8,128)(2,1)}, u32[]{:S(2)}) copy-start(bf16[8,512,128]{2,1,0:T(8,128)(2,1)} %get-tuple-element.16.more) | copy-start | bytes 3145732
  60.0 17.3 %collective-permute-start.10 = (bf16[4,2,128,512]{3,2,1,0:T(8,128)(2,1)S(1)}, bf16[4,2,128,512]{3,2,1,0:T(8,128)(2,1)S(1)}, u32[]{:S(2)}, u32[]{:S(2)}) collective-permute-start(bf16[4,2,128,512]{3,2,1,0:T(8,128)(2,1)S(1)} %combine.3), channel_id=1, source_target_pairs={{0,1},{1,0},{2,3},{3,2},{4,5},{5,4},{6,7},{7,6},{8,15},{9,10},{10,... | collective-permute-start | bytes 3145736 | tf_op jit(solution)/shard_map/ppermute | solution.py:354
  64.8 12.6 %collective-permute-start.8 = (bf16[1,1024,128]{2,1,0:T(8,128)(2,1)}, bf16[1,1024,128]{2,1,0:T(8,128)(2,1)S(1)}, u32[]{:S(2)}, u32[]{:S(2)}) collective-permute-start(bf16[1,1024,128]{2,1,0:T(8,128)(2,1)} %bitcast.5.refs_1_), channel_id=1, source_target_pairs={{0,64},{64,0},{1,65},{65,1},{2,66},{66,2},{3,67},{67,3},{4,68},{68... | collective-permute-start | bytes 786440 | tf_op jit(solution)/shard_map/ppermute | solution.py:344
  69.0 4.5 %copy-start = (bf16[3,1024,128]{2,1,0:T(8,128)(2,1)}, bf16[3,1024,128]{2,1,0:T(8,128)(2,1)S(1)}, u32[]{:S(2)}) copy-start(bf16[3,1024,128]{2,1,0:T(8,128)(2,1)S(1)} %pad_maximum_fusion.1.second.third.refs_2_) | copy-start | bytes 2359300
  77.3 8.6 %copy-start.1 = (bf16[3,1024,128]{2,1,0:T(8,128)(2,1)S(1)}, bf16[3,1024,128]{2,1,0:T(8,128)(2,1)}, u32[]{:S(2)}) copy-start(bf16[3,1024,128]{2,1,0:T(8,128)(2,1)} %copy-done) | copy-start | bytes 2359300
  78.4 0.7 copy-start.2
  79.1 33.1 %all-to-all-start.2 = ((bf16[4,2,128,512]{3,2,1,0:T(8,128)(2,1)}), bf16[4,2,128,512]{3,2,1,0:T(8,128)(2,1)S(1)}, u32[]{:S(2)}, u32[]{:S(2)}) async-start(bf16[4,2,128,512]{3,2,1,0:T(8,128)(2,1)} %add.1), calls=%async_computation.2 | async-start | bytes 2097152 | tf_op jit(solution)/shard_map/all_to_all | solution.py:322
  85.9 50.1 %copy-start.3 = (bf16[1,1024,128]{2,1,0:T(8,128)(2,1)S(1)}, bf16[1,1024,128]{2,1,0:T(8,128)(2,1)}, u32[]{:S(2)}) copy-start(bf16[1,1024,128]{2,1,0:T(8,128)(2,1)} %copy-done.2) | copy-start | bytes 786436
  85.9 19.1 %collective-permute-start.9 = (bf16[3,1024,128]{2,1,0:T(8,128)(2,1)S(1)}, bf16[3,1024,128]{2,1,0:T(8,128)(2,1)S(1)}, u32[]{:S(2)}, u32[]{:S(2)}) collective-permute-start(bf16[3,1024,128]{2,1,0:T(8,128)(2,1)S(1)} %copy-done.1), channel_id=1, source_target_pairs={{0,64},{64,0},{1,65},{65,1},{2,66},{66,2},{3,67},{67,3},{4,68},{68... | collective-permute-start | bytes 2359304 | tf_op jit(solution)/shard_map/ppermute | solution.py:346
  128.0 47.1 %copy-start.4 = (s32[64,64]{1,0:T(8,128)S(1)}, s32[64,64]{1,0:T(8,128)}, u32[]{:S(2)}) copy-start(s32[64,64]{1,0:T(8,128)} %pattern.3) | copy-start | bytes 49156
  128.0 8.0 %collective-permute-start.11 = (bf16[8,128,512]{2,1,0:T(8,128)(2,1)S(1)}, bf16[8,128,512]{2,1,0:T(8,128)(2,1)S(1)}, u32[]{:S(2)}, u32[]{:S(2)}) collective-permute-start(bf16[8,128,512]{2,1,0:T(8,128)(2,1)S(1)} %all_to_all.25.refs_6_), channel_id=1, source_target_pairs={{0,8},{8,0},{1,9},{9,1},{2,10},{10,2},{3,11},{11,3},{4,12},{12,4},... | collective-permute-start | bytes 3145736 | tf_op jit(solution)/shard_map/ppermute | solution.py:359

commit v12 on v10

--- a/solution.py
+++ b/solution.py
@@ -338,9 +338,9 @@
     opposite = jnp.where(lax.axis_index("rc") == 0, two, sixth)
     four = lax.ppermute(opposite, ("rc", "ch", "cl"), down + up)
     swap = [(0, 1), (1, 0)]
-    near = jnp.stack([sparse, one, two, last])
+    near = jnp.stack([sparse, one, two, last, sixth])
     far = lax.ppermute(near, "lq", swap)
-    near_late = jnp.stack([sixth, fifth, three, four])
+    near_late = jnp.stack([fifth, three, four])
     far_late = lax.ppermute(near_late, "lq", swap)
 
     anyone = jnp.max(got[:, BODY, FLAG].astype(jnp.float32)) > 0

time: 175 us -> 188 us (1.074)
  the two profiles are of different devices: /device:TPU:1 before, /device:TPU:64 now
where the time goes in v12:
time: 188 us; the launch traced here: 187 us
  blocking collectives  55.7 us (30%)
  starting transfers between devices  48.9 us (26%)
  waiting for transfers between devices  46.4 us (25%)
  Pallas kernels  21.7 us (12%)
  local copies, waits for them, and re-layouts  10.4 us (6%)
  other arithmetic  2.57 us (1%)
    all_to_all x2, blocking collectives, exchange(): return lax.all_to_all(values, axes, split_axis=0, concat_axis=0, tiled=True)  55.7 us
    ppermute x6, starting transfers between devices, ahead(): lax.ppermute(block, ('ch', 'cl'), [(c, (c - distance) % SIDE) for c in ra...  24.8 us
    ppermute x1, waiting for transfers between devices, body(): far_late = lax.ppermute(near_late, 'lq', swap)  17.4 us
    ppermute x1, waiting for transfers between devices, body(): far = lax.ppermute(near, 'lq', swap)  12.2 us
    all_to_all x2, starting transfers between devices, exchange(): return lax.all_to_all(values, axes, split_axis=0, concat_axis=0, tiled=True)  9.63 us
    pallas_call x2, Pallas kernels, combine(): pl.pallas_call(functools.partial(combine_kernel, keeps), out_shape=jax.Sh...  9.6 us
    unnamed x24, local copies, waits for them, and re-layouts  8.76 us
    ppermute x6, waiting for transfers between devices, ahead(): lax.ppermute(block, ('ch', 'cl'), [(c, (c - distance) % SIDE) for c in ra...  8.34 us
  transfers between devices with their start and end apart: 13, of which 6 were waited for; matrix products, arithmetic and copies ran while one was open for 6% of the time, Pallas kernels for 5%

profile of v12, /device:TPU:64, one launch (start us, length us, event | category | flops | bytes accessed | tf_op | source)
XLA Modules:
  0.0 186.6 jit_solution(16102345949323316133)
XLA Ops:
  0.0 4.4 %pack.1 = (bf16[8,1552,128]{2,1,0:T(8,128)(2,1)}, bf16[8,512,128]{2,1,0:T(8,128)(2,1)}, bf16[1024,128]{1,0:T(8,128)(2,1)}) custom-call(s32[64]{0:T(128)} %bitcast.17, s32[64]{0:T(128)} %slots.1, s32[64,64]{1,0:T(8,128)} %pattern.3, bf16[64,128,128]{2,1,0:T(8,128)(2,1)} %contributions.1, bf16[1024,128]{1,0:T(8,128)(2,1)} %density.1), custom_call_target="tpu_custom_call" | custom-call | bytes 7340032 | tf_op jit(solution)/shard_map/pack/pallas_call | solution.py:86
  4.4 4.3 %all-to-all-start.1 = ((bf16[8,1552,128]{2,1,0:T(8,128)(2,1)}), bf16[8,1552,128]{2,1,0:T(8,128)(2,1)S(1)}, u32[]{:S(2)}, u32[]{:S(2)}) async-start(bf16[8,1552,128]{2,1,0:T(8,128)(2,1)} %get-tuple-element.14), calls=%async_computation.1 | async-start | bytes 6356992 | tf_op jit(solution)/shard_map/all_to_all | solution.py:322
  8.7 10.1 %collective-permute-start.1 = (bf16[1024,128]{1,0:T(8,128)(2,1)}, bf16[1024,128]{1,0:T(8,128)(2,1)S(1)}, u32[]{:S(2)}, u32[]{:S(2)}) collective-permute-start(bf16[1024,128]{1,0:T(8,128)(2,1)} %get-tuple-element.13), channel_id=1, source_target_pairs={{0,6},{1,7},{2,0},{3,1},{4,2},{5,3},{6,4},{7,5},{8,14},{9,15},{10,... | collective-permute-start | bytes 786440 | tf_op jit(solution)/shard_map/ppermute | solution.py:330
  18.8 1.9 %collective-permute-start.3 = (bf16[1024,128]{1,0:T(8,128)(2,1)}, bf16[1024,128]{1,0:T(8,128)(2,1)}, u32[]{:S(2)}, u32[]{:S(2)}) collective-permute-start(bf16[1024,128]{1,0:T(8,128)(2,1)} %get-tuple-element.13), channel_id=1, source_target_pairs={{0,2},{1,3},{2,4},{3,5},{4,6},{5,7},{6,0},{7,1},{8,10},{9,11},{10,... | collective-permute-start | bytes 786440 | tf_op jit(solution)/shard_map/ppermute | solution.py:330
  20.7 2.4 %collective-permute-start = (bf16[1024,128]{1,0:T(8,128)(2,1)}, bf16[1024,128]{1,0:T(8,128)(2,1)}, u32[]{:S(2)}, u32[]{:S(2)}) collective-permute-start(bf16[1024,128]{1,0:T(8,128)(2,1)} %get-tuple-element.13), channel_id=1, source_target_pairs={{0,7},{1,0},{2,1},{3,2},{4,3},{5,4},{6,5},{7,6},{8,15},{9,8},{10,9... | collective-permute-start | bytes 786440 | tf_op jit(solution)/shard_map/ppermute | solution.py:330
  23.2 3.4 %collective-permute-start.2 = (bf16[1024,128]{1,0:T(8,128)(2,1)}, bf16[1024,128]{1,0:T(8,128)(2,1)}, u32[]{:S(2)}, u32[]{:S(2)}) collective-permute-start(bf16[1024,128]{1,0:T(8,128)(2,1)} %get-tuple-element.13), channel_id=1, source_target_pairs={{0,1},{1,2},{2,3},{3,4},{4,5},{5,6},{6,7},{7,0},{8,9},{9,10},{10,1... | collective-permute-start | bytes 786440 | tf_op jit(solution)/shard_map/ppermute | solution.py:330
  26.6 1.7 bitcast_dynamic-update-slice_fusion.4
  28.3 2.0 %collective-permute-done.1 = bf16[1024,128]{1,0:T(8,128)(2,1)S(1)} collective-permute-done((bf16[1024,128]{1,0:T(8,128)(2,1)}, bf16[1024,128]{1,0:T(8,128)(2,1)S(1)}, u32[]{:S(2)}, u32[]{:S(2)}) %collective-permute-start.1) | collective-permute-done | bytes 262176 | tf_op jit(solution)/shard_map/ppermute | solution.py:330
  30.3 6.3 %collective-permute-done.3 = bf16[1024,128]{1,0:T(8,128)(2,1)} collective-permute-done((bf16[1024,128]{1,0:T(8,128)(2,1)}, bf16[1024,128]{1,0:T(8,128)(2,1)}, u32[]{:S(2)}, u32[]{:S(2)}) %collective-permute-start.3) | collective-permute-done | bytes 262176 | tf_op jit(solution)/shard_map/ppermute | solution.py:330
  37.4 1.9 %collective-permute-start.6 = (bf16[1024,128]{1,0:T(8,128)(2,1)}, bf16[1024,128]{1,0:T(8,128)(2,1)S(1)}, u32[]{:S(2)}, u32[]{:S(2)}) collective-permute-start(bf16[1024,128]{1,0:T(8,128)(2,1)} %broadcast_select_fusion), channel_id=1, source_target_pairs={{0,6},{1,7},{2,0},{3,1},{4,2},{5,3},{6,4},{7,5},{8,10},{9,11},{10,... | collective-permute-start | bytes 786440 | tf_op jit(solution)/shard_map/ppermute | solution.py:339
  39.3 5.1 %collective-permute-start.4 = (bf16[1024,128]{1,0:T(8,128)(2,1)}, bf16[1024,128]{1,0:T(8,128)(2,1)}, u32[]{:S(2)}, u32[]{:S(2)}) collective-permute-start(bf16[1024,128]{1,0:T(8,128)(2,1)} %collective-permute-done.3), channel_id=1, source_target_pairs={{0,1},{1,2},{2,3},{3,4},{4,5},{5,6},{6,7},{7,0},{8,9},{9,10},{10,1... | collective-permute-start | bytes 786440 | tf_op jit(solution)/shard_map/ppermute | solution.py:330
  44.4 1.9 %collective-permute-start.5 = (bf16[1024,128]{1,0:T(8,128)(2,1)}, bf16[1024,128]{1,0:T(8,128)(2,1)}, u32[]{:S(2)}, u32[]{:S(2)}) collective-permute-start(bf16[1024,128]{1,0:T(8,128)(2,1)} %copy-done.10), channel_id=1, source_target_pairs={{0,7},{1,0},{2,1},{3,2},{4,3},{5,4},{6,5},{7,6},{8,15},{9,8},{10,9... | collective-permute-start | bytes 786440 | tf_op jit(solution)/shard_map/ppermute | solution.py:330
  46.3 1.7 bitcast_dynamic-update-slice_fusion.3
  48.0 1.7 bitcast_dynamic-update-slice_fusion.2
  49.7 1.7 bitcast_dynamic-update-slice_fusion.1
  51.3 1.7 bitcast_dynamic-update-slice_fusion.first.refs_0_
  53.0 3.5 %collective-permute-start.7 = (bf16[5,1024,128]{2,1,0:T(8,128)(2,1)}, bf16[5,1024,128]{2,1,0:T(8,128)(2,1)}, u32[]{:S(2)}, u32[]{:S(2)}) collective-permute-start(bf16[5,1024,128]{2,1,0:T(8,128)(2,1)} %bitcast_dynamic-update-slice_fusion.first.refs_0_), channel_id=1, source_target_pairs={{0,64},{64,0},{1,65},{65,1},{2,66},{66,2},{3,67},{67,3},{4,68},{68... | collective-permute-start | bytes 3932168 | tf_op jit(solution)/shard_map/ppermute | solution.py:342
  57.9 4.8 %combine.3 = bf16[4,2,128,512]{3,2,1,0:T(8,128)(2,1)S(1)} custom-call(bf16[8,1552,128]{2,1,0:T(8,128)(2,1)S(1)} %all-to-all-done.1.got, bf16[8,512,128]{2,1,0:T(8,128)(2,1)} %get-tuple-element.16.more, bf16[1024,128]{1,0:T(8,128)(2,1)} %collective-permute-done.5.first, bf16[1024,128]{1,0:T(8,128)(2,1)S(1)} %collective-permute-done.6.second, ...), custom_call_target="tpu_custom_call" | custom-call | flops 2097152 | bytes 4194304 | tf_op jit(solution)/shard_map/combine/pallas_call | solution.py:183
  62.8 3.7 %collective-permute-start.9 = (bf16[4,2,128,512]{3,2,1,0:T(8,128)(2,1)S(1)}, bf16[4,2,128,512]{3,2,1,0:T(8,128)(2,1)S(1)}, u32[]{:S(2)}, u32[]{:S(2)}) collective-permute-start(bf16[4,2,128,512]{3,2,1,0:T(8,128)(2,1)S(1)} %combine.3), channel_id=1, source_target_pairs={{0,1},{1,0},{2,3},{3,2},{4,5},{5,4},{6,7},{7,6},{8,15},{9,10},{10,... | collective-permute-start | bytes 3145736 | tf_op jit(solution)/shard_map/ppermute | solution.py:352
  67.6 4.8 %combine.2.keep = bf16[4,2,128,512]{3,2,1,0:T(8,128)(2,1)S(1)} custom-call(bf16[8,1552,128]{2,1,0:T(8,128)(2,1)S(1)} %all-to-all-done.1.got, bf16[8,512,128]{2,1,0:T(8,128)(2,1)S(1)} %copy-done.8, bf16[5,1024,128]{2,1,0:T(8,128)(2,1)S(1)} %copy-done.2, bf16[3,1024,128]{2,1,0:T(8,128)(2,1)S(1)} %pad_maximum_fusion.second.third.refs_1_, ...), custom_call_target="tpu_custom_call" | custom-call | flops 2097152 | bytes 4194304 | tf_op jit(solution)/shard_map/combine/pallas_call | solution.py:183
  72.4 12.2 %collective-permute-done.7.wait.refs_2_ = bf16[5,1024,128]{2,1,0:T(8,128)(2,1)} collective-permute-done((bf16[5,1024,128]{2,1,0:T(8,128)(2,1)}, bf16[5,1024,128]{2,1,0:T(8,128)(2,1)}, u32[]{:S(2)}, u32[]{:S(2)}) %collective-permute-start.7) | collective-permute-done | bytes 1310752 | tf_op jit(solution)/shard_map/ppermute | solution.py:342
  85.8 5.3 %all-to-all-start.2 = ((bf16[4,2,128,512]{3,2,1,0:T(8,128)(2,1)}), bf16[4,2,128,512]{3,2,1,0:T(8,128)(2,1)S(1)}, u32[]{:S(2)}, u32[]{:S(2)}) async-start(bf16[4,2,128,512]{3,2,1,0:T(8,128)(2,1)} %add.1), calls=%async_computation.2 | async-start | bytes 2097152 | tf_op jit(solution)/shard_map/all_to_all | solution.py:322
  91.1 3.5 %collective-permute-start.8 = (bf16[3,1024,128]{2,1,0:T(8,128)(2,1)S(1)}, bf16[3,1024,128]{2,1,0:T(8,128)(2,1)S(1)}, u32[]{:S(2)}, u32[]{:S(2)}) collective-permute-start(bf16[3,1024,128]{2,1,0:T(8,128)(2,1)S(1)} %copy-done.1), channel_id=1, source_target_pairs={{0,64},{64,0},{1,65},{65,1},{2,66},{66,2},{3,67},{67,3},{4,68},{68... | collective-permute-start | bytes 2359304 | tf_op jit(solution)/shard_map/ppermute | solution.py:344
  94.6 17.4 %collective-permute-done.8.far.refs_3_ = bf16[3,1024,128]{2,1,0:T(8,128)(2,1)S(1)} collective-permute-done((bf16[3,1024,128]{2,1,0:T(8,128)(2,1)S(1)}, bf16[3,1024,128]{2,1,0:T(8,128)(2,1)S(1)}, u32[]{:S(2)}, u32[]{:S(2)}) %collective-permute-start.8) | collective-permute-done | bytes 786464 | tf_op jit(solution)/shard_map/ppermute | solution.py:344
  112.8 5.8 %all-to-all-done.2.parts = bf16[4,2,128,512]{3,2,1,0:T(8,128)(2,1)S(1)} async-done(((bf16[4,2,128,512]{3,2,1,0:T(8,128)(2,1)}), bf16[4,2,128,512]{3,2,1,0:T(8,128)(2,1)S(1)}, u32[]{:S(2)}, u32[]{:S(2)}) %all-to-all-start.2) | async-done | bytes 1048608 | tf_op jit(solution)/shard_map/all_to_all | solution.py:322
  118.6 1.1 copy-done.5
  119.9 20.6 %all_to_all.25.refs_4_ = bf16[8,128,512]{2,1,0:T(8,128)(2,1)S(1)} all-to-all(bf16[8,128,512]{2,1,0:T(8,128)(2,1)S(1)} %spread.1), channel_id=1, replica_groups=mesh['lg'=4,'lq'=2,'rx'=4,'rc'=2,'ch'=4,'cl'=2] {'lq','rx'}, dimensions={0} | all-to-all | bytes 2097152 | tf_op jit(solution)/shard_map/all_to_all | solution.py:322
  140.5 1.9 %collective-permute-start.10 = (bf16[8,128,512]{2,1,0:T(8,128)(2,1)S(1)}, bf16[8,128,512]{2,1,0:T(8,128)(2,1)S(1)}, u32[]{:S(2)}, u32[]{:S(2)}) collective-permute-start(bf16[8,128,512]{2,1,0:T(8,128)(2,1)S(1)} %all_to_all.25.refs_4_), channel_id=1, source_target_pairs={{0,8},{8,0},{1,9},{9,1},{2,10},{10,2},{3,11},{11,3},{4,12},{12,4},... | collective-permute-start | bytes 3145736 | tf_op jit(solution)/shard_map/ppermute | solution.py:357
  142.4 2.6 %collective-permute-done.10.refs_5_ = bf16[8,128,512]{2,1,0:T(8,128)(2,1)S(1)} collective-permute-done((bf16[8,128,512]{2,1,0:T(8,128)(2,1)S(1)}, bf16[8,128,512]{2,1,0:T(8,128)(2,1)S(1)}, u32[]{:S(2)}, u32[]{:S(2)}) %collective-permute-start.10) | collective-permute-done | bytes 1048608 | tf_op jit(solution)/shard_map/ppermute | solution.py:357
  145.1 4.5 %product.1 = bf16[1024,512]{1,0:T(8,128)(2,1)S(1)} custom-call(bf16[5,1024,128]{2,1,0:T(8,128)(2,1)S(1)} %copy-done.3, bf16[3,1024,128]{2,1,0:T(8,128)(2,1)S(1)} %copy-done.1, bf16[5,1024,128]{2,1,0:T(8,128)(2,1)} %collective-permute-done.7.wait.refs_2_, bf16[3,1024,128]{2,1,0:T(8,128)(2,1)S(1)} %copy-done.6, bf16[8,128,512]{2,1,0:T(8,128)(2,1)S(1)} %all_to_all.25.refs_4_, ...), custom_call_target="tpu_custom_call" | custom-call | flops 2147483648 | bytes 7340032 | tf_op jit(solution)/shard_map/product/pallas_call | solution.py:279
  149.6 35.0 %all_to_all.26.terms = bf16[8,128,512]{2,1,0:T(8,128)(2,1)S(1)} all-to-all(bf16[8,128,512]{2,1,0:T(8,128)(2,1)S(1)} %bitcast.15), channel_id=1, replica_groups=mesh['lg'=4,'lq'=2,'rx'=4,'rc'=2,'ch'=4,'cl'=2] {'lg','lq'}, dimensions={0} | all-to-all | bytes 2097152 | tf_op jit(solution)/shard_map/all_to_all | solution.py:322
  184.7 1.9 %finish.1 = bf16[128,1024]{1,0:T(8,128)(2,1)} custom-call(s32[64,64]{1,0:T(8,128)S(1)} %copy-done.7, bf16[8,128,512]{2,1,0:T(8,128)(2,1)S(1)} %all_to_all.26.terms), custom_call_target="tpu_custom_call" | custom-call | flops 1048576 | bytes 2097152 | tf_op jit(solution)/shard_map/finish/pallas_call | solution.py:307
  (32 shorter events, 4.8 us)
Async XLA Ops:
  4.4 52.1 %all-to-all-start.1 = ((bf16[8,1552,128]{2,1,0:T(8,128)(2,1)}), bf16[8,1552,128]{2,1,0:T(8,128)(2,1)S(1)}, u32[]{:S(2)}, u32[]{:S(2)}) async-start(bf16[8,1552,128]{2,1,0:T(8,128)(2,1)} %get-tuple-element.14), calls=%async_computation.1 | async-start | bytes 6356992 | tf_op jit(solution)/shard_map/all_to_all | solution.py:322
  8.7 21.6 %collective-permute-start.1 = (bf16[1024,128]{1,0:T(8,128)(2,1)}, bf16[1024,128]{1,0:T(8,128)(2,1)S(1)}, u32[]{:S(2)}, u32[]{:S(2)}) collective-permute-start(bf16[1024,128]{1,0:T(8,128)(2,1)} %get-tuple-element.13), channel_id=1, source_target_pairs={{0,6},{1,7},{2,0},{3,1},{4,2},{5,3},{6,4},{7,5},{8,14},{9,15},{10,... | collective-permute-start | bytes 786440 | tf_op jit(solution)/shard_map/ppermute | solution.py:330
  18.8 17.8 %collective-permute-start.3 = (bf16[1024,128]{1,0:T(8,128)(2,1)}, bf16[1024,128]{1,0:T(8,128)(2,1)}, u32[]{:S(2)}, u32[]{:S(2)}) collective-permute-start(bf16[1024,128]{1,0:T(8,128)(2,1)} %get-tuple-element.13), channel_id=1, source_target_pairs={{0,2},{1,3},{2,4},{3,5},{4,6},{5,7},{6,0},{7,1},{8,10},{9,11},{10,... | collective-permute-start | bytes 786440 | tf_op jit(solution)/shard_map/ppermute | solution.py:330
  20.7 25.6 %collective-permute-start = (bf16[1024,128]{1,0:T(8,128)(2,1)}, bf16[1024,128]{1,0:T(8,128)(2,1)}, u32[]{:S(2)}, u32[]{:S(2)}) collective-permute-start(bf16[1024,128]{1,0:T(8,128)(2,1)} %get-tuple-element.13), channel_id=1, source_target_pairs={{0,7},{1,0},{2,1},{3,2},{4,3},{5,4},{6,5},{7,6},{8,15},{9,8},{10,9... | collective-permute-start | bytes 786440 | tf_op jit(solution)/shard_map/ppermute | solution.py:330
  23.2 26.5 %collective-permute-start.2 = (bf16[1024,128]{1,0:T(8,128)(2,1)}, bf16[1024,128]{1,0:T(8,128)(2,1)}, u32[]{:S(2)}, u32[]{:S(2)}) collective-permute-start(bf16[1024,128]{1,0:T(8,128)(2,1)} %get-tuple-element.13), channel_id=1, source_target_pairs={{0,1},{1,2},{2,3},{3,4},{4,5},{5,6},{6,7},{7,0},{8,9},{9,10},{10,1... | collective-permute-start | bytes 786440 | tf_op jit(solution)/shard_map/ppermute | solution.py:330
  30.3 6.3 %copy-start.10 = (bf16[1024,128]{1,0:T(8,128)(2,1)}, bf16[1024,128]{1,0:T(8,128)(2,1)S(1)}, u32[]{:S(2)}) copy-start(bf16[1024,128]{1,0:T(8,128)(2,1)S(1)} %collective-permute-done.1) | copy-start | bytes 786436
  37.4 20.5 %collective-permute-start.6 = (bf16[1024,128]{1,0:T(8,128)(2,1)}, bf16[1024,128]{1,0:T(8,128)(2,1)S(1)}, u32[]{:S(2)}, u32[]{:S(2)}) collective-permute-start(bf16[1024,128]{1,0:T(8,128)(2,1)} %broadcast_select_fusion), channel_id=1, source_target_pairs={{0,6},{1,7},{2,0},{3,1},{4,2},{5,3},{6,4},{7,5},{8,10},{9,11},{10,... | collective-permute-start | bytes 786440 | tf_op jit(solution)/shard_map/ppermute | solution.py:339
  39.3 18.6 %collective-permute-start.4 = (bf16[1024,128]{1,0:T(8,128)(2,1)}, bf16[1024,128]{1,0:T(8,128)(2,1)}, u32[]{:S(2)}, u32[]{:S(2)}) collective-permute-start(bf16[1024,128]{1,0:T(8,128)(2,1)} %collective-permute-done.3), channel_id=1, source_target_pairs={{0,1},{1,2},{2,3},{3,4},{4,5},{5,6},{6,7},{7,0},{8,9},{9,10},{10,1... | collective-permute-start | bytes 786440 | tf_op jit(solution)/shard_map/ppermute | solution.py:330
  44.4 13.5 %collective-permute-start.5 = (bf16[1024,128]{1,0:T(8,128)(2,1)}, bf16[1024,128]{1,0:T(8,128)(2,1)}, u32[]{:S(2)}, u32[]{:S(2)}) collective-permute-start(bf16[1024,128]{1,0:T(8,128)(2,1)} %copy-done.10), channel_id=1, source_target_pairs={{0,7},{1,0},{2,1},{3,2},{4,3},{5,4},{6,5},{7,6},{8,15},{9,8},{10,9... | collective-permute-start | bytes 786440 | tf_op jit(solution)/shard_map/ppermute | solution.py:330
  53.0 31.6 %collective-permute-start.7 = (bf16[5,1024,128]{2,1,0:T(8,128)(2,1)}, bf16[5,1024,128]{2,1,0:T(8,128)(2,1)}, u32[]{:S(2)}, u32[]{:S(2)}) collective-permute-start(bf16[5,1024,128]{2,1,0:T(8,128)(2,1)} %bitcast_dynamic-update-slice_fusion.first.refs_0_), channel_id=1, source_target_pairs={{0,64},{64,0},{1,65},{65,1},{2,66},{66,2},{3,67},{67,3},{4,68},{68... | collective-permute-start | bytes 3932168 | tf_op jit(solution)/shard_map/ppermute | solution.py:342
  57.9 9.7 %copy-start.8 = (bf16[8,512,128]{2,1,0:T(8,128)(2,1)S(1)}, bf16[8,512,128]{2,1,0:T(8,128)(2,1)}, u32[]{:S(2)}) copy-start(bf16[8,512,128]{2,1,0:T(8,128)(2,1)} %get-tuple-element.16.more) | copy-start | bytes 3145732
  62.7 4.9 %copy-start.2 = (bf16[5,1024,128]{2,1,0:T(8,128)(2,1)S(1)}, bf16[5,1024,128]{2,1,0:T(8,128)(2,1)}, u32[]{:S(2)}) copy-start(bf16[5,1024,128]{2,1,0:T(8,128)(2,1)} %bitcast_dynamic-update-slice_fusion.first.refs_0_) | copy-start | bytes 3932164
  62.8 21.9 %collective-permute-start.9 = (bf16[4,2,128,512]{3,2,1,0:T(8,128)(2,1)S(1)}, bf16[4,2,128,512]{3,2,1,0:T(8,128)(2,1)S(1)}, u32[]{:S(2)}, u32[]{:S(2)}) collective-permute-start(bf16[4,2,128,512]{3,2,1,0:T(8,128)(2,1)S(1)} %combine.3), channel_id=1, source_target_pairs={{0,1},{1,0},{2,3},{3,2},{4,5},{5,4},{6,7},{7,6},{8,15},{9,10},{10,... | collective-permute-start | bytes 3145736 | tf_op jit(solution)/shard_map/ppermute | solution.py:352
  67.6 4.8 %copy-start = (bf16[3,1024,128]{2,1,0:T(8,128)(2,1)}, bf16[3,1024,128]{2,1,0:T(8,128)(2,1)S(1)}, u32[]{:S(2)}) copy-start(bf16[3,1024,128]{2,1,0:T(8,128)(2,1)S(1)} %pad_maximum_fusion.second.third.refs_1_) | copy-start | bytes 2359300
  85.8 5.3 %copy-start.1 = (bf16[3,1024,128]{2,1,0:T(8,128)(2,1)S(1)}, bf16[3,1024,128]{2,1,0:T(8,128)(2,1)}, u32[]{:S(2)}) copy-start(bf16[3,1024,128]{2,1,0:T(8,128)(2,1)} %copy-done) | copy-start | bytes 2359300
  85.8 32.8 %all-to-all-start.2 = ((bf16[4,2,128,512]{3,2,1,0:T(8,128)(2,1)}), bf16[4,2,128,512]{3,2,1,0:T(8,128)(2,1)S(1)}, u32[]{:S(2)}, u32[]{:S(2)}) async-start(bf16[4,2,128,512]{3,2,1,0:T(8,128)(2,1)} %add.1), calls=%async_computation.2 | async-start | bytes 2097152 | tf_op jit(solution)/shard_map/all_to_all | solution.py:322
  91.1 20.8 %collective-permute-start.8 = (bf16[3,1024,128]{2,1,0:T(8,128)(2,1)S(1)}, bf16[3,1024,128]{2,1,0:T(8,128)(2,1)S(1)}, u32[]{:S(2)}, u32[]{:S(2)}) collective-permute-start(bf16[3,1024,128]{2,1,0:T(8,128)(2,1)S(1)} %copy-done.1), channel_id=1, source_target_pairs={{0,64},{64,0},{1,65},{65,1},{2,66},{66,2},{3,67},{67,3},{4,68},{68... | collective-permute-start | bytes 2359304 | tf_op jit(solution)/shard_map/ppermute | solution.py:344
  111.9 0.9 copy-start.4
  118.6 1.1 copy-start.5
  119.9 25.2 %copy-start.3 = (bf16[5,1024,128]{2,1,0:T(8,128)(2,1)S(1)}, bf16[5,1024,128]{2,1,0:T(8,128)(2,1)}, u32[]{:S(2)}) copy-start(bf16[5,1024,128]{2,1,0:T(8,128)(2,1)} %bitcast_dynamic-update-slice_fusion.first.refs_0_) | copy-start | bytes 3932164
  119.9 25.2 %copy-start.6 = (bf16[3,1024,128]{2,1,0:T(8,128)(2,1)S(1)}, bf16[3,1024,128]{2,1,0:T(8,128)(2,1)}, u32[]{:S(2)}) copy-start(bf16[3,1024,128]{2,1,0:T(8,128)(2,1)} %copy-done.4) | copy-start | bytes 2359300
  140.5 4.5 %collective-permute-start.10 = (bf16[8,128,512]{2,1,0:T(8,128)(2,1)S(1)}, bf16[8,128,512]{2,1,0:T(8,128)(2,1)S(1)}, u32[]{:S(2)}, u32[]{:S(2)}) collective-permute-start(bf16[8,128,512]{2,1,0:T(8,128)(2,1)S(1)} %all_to_all.25.refs_4_), channel_id=1, source_target_pairs={{0,8},{8,0},{1,9},{9,1},{2,10},{10,2},{3,11},{11,3},{4,12},{12,4},... | collective-permute-start | bytes 3145736 | tf_op jit(solution)/shard_map/ppermute | solution.py:357
  149.6 35.1 %copy-start.7 = (s32[64,64]{1,0:T(8,128)S(1)}, s32[64,64]{1,0:T(8,128)}, u32[]{:S(2)}) copy-start(s32[64,64]{1,0:T(8,128)} %pattern.3) | copy-start | bytes 49156
